TPU v7x, 32 devices: a whole 2x2x4 slice. The times are simulated.
32 devices in a mesh: seq: 8 (over y, x, core), res: 4 (over z).
Axes of the slice: x: 2, y: 2, z: 4, core: 2. Of those that a mesh axis runs over, the one named last changes fastest.
Arguments:
- states: bfloat16 [256, 128, 768], P('seq', 'res'), may hold values from -6 to 6
- row_query: bfloat16 [768, 768], replicated, as said below
- row_key: bfloat16 [768, 768], replicated
- row_value: bfloat16 [768, 768], replicated, may hold values from -0.21875 to 0.21875
- row_out: bfloat16 [768, 768], replicated, may hold values from -0.21875 to 0.21875
- col_query: bfloat16 [768, 768], replicated, as said below
- col_key: bfloat16 [768, 768], replicated
- col_value: bfloat16 [768, 768], replicated, may hold values from -0.21875 to 0.21875
- col_out: bfloat16 [768, 768], replicated, may hold values from -0.21875 to 0.21875
Outputs:
- updated: bfloat16 [256, 128, 768], P('seq', 'res')
Inputs may be any that keep to these rules, and one draw needn't show every extreme that they name: No bound on the size of row_query and row_key entries or of the scores they give is promised. No bound on the size of col_query and col_key entries or of the scores they give is promised.
All inputs are finite; a program needn't handle non-finite values.
Results may differ from a plain program's by a relative error of at most 0.02.
Values may be sent and summed in bfloat16 or wider, within the bound.
No kernel may reach another device: no remote copies, remote signals or barrier semaphores. Data moves between devices by JAX's collectives and lax.ppermute only.
A program may use at most 128 MiB of HBM per device.

v0:
```python
import math

import jax
import jax.numpy as jnp
from jax import lax
from jax.sharding import PartitionSpec as P

D = 768
HEADS = 12


def normalize(states):
    values = states.astype(jnp.float32)
    center = values - jnp.mean(values, axis=-1, keepdims=True)
    spread = jnp.mean(center * center, axis=-1, keepdims=True)
    return (center * lax.rsqrt(spread + 1e-05)).astype(jnp.bfloat16)


def project(inputs, weight):
    return jnp.dot(inputs, weight, preferred_element_type=jnp.float32)


def split_heads(field):
    return field.reshape(field.shape[0], field.shape[1], HEADS, D // HEADS)


def on_device(
    states, row_query, row_key, row_value, row_out, col_query, col_key, col_value, col_out
):
    row_count, col_count = (states.shape[0], states.shape[1])
    head_dim = D // HEADS
    all_rows = row_count * lax.axis_size("seq")
    tied_scale = head_dim ** (-0.5) / math.sqrt(all_rows)
    normed = normalize(states)
    q1 = project(normed, row_query).astype(jnp.bfloat16)
    k1 = project(normed, row_key).astype(jnp.bfloat16)
    v1 = project(normed, row_value).astype(jnp.bfloat16)
    q_moved, k_moved, v_moved = (
        lax.all_to_all(q1, "res", split_axis=0, concat_axis=1, tiled=True),
        lax.all_to_all(k1, "res", split_axis=0, concat_axis=1, tiled=True),
        lax.all_to_all(v1, "res", split_axis=0, concat_axis=1, tiled=True),
    )
    partial_value = (
        jnp.einsum(
            "rihd,rjhd->hij",
            split_heads(q_moved),
            split_heads(k_moved),
            preferred_element_type=jnp.float32,
        )
        * tied_scale
    )
    tied = lax.psum(partial_value, ("seq", "res"))
    prob1 = jax.nn.softmax(tied, axis=-1).astype(jnp.bfloat16)
    o_moved = jnp.einsum(
        "hij,rjhd->rihd", prob1, split_heads(v_moved), preferred_element_type=jnp.float32
    ).astype(jnp.bfloat16)
    o_moved = o_moved.reshape(o_moved.shape[0], o_moved.shape[1], D)
    o1 = lax.all_to_all(o_moved, "res", split_axis=1, concat_axis=0, tiled=True)
    mid = (states.astype(jnp.float32) + project(o1, row_out)).astype(jnp.bfloat16)
    normed2 = normalize(mid)
    q2 = project(normed2, col_query).astype(jnp.bfloat16)
    k2 = project(normed2, col_key).astype(jnp.bfloat16)
    v2 = project(normed2, col_value).astype(jnp.bfloat16)
    q_cols, k_cols, v_cols = (
        lax.all_to_all(q2, "seq", split_axis=1, concat_axis=0, tiled=True),
        lax.all_to_all(k2, "seq", split_axis=1, concat_axis=0, tiled=True),
        lax.all_to_all(v2, "seq", split_axis=1, concat_axis=0, tiled=True),
    )
    gathered_rows, local_cols = (q_cols.shape[0], q_cols.shape[1])

    def arrange(field):
        return field.reshape(gathered_rows, local_cols, HEADS, head_dim).transpose(1, 0, 2, 3)

    def attend(triple):
        query_col, key_col, value_col = triple
        score = jnp.einsum(
            "rhd,shd->hrs", query_col, key_col, preferred_element_type=jnp.float32
        ) * head_dim ** (-0.5)
        prob2 = jax.nn.softmax(score, axis=-1).astype(jnp.bfloat16)
        return jnp.einsum(
            "hrs,shd->rhd", prob2, value_col, preferred_element_type=jnp.float32
        ).astype(jnp.bfloat16)

    o2 = lax.map(attend, (arrange(q_cols), arrange(k_cols), arrange(v_cols)))
    o2 = o2.reshape(local_cols, gathered_rows, D).transpose(1, 0, 2)
    colupd = project(o2, col_out).astype(jnp.bfloat16)
    colupd = lax.all_to_all(colupd, "seq", split_axis=0, concat_axis=1, tiled=True)
    return (mid.astype(jnp.float32) + colupd.astype(jnp.float32)).astype(jnp.bfloat16)


def solution(mesh):
    placed = (P("seq", "res", None), P(), P(), P(), P(), P(), P(), P(), P())
    return jax.shard_map(
        on_device, mesh=mesh, in_specs=placed, out_specs=P("seq", "res", None), check_vma=False
    )
```

profile of v0, /device:TPU:0, one launch (start us, length us, event | category | flops | bytes accessed | tf_op | source)
XLA Modules:
  0.0 483.4 jit_solution(3874215341209840229)
XLA Ops:
  11.7 6.3 %all-to-all-start.1 = ((bf16[32,32,768]{2,1,0:T(8,128)(2,1)}), bf16[32,32,768]{2,1,0:T(8,128)(2,1)}, u32[]{:S(2)}, u32[]{:S(2)}) async-start(bf16[32,32,768]{2,1,0:T(8,128)(2,1)} %convolution_convert_fusion.5), calls=%async_computation.1 | async-start | bytes 3145728 | tf_op jit(solution)/shard_map/all_to_all | solution.py:39
  21.9 33.2 %all-to-all-done.1 = bf16[32,32,768]{2,1,0:T(8,128)(2,1)} async-done(((bf16[32,32,768]{2,1,0:T(8,128)(2,1)}), bf16[32,32,768]{2,1,0:T(8,128)(2,1)}, u32[]{:S(2)}, u32[]{:S(2)}) %all-to-all-start.1) | async-done | bytes 1572896 | tf_op jit(solution)/shard_map/all_to_all | solution.py:39
  55.1 4.4 all-to-all-start.2
  63.3 32.7 %all-to-all-done.2 = bf16[32,32,768]{2,1,0:T(8,128)(2,1)} async-done(((bf16[32,32,768]{2,1,0:T(8,128)(2,1)}), bf16[32,32,768]{2,1,0:T(8,128)(2,1)}, u32[]{:S(2)}, u32[]{:S(2)}) %all-to-all-start.2) | async-done | bytes 1572896 | tf_op jit(solution)/shard_map/all_to_all | solution.py:40
  96.0 4.4 all-to-all-start
  103.3 5.9 %reshape.63 = bf16[8,128,12,64]{3,2,1,0:T(8,128)(2,1)} reshape(bf16[8,4,32,768]{3,2,1,0:T(8,128)(2,1)} %bitcast.128) | data formatting | bytes 3145728 | tf_op jit(solution)/shard_map/reshape | solution.py:24
  111.9 5.9 %reshape.64 = bf16[8,128,12,64]{3,2,1,0:T(8,128)(2,1)} reshape(bf16[8,4,32,768]{3,2,1,0:T(8,128)(2,1)} %bitcast.129) | data formatting | bytes 3145728 | tf_op jit(solution)/shard_map/reshape | solution.py:24
  117.8 5.9 %fusion.49 = f32[12,128,128]{2,1,0:T(8,128)} fusion(bf16[8,128,12,64]{3,2,1,0:T(8,128)(2,1)} %reshape.64, bf16[8,128,12,64]{3,2,1,0:T(8,128)(2,1)} %reshape.63), kind=kOutput, calls=%fused_computation.62 | convolution fusion | flops 201523200 | bytes 3932160 | tf_op jit(solution)/shard_map/rihd,rjhd->hij/dot_general | solution.py:44
  123.7 13.9 %all-to-all-done = bf16[32,32,768]{2,1,0:T(8,128)(2,1)} async-done(((bf16[32,32,768]{2,1,0:T(8,128)(2,1)}), bf16[32,32,768]{2,1,0:T(8,128)(2,1)}, u32[]{:S(2)}, u32[]{:S(2)}) %all-to-all-start) | async-done | bytes 1572896 | tf_op jit(solution)/shard_map/all_to_all | solution.py:41
  140.3 5.9 %reshape.62 = bf16[8,128,12,64]{3,2,1,0:T(8,128)(2,1)} reshape(bf16[8,4,32,768]{3,2,1,0:T(8,128)(2,1)} %bitcast.130) | data formatting | bytes 3145728 | tf_op jit(solution)/shard_map/reshape | solution.py:24
  146.2 108.8 %all-reduce.2.cloned.1.call-done = f32[12,128,128]{2,1,0:T(8,128)} async-done(((f32[12,128,128]{2,1,0:T(8,128)}), f32[12,128,128]{2,1,0:T(8,128)}) %all-reduce.2.cloned.1.call-update) | async-done | bytes 786448 | tf_op jit(solution)/shard_map/psum | solution.py:52
  256.8 8.2 %fusion.39 = bf16[8,128,12,64]{1,3,0,2:T(8,128)(2,1)} fusion(bf16[8,128,12,64]{3,2,1,0:T(8,128)(2,1)} %reshape.62, f32[12,128]{1,0:T(8,128)S(1)} %fusion.71, f32[12,128,128]{2,1,0:T(8,128)} %all-reduce.2.cloned.1.call-done), kind=kOutput, calls=%fused_computation.58 | convolution fusion | flops 202704512 | bytes 3938304 | tf_op jit(solution)/shard_map/hij,rjhd->rihd/dot_general | solution.py:54
  270.6 40.0 %all_to_all.117 = bf16[8,128,768]{2,0,1:T(8,128)(2,1)S(1)} all-to-all(bf16[8,128,768]{2,0,1:T(8,128)(2,1)} %copy.42), channel_id=1, replica_groups=mesh['seq'=8,'res'=4] {'res'}, dimensions={1} | all-to-all | bytes 3145728 | tf_op jit(solution)/shard_map/all_to_all | solution.py:58
  326.9 15.5 %all-to-all-done.6 = bf16[32,32,768]{2,0,1:T(8,128)(2,1)S(1)} async-done(((bf16[32,32,768]{2,0,1:T(8,128)(2,1)}), bf16[32,32,768]{2,0,1:T(8,128)(2,1)S(1)}, u32[]{:S(2)}, u32[]{:S(2)}) %all-to-all-start.6) | async-done | bytes 1572896 | tf_op jit(solution)/shard_map/all_to_all | solution.py:66
  351.9 15.8 %all-to-all-done.5 = bf16[32,32,768]{2,0,1:T(8,128)(2,1)} async-done(((bf16[32,32,768]{2,0,1:T(8,128)(2,1)}), bf16[32,32,768]{2,0,1:T(8,128)(2,1)}, u32[]{:S(2)}, u32[]{:S(2)}) %all-to-all-start.5) | async-done | bytes 1572896 | tf_op jit(solution)/shard_map/all_to_all | solution.py:65
  373.3 5.9 %reshape.68 = bf16[256,4,12,64]{3,2,0,1:T(8,128)(2,1)} reshape(bf16[8,32,4,768]{3,1,0,2:T(8,128)(2,1)} %bitcast.131) | data formatting | bytes 3145728 | tf_op jit(solution)/shard_map/reshape | solution.py:72
  379.2 4.4 copy.53
  386.2 5.9 %reshape.67 = bf16[256,4,12,64]{3,2,0,1:T(8,128)(2,1)} reshape(bf16[8,32,4,768]{3,1,0,2:T(8,128)(2,1)} %bitcast.132) | data formatting | bytes 3145728 | tf_op jit(solution)/shard_map/reshape | solution.py:72
  392.1 5.3 %copy.52 = bf16[4,256,12,64]{1,3,2,0:T(8,128)(2,1)} copy(bf16[4,256,12,64]{3,2,1,0:T(8,128)(2,1)} %bitcast.123) | data formatting | bytes 3145728 | tf_op jit(solution)/shard_map/while | solution.py:84
  400.1 5.9 %reshape.66 = bf16[256,4,12,64]{3,2,0,1:T(8,128)(2,1)} reshape(bf16[8,32,4,768]{3,1,0,2:T(8,128)(2,1)} %bitcast.133) | data formatting | bytes 3145728 | tf_op jit(solution)/shard_map/reshape | solution.py:72
  405.9 5.3 %copy.51 = bf16[4,256,12,64]{1,3,2,0:T(8,128)(2,1)} copy(bf16[4,256,12,64]{3,2,1,0:T(8,128)(2,1)} %bitcast.124) | data formatting | bytes 3145728 | tf_op jit(solution)/shard_map/while | solution.py:84
  411.2 24.7 %while.10 = (s32[]{:T(128)}, bf16[4,256,12,64]{1,3,2,0:T(8,128)(2,1)}, bf16[4,256,12,64]{1,3,2,0:T(8,128)(2,1)}, bf16[4,256,12,64]{1,3,2,0:T(8,128)(2,1)}, bf16[4,256,12,64]{1,3,2,0:T(8,128)(2,1)S(1)}, /*index=5*/s32[]{:T(128)}) while((s32[]{:T(128)}, bf16[4,256,12,64]{1,3,2,0:T(8,128)(2,1)}, bf16[4,256,12,64]{1,3,2,0:T(8,128)(2,1)}, ...), condition=%wide.region_10.11_spmd, body=%wide.region_7.10_spmd.sunk | while | flops 206242048 | bytes 14182469 | solution.py:84
  440.4 24.9 %all_to_all.118 = bf16[256,4,768]{2,1,0:T(4,128)(2,1)S(1)} all-to-all(bf16[256,4,768]{2,1,0:T(4,128)(2,1)S(1)} %copy.55), channel_id=1, replica_groups=mesh['seq'=8,'res'=4] {'seq'}, dimensions={0} | all-to-all | bytes 3145728 | tf_op jit(solution)/shard_map/all_to_all | solution.py:87
  467.8 5.1 %reshape.70 = f32[32,32,768]{2,1,0:T(8,128)} reshape(f32[32,8,4,768]{3,2,1,0:T(4,128)} %copy_bitcast_fusion) | data formatting | bytes 6291456 | tf_op jit(solution)/shard_map/convert_element_type | solution.py:88
  (67 shorter events, 100.6 us)
Async XLA Ops:
  6.5 304.4 %copy-start = (bf16[768,768]{1,0:T(8,128)(2,1)S(1)}, bf16[768,768]{1,0:T(8,128)(2,1)}, u32[]{:S(2)}) copy-start(bf16[768,768]{1,0:T(8,128)(2,1)} %param.15) | copy-start | bytes 3538948
  6.5 2.0 copy-start.2
  6.5 2.6 copy-start.5
  11.7 43.4 %all-to-all-start.1 = ((bf16[32,32,768]{2,1,0:T(8,128)(2,1)}), bf16[32,32,768]{2,1,0:T(8,128)(2,1)}, u32[]{:S(2)}, u32[]{:S(2)}) async-start(bf16[32,32,768]{2,1,0:T(8,128)(2,1)} %convolution_convert_fusion.5), calls=%async_computation.1 | async-start | bytes 3145728 | tf_op jit(solution)/shard_map/all_to_all | solution.py:39
  55.1 40.9 %all-to-all-start.2 = ((bf16[32,32,768]{2,1,0:T(8,128)(2,1)}), bf16[32,32,768]{2,1,0:T(8,128)(2,1)}, u32[]{:S(2)}, u32[]{:S(2)}) async-start(bf16[32,32,768]{2,1,0:T(8,128)(2,1)} %convolution_convert_fusion.4), calls=%async_computation.2 | async-start | bytes 3145728 | tf_op jit(solution)/shard_map/all_to_all | solution.py:40
  96.0 41.6 %all-to-all-start = ((bf16[32,32,768]{2,1,0:T(8,128)(2,1)}), bf16[32,32,768]{2,1,0:T(8,128)(2,1)}, u32[]{:S(2)}, u32[]{:S(2)}) async-start(bf16[32,32,768]{2,1,0:T(8,128)(2,1)} %convolution_convert_fusion.6), calls=%async_computation | async-start | bytes 3145728 | tf_op jit(solution)/shard_map/all_to_all | solution.py:41
  100.4 154.5 %all-reduce.2.cloned.1.call-start = ((), (), s32[]{:S(2)}) async-start(), calls=%async_computation.8 | async-start | bytes 1572864 | tf_op jit(solution)/shard_map/psum | solution.py:52
  312.5 3.3 copy-start.3
  312.5 1.8 copy-start.6
  317.8 24.5 %all-to-all-start.6 = ((bf16[32,32,768]{2,0,1:T(8,128)(2,1)}), bf16[32,32,768]{2,0,1:T(8,128)(2,1)S(1)}, u32[]{:S(2)}, u32[]{:S(2)}) async-start(bf16[32,32,768]{2,0,1:T(8,128)(2,1)} %copy.49), calls=%async_computation.6 | async-start | bytes 3145728 | tf_op jit(solution)/shard_map/all_to_all | solution.py:66
  342.4 25.3 %all-to-all-start.5 = ((bf16[32,32,768]{2,0,1:T(8,128)(2,1)}), bf16[32,32,768]{2,0,1:T(8,128)(2,1)}, u32[]{:S(2)}, u32[]{:S(2)}) async-start(bf16[32,32,768]{2,0,1:T(8,128)(2,1)} %copy.47), calls=%async_computation.5 | async-start | bytes 3145728 | tf_op jit(solution)/shard_map/all_to_all | solution.py:65
  367.7 29.6 %all-to-all-start.4 = ((bf16[32,32,768]{2,0,1:T(8,128)(2,1)}), bf16[32,32,768]{2,0,1:T(8,128)(2,1)}, u32[]{:S(2)}, u32[]{:S(2)}) async-start(bf16[32,32,768]{2,0,1:T(8,128)(2,1)} %copy.45), calls=%async_computation.4 | async-start | bytes 3145728 | tf_op jit(solution)/shard_map/all_to_all | solution.py:67
  435.9 1.8 copy-start.7
  467.8 5.1 %copy-start.4 = (bf16[32,32,768]{2,1,0:T(8,128)(2,1)S(1)}, bf16[32,32,768]{2,1,0:T(8,128)(2,1)}, u32[]{:S(2)}) copy-start(bf16[32,32,768]{2,1,0:T(8,128)(2,1)} %copy-done.3) | copy-start | bytes 4718596
  472.9 3.6 copy-start.1
Sparse Core Ops, SparseCore 0:
  123.9 131.0 all-reduce.1
where the time goes:
time: 486 us; the launch traced here: 483 us
  waiting for transfers between devices  220 us (45%)
  local copies, waits for them, and re-layouts  86.4 us (18%)
  blocking collectives  64.9 us (13%)
  matrix products  50.4 us (10%)
  starting transfers between devices  27.7 us (6%)
  other arithmetic  20.6 us (4%)
  between operations  13.6 us (3%)
    psum x1, waiting for transfers between devices, on_device(): tied = lax.psum(partial_value, ('seq', 'res'))  109 us
    all_to_all x1, blocking collectives, on_device(): o1 = lax.all_to_all(o_moved, 'res', split_axis=1, concat_axis=0, tiled=True)  40 us
    all_to_all x1, waiting for transfers between devices, on_device(): lax.all_to_all(q1, 'res', split_axis=0, concat_axis=1, tiled=True)  33.2 us
    all_to_all x1, waiting for transfers between devices, on_device(): lax.all_to_all(k1, 'res', split_axis=0, concat_axis=1, tiled=True)  32.7 us
    all_to_all x1, blocking collectives, on_device(): lax.all_to_all(colupd, 'seq', split_axis=0, concat_axis=1, tiled=True)  24.9 us
    dot_general x8, matrix products, project(): return jnp.dot(inputs, weight, preferred_element_type=jnp.float32)  21.1 us
    reshape x3, local copies, waits for them, and re-layouts, split_heads(): return field.reshape(field.shape[0], field.shape[1], HEADS, D // HEADS)  17.7 us
    reshape x3, local copies, waits for them, and re-layouts, arrange(): field.reshape(gathered_rows, local_cols, HEADS, head_dim)  17.6 us
  transfers between devices with their start and end apart: 7, of which 6 were waited for; matrix products, arithmetic and copies ran while one was open for 16% of the time, Pallas kernels for 0%

commit v1 on v0

v1 whole, which is shorter than its diff:
```python
import functools
import math

import jax
import jax.numpy as jnp
from jax import lax
from jax.experimental import pallas as pl
from jax.experimental.pallas import tpu as pltpu
from jax.sharding import Mesh
from jax.sharding import PartitionSpec as P

HEADS = 12
CORES = 2
CHUNKS = 2
VMEM_BYTES = 56 * 1024 * 1024

BF16 = jnp.bfloat16
F32 = jnp.float32


def normalize(values):
    center = values - jnp.mean(values, axis=-1, keepdims=True)
    spread = jnp.mean(center * center, axis=-1, keepdims=True)
    return (center * lax.rsqrt(spread + 1e-05)).astype(BF16)


def dot(left, right):
    return jnp.dot(left, right, preferred_element_type=F32)


def dot_nt(left, right):
    return lax.dot_general(left, right, (((1,), (1,)), ((), ())), preferred_element_type=F32)


def head_masks(shape, head_dim):
    lane = lax.broadcasted_iota(jnp.int32, shape, len(shape) - 1)
    first = lax.rem(lane, 2 * head_dim) < head_dim
    return first, jnp.logical_not(first)


def permutation(size, source):
    wanted = source(lax.broadcasted_iota(jnp.int32, (size, size), 0))
    return (wanted == lax.broadcasted_iota(jnp.int32, (size, size), 1)).astype(F32).astype(BF16)


def row_scores(core_ref, x_ref, wq_ref, wk_ref, wv_ref, mine_ref, other_ref, v_ref):
    parts, rows, block, width = x_ref.shape
    cols = parts * block
    head_dim = width // HEADS
    pair = 2 * head_dim
    half_pairs = HEADS // 2 // CORES
    piece = block // CHUNKS

    values = x_ref[...].astype(F32)
    values = jnp.concatenate(
        [values[:, row].reshape(cols, width) for row in range(rows)], axis=0
    )
    normed = normalize(values)
    q = dot(normed, wq_ref[...])
    k = dot(normed, wk_ref[...])
    v = dot(normed, wv_ref[...])
    v_ref[...] = v.astype(BF16).reshape(rows, cols, width)
    first, second = head_masks(k.shape, head_dim)
    q = q.astype(BF16)
    k_first = jnp.where(first, k, 0.0).astype(BF16)
    k_second = jnp.where(second, k, 0.0).astype(BF16)

    def beside(field, at):
        lanes = slice(at * pair, (at + 1) * pair)
        return jnp.concatenate(
            [field[row * cols : (row + 1) * cols, lanes] for row in range(rows)], axis=1
        )

    scores = []
    for at in range(HEADS // 2):
        keys = jnp.concatenate([beside(k_first, at), beside(k_second, at)], axis=0)
        score = dot_nt(beside(q, at), keys)
        score = score.reshape(parts, CHUNKS, piece, 2 * cols)
        scores.append(jnp.swapaxes(score, 0, 1).reshape(cols, 2 * cols))

    def put(low_ref, high_ref):
        for at in range(half_pairs):
            low, high = scores[at], scores[half_pairs + at]

            @pl.when(pl.program_id(0) == 0)
            def _():
                low_ref[at] = low
                high_ref[at] = high

            @pl.when(pl.program_id(0) > 0)
            def _():
                low_ref[at] += low
                high_ref[at] += high

    @pl.when(core_ref[0] == 0)
    def _():
        put(mine_ref, other_ref)

    @pl.when(core_ref[0] == 1)
    def _():
        put(other_ref, mine_ref)


def row_softmax(scale, parts_ref, prob_ref):
    tied = parts_ref[0]
    for at in range(1, parts_ref.shape[0]):
        tied = tied + parts_ref[at]
    tied = tied * scale
    cols = tied.shape[1] // 2
    halves = []
    for half in (tied[:, :cols], tied[:, cols:]):
        top = jnp.exp(half - jnp.max(half, axis=-1, keepdims=True))
        halves.append(top / jnp.sum(top, axis=-1, keepdims=True))
    prob = jnp.concatenate(halves, axis=1).astype(BF16)
    for at in range(prob_ref.shape[0]):
        prob_ref[at] = prob


def row_update(seq_size, core_ref, mine_ref, other_ref, v_ref, x_ref, wo_ref, mid_ref, o_ref):
    parts, rows, block, width = x_ref.shape
    cols = parts * block
    head_dim = width // HEADS
    pair = 2 * head_dim
    half_pairs = HEADS // 2 // CORES
    piece = block // CHUNKS
    first, second = head_masks((cols, pair), head_dim)

    for prob_ref, low in ((mine_ref, core_ref[0]), (other_ref, 1 - core_ref[0])):
        for at in range(half_pairs):
            lanes = pl.ds(pl.multiple_of((low * half_pairs + at) * pair, pair), pair)
            prob = prob_ref[at]
            for row in range(0, rows, 2):
                fields = [v_ref[row + step, :, lanes].astype(F32) for step in range(2)]
                values = jnp.concatenate(
                    [
                        jnp.concatenate(
                            [jnp.where(mask, field, 0.0).astype(BF16) for field in fields], axis=1
                        )
                        for mask in (first, second)
                    ],
                    axis=0,
                )
                result = dot(prob, values).astype(BF16)
                o_ref[row, :, lanes] = result[:, :pair]
                o_ref[row + 1, :, lanes] = result[:, pair:]

    tokens = rows * parts * piece
    at_once = piece // seq_size

    def source(token):
        row = lax.rem(token, rows)
        rest = lax.div(token, rows)
        inner = lax.rem(rest, at_once)
        rest = lax.div(rest, at_once)
        part = lax.rem(rest, parts)
        owner = lax.div(rest, parts)
        return (row * parts + part) * piece + owner * at_once + inner

    order = permutation(tokens, source)
    for chunk in range(CHUNKS):
        attended = o_ref[:, chunk * parts * piece : (chunk + 1) * parts * piece, :]
        residual = jnp.swapaxes(x_ref[:, :, chunk * piece : (chunk + 1) * piece, :], 0, 1)
        mid = residual.reshape(tokens, width).astype(F32) + dot(
            attended.reshape(tokens, width), wo_ref[...]
        )
        mid_ref[chunk] = dot(order, mid.astype(BF16)).astype(BF16)


def column_update(at_once, rows, mid_ref, wq_ref, wk_ref, wv_ref, wo_ref, out_ref, o_ref):
    total, width = mid_ref.shape
    all_rows = total // at_once
    head_dim = width // HEADS
    pair = 2 * head_dim
    scale = head_dim ** (-0.5)

    mid = mid_ref[...].astype(F32)
    if at_once > 1:
        mid = mid.reshape(all_rows // rows, at_once, rows, width)
        mid = jnp.concatenate(
            [mid[:, at].reshape(all_rows, width) for at in range(at_once)], axis=0
        )
    normed = normalize(mid)
    q = (dot(normed, wq_ref[...]).astype(BF16) * scale).astype(BF16)
    k = dot(normed, wk_ref[...])
    v = dot(normed, wv_ref[...])
    first, second = head_masks(k.shape, head_dim)
    k_first = jnp.where(first, k, 0.0).astype(BF16)
    k_second = jnp.where(second, k, 0.0).astype(BF16)
    v_first = jnp.where(first, v, 0.0).astype(BF16)
    v_second = jnp.where(second, v, 0.0).astype(BF16)
    one_first, one_second = (
        mask.astype(F32).astype(BF16) for mask in head_masks((all_rows, pair), head_dim)
    )

    for at in range(at_once):
        own = slice(at * all_rows, (at + 1) * all_rows)
        for head in range(HEADS // 2):
            lanes = slice(head * pair, (head + 1) * pair)
            keys = jnp.concatenate([k_first[own, lanes], k_second[own, lanes]], axis=0)
            score = dot_nt(q[own, lanes], keys)
            tops = []
            for half in (score[:, :all_rows], score[:, all_rows:]):
                tops.append(jnp.exp(half - jnp.max(half, axis=-1, keepdims=True)).astype(BF16))
            values = jnp.concatenate(
                [
                    jnp.concatenate([v_first[own, lanes], one_first], axis=1),
                    jnp.concatenate([v_second[own, lanes], one_second], axis=1),
                ],
                axis=0,
            )
            result = dot(jnp.concatenate(tops, axis=1), values)
            o_ref[own, lanes] = (result[:, :pair] / result[:, pair:]).astype(BF16)

    update = dot(o_ref[...], wo_ref[...]).astype(BF16).astype(F32)
    updated = (mid + update).astype(BF16)
    owners, kept = out_ref.shape[0], out_ref.shape[2]
    for at in range(at_once):
        out_ref[:, at] = updated[at * all_rows : (at + 1) * all_rows].reshape(owners, kept, width)


def assemble(*refs):
    out_ref = refs[-1]
    rows, cols, width = out_ref.shape
    pieces = [ref[...].reshape(-1, width) for ref in refs[:-1]]
    tokens = rows * cols

    def source(token):
        return lax.rem(token, cols) * rows + lax.div(token, cols)

    gathered = jnp.concatenate(pieces, axis=0)
    moved = dot(permutation(tokens, source), gathered)
    out_ref[...] = moved.astype(BF16).reshape(rows, cols, width)


def whole(shape):
    return pl.BlockSpec(shape, lambda *_: (0,) * len(shape))


def params():
    return pltpu.CompilerParams(vmem_limit_bytes=VMEM_BYTES)


def cost(flops, moved, special=0):
    return pl.CostEstimate(flops=int(flops), bytes_accessed=int(moved), transcendentals=int(special))


def on_device(
    states, row_query, row_key, row_value, row_out, col_query, col_key, col_value, col_out
):
    rows, block, width = states.shape
    pairs_size, res_size = lax.axis_size("pair"), lax.axis_size("res")
    seq_size = pairs_size * CORES
    all_rows, cols = rows * seq_size, block * res_size
    head_dim = width // HEADS
    own_rows = rows // res_size
    half_pairs = HEADS // 2 // CORES
    core = lax.axis_index("core").astype(jnp.int32).reshape(1)
    swap = [(0, 1), (1, 0)]
    smem = pl.BlockSpec(memory_space=pltpu.SMEM)
    weight = whole((width, width))

    x = lax.all_to_all(states, "res", split_axis=0, concat_axis=0, tiled=True)
    x = x.reshape(res_size, own_rows, block, width)

    at_once = min(2, own_rows)
    tied_shape = (half_pairs, cols, 2 * cols)
    mine, other, v = pl.pallas_call(
        row_scores,
        grid=(own_rows // at_once,),
        in_specs=[smem, pl.BlockSpec((res_size, at_once, block, width), lambda g: (0, g, 0, 0))]
        + [weight] * 3,
        out_specs=[
            whole(tied_shape),
            whole(tied_shape),
            pl.BlockSpec((at_once, cols, width), lambda g: (g, 0, 0)),
        ],
        out_shape=[
            jax.ShapeDtypeStruct(tied_shape, F32),
            jax.ShapeDtypeStruct(tied_shape, F32),
            jax.ShapeDtypeStruct((own_rows, cols, width), BF16),
        ],
        compiler_params=params(),
        cost_estimate=cost(8 * own_rows * cols * width * width, 12e6),
        name="row_scores",
    )(core, x, row_query, row_key, row_value)

    shares = pairs_size * res_size
    partial = mine + lax.ppermute(other, "core", swap)
    partial = partial.reshape(shares, half_pairs * cols // shares, 2 * cols)
    partial = lax.all_to_all(partial, ("pair", "res"), split_axis=0, concat_axis=0, tiled=True)
    prob = pl.pallas_call(
        functools.partial(row_softmax, head_dim ** (-0.5) / math.sqrt(all_rows)),
        out_shape=jax.ShapeDtypeStruct(partial.shape, BF16),
        compiler_params=params(),
        name="row_softmax",
    )(partial)
    prob = lax.all_to_all(prob, ("pair", "res"), split_axis=0, concat_axis=0, tiled=True)
    prob = prob.reshape(tied_shape)
    prob_other = lax.ppermute(prob, "core", swap)

    tokens = own_rows * cols // CHUNKS
    mid = pl.pallas_call(
        functools.partial(row_update, seq_size),
        in_specs=[smem]
        + [pl.BlockSpec(memory_space=pltpu.VMEM)] * 5,
        out_shape=jax.ShapeDtypeStruct((CHUNKS, tokens, width), BF16),
        scratch_shapes=[pltpu.VMEM((own_rows, cols, width), BF16)],
        compiler_params=params(),
        cost_estimate=cost(3 * own_rows * cols * width * width, 8e6),
        name="row_update",
    )(core, prob, prob_other, v, x, row_out)

    col_at_once = block // CHUNKS // seq_size
    out = []
    for chunk in range(CHUNKS):
        moved = lax.all_to_all(
            mid[chunk], ("pair", "core", "res"), split_axis=0, concat_axis=0, tiled=True
        )
        updated = pl.pallas_call(
            functools.partial(column_update, col_at_once, own_rows),
            out_shape=jax.ShapeDtypeStruct((seq_size, col_at_once, rows, width), BF16),
            scratch_shapes=[pltpu.VMEM((tokens, width), BF16)],
            compiler_params=params(),
            cost_estimate=cost(10 * tokens * width * width, 8e6, tokens * all_rows * HEADS),
            name="column_update",
        )(moved, col_query, col_key, col_value, col_out)
        out.append(
            lax.all_to_all(updated, ("pair", "core"), split_axis=0, concat_axis=0, tiled=True)
        )

    row_step = 16
    piece = pl.BlockSpec((seq_size, col_at_once, row_step, width), lambda g: (0, 0, g, 0))
    return pl.pallas_call(
        assemble,
        grid=(rows // row_step,),
        in_specs=[piece] * CHUNKS,
        out_specs=pl.BlockSpec((row_step, block, width), lambda g: (g, 0, 0)),
        out_shape=jax.ShapeDtypeStruct((rows, block, width), BF16),
        compiler_params=params(),
        name="assemble",
    )(*out)


def solution(mesh):
    seq_size, res_size = mesh.devices.shape
    split = Mesh(
        mesh.devices.reshape(seq_size // CORES, CORES, res_size), ("pair", "core", "res")
    )
    placed = P(("pair", "core"), "res", None)
    return jax.shard_map(
        on_device,
        mesh=split,
        in_specs=(placed,) + (P(),) * 8,
        out_specs=placed,
        check_vma=False,
    )
```

time: 486 us -> 183 us (0.38)
  waiting for transfers between devices: 220 us -> 56.1 us
  local copies, waits for them, and re-layouts: 86.4 us -> 4.16 us
  matrix products: 50.4 us -> 0 us
  Pallas kernels: 0 us -> 37.5 us
  other arithmetic: 20.6 us -> 1.05 us
  between operations: 13.6 us -> 0.03 us
  starting transfers between devices: 27.7 us -> 14.5 us
    psum x1 -> x0, waiting for transfers between devices: 109 us -> none  [on_device(): tied = lax.psum(partial_value, ('seq', 'res'))]
    all_to_all x6 -> x3, waiting for transfers between devices: 111 us -> 52.7 us  [the longest x1 37 us: on_device(): x = lax.all_to_all(states, 'res', split_axis=0, concat_axis=0, tiled=True)]
    dot_general x18 -> x0, matrix products: 50.4 us -> none  [the longest x8 21.1 us: project(): return jnp.dot(inputs, weight, preferred_element_type=jnp.float32)]
    reshape x8 -> x0, local copies, waits for them, and re-layouts: 40 us -> none  [the longest x3 17.7 us: split_heads(): return field.reshape(field.shape[0], field.shape[1], HEADS, D // HEADS)]
    pallas_call x0 -> x6, Pallas kernels: none -> 37.5 us  [the longest x2 16.5 us: on_device(): pl.pallas_call(functools.partial(column_update, col_at_once, own_rows), o...]
    convert_element_type x6 -> x0, local copies, waits for them, and re-layouts: 15.1 us -> none  [the longest x1 5.06 us: on_device(): colupd.astype(jnp.float32)]
    all_to_all x7 -> x0, local copies, waits for them, and re-layouts: 15 us -> none  [the longest x1 2.71 us: on_device(): lax.all_to_all(v2, 'seq', split_axis=1, concat_axis=0, tiled=True)]
    while x3 -> x0, local copies, waits for them, and re-layouts: 14.9 us -> none  [on_device(): o2 = lax.map(attend, (arrange(q_cols), arrange(k_cols), arrange(v_cols)))]
  transfers between devices with their start and end apart: 7 -> 5, of which waited for: 6 -> 5; matrix products, arithmetic and copies ran while one was open for 16% -> 0% of each run, Pallas kernels for 0% -> 9%
where the time goes in v1:
time: 183 us; the launch traced here: 182 us
  blocking collectives  68.9 us (38%)
  waiting for transfers between devices  56.1 us (31%)
  Pallas kernels  37.5 us (20%)
  starting transfers between devices  14.5 us (8%)
  local copies, waits for them, and re-layouts  4.16 us (2%)
    all_to_all x1, waiting for transfers between devices, on_device(): x = lax.all_to_all(states, 'res', split_axis=0, concat_axis=0, tiled=True)  37 us
    all_to_all x1, blocking collectives, on_device(): lax.all_to_all(mid[chunk], ('pair', 'core', 'res'), split_axis=0, concat_...  22 us
    all_to_all x1, blocking collectives, on_device(): lax.all_to_all(partial, ('pair', 'res'), split_axis=0, concat_axis=0, til...  18.3 us
    all_to_all x1, blocking collectives, on_device(): lax.all_to_all(updated, ('pair', 'core'), split_axis=0, concat_axis=0, ti...  16.7 us
    pallas_call x2, Pallas kernels, on_device(): pl.pallas_call(functools.partial(column_update, col_at_once, own_rows), o...  16.5 us
    all_to_all x1, blocking collectives, on_device(): lax.all_to_all(prob, ('pair', 'res'), split_axis=0, concat_axis=0, tiled=...  11.9 us
    all_to_all x1, waiting for transfers between devices, on_device(): lax.all_to_all(mid[chunk], ('pair', 'core', 'res'), split_axis=0, concat_...  11.4 us
    pallas_call x1, Pallas kernels, on_device(): pl.pallas_call(row_scores, grid=(own_rows // at_once,), in_specs=[smem, p...  9.6 us
  transfers between devices with their start and end apart: 5, of which 5 were waited for; matrix products, arithmetic and copies ran while one was open for 0% of the time, Pallas kernels for 9%

profile of v1, /device:TPU:0, one launch (start us, length us, event | category | flops | bytes accessed | tf_op | source)
XLA Modules:
  0.0 182.3 jit_solution(16881173040792508905)
XLA Ops:
  0.0 6.3 %all-to-all-start = ((bf16[32,32,768]{2,1,0:T(8,128)(2,1)}), bf16[32,32,768]{2,1,0:T(8,128)(2,1)S(1)}, u32[]{:S(2)}, u32[]{:S(2)}) async-start(bf16[32,32,768]{2,1,0:T(8,128)(2,1)} %param.9), calls=%async_computation | async-start | bytes 3145728 | tf_op jit(solution)/shard_map/all_to_all | solution.py:262
  6.3 37.0 %all-to-all-done = bf16[32,32,768]{2,1,0:T(8,128)(2,1)S(1)} async-done(((bf16[32,32,768]{2,1,0:T(8,128)(2,1)}), bf16[32,32,768]{2,1,0:T(8,128)(2,1)S(1)}, u32[]{:S(2)}, u32[]{:S(2)}) %all-to-all-start) | async-done | bytes 1572896 | tf_op jit(solution)/shard_map/all_to_all | solution.py:262
  43.3 1.1 copy-done.1
  44.4 9.6 %row_scores.1 = (f32[3,128,256]{2,1,0:T(8,128)}, f32[3,128,256]{2,1,0:T(8,128)}, bf16[8,128,768]{2,1,0:T(8,128)(2,1)}) custom-call(s32[1]{0:T(128)} %bitcast.core_ref, bf16[4,8,32,768]{3,2,1,0:T(8,128)(2,1)} %bitcast.9, bf16[768,768]{1,0:T(8,128)(2,1)} %wq_ref.3, bf16[768,768]{1,0:T(8,128)(2,1)} %wk_ref.3, bf16[768,768]{1,0:T(8,128)(2,1)} %wv_ref.3), custom_call_target="tpu_custom_call" | custom-call | flops 4831838208 | bytes 12000000 | tf_op jit(solution)/shard_map/row_scores/pallas_call | solution.py:267
  54.0 0.0 collective-permute-start
  54.0 1.9 %collective-permute-done = f32[3,128,256]{2,1,0:T(8,128)S(1)} collective-permute-done((f32[3,128,256]{2,1,0:T(8,128)}, f32[3,128,256]{2,1,0:T(8,128)S(1)}, u32[]{:S(2)}, u32[]{:S(2)}) %collective-permute-start) | collective-permute-done | bytes 393248 | tf_op jit(solution)/shard_map/ppermute | solution.py:288
  56.0 1.0 add.3
  57.0 18.3 %all_to_all.47.parts_ref = f32[16,24,256]{2,1,0:T(8,128)} all-to-all(f32[16,24,256]{2,1,0:T(8,128)S(1)} %bitcast.11), channel_id=1, replica_groups=mesh['pair'=4,'core'=2,'res'=4] {'pair','res'}, dimensions={0} | all-to-all | bytes 786432 | tf_op jit(solution)/shard_map/all_to_all | solution.py:290
  75.3 1.9 %row_softmax.1 = bf16[16,24,256]{2,1,0:T(8,128)(2,1)} custom-call(f32[16,24,256]{2,1,0:T(8,128)} %all_to_all.47.parts_ref), custom_call_target="tpu_custom_call" | custom-call | tf_op jit(solution)/shard_map/row_softmax/pallas_call | solution.py:291
  77.2 11.9 %all_to_all.48 = bf16[16,24,256]{2,1,0:T(8,128)(2,1)S(1)} all-to-all(bf16[16,24,256]{2,1,0:T(8,128)(2,1)} %row_softmax.1), channel_id=1, replica_groups=mesh['pair'=4,'core'=2,'res'=4] {'pair','res'}, dimensions={0} | all-to-all | bytes 393216 | tf_op jit(solution)/shard_map/all_to_all | solution.py:297
  89.1 0.0 collective-permute-start.1
  89.1 1.4 collective-permute-done.1.other_ref
  90.5 0.7 copy-done.4
  91.2 6.4 %row_update.1 = bf16[2,512,768]{2,1,0:T(8,128)(2,1)} custom-call(s32[1]{0:T(128)} %bitcast.core_ref, bf16[3,128,256]{2,1,0:T(8,128)(2,1)} %bitcast.15, bf16[3,128,256]{2,1,0:T(8,128)(2,1)} %copy-done.4, bf16[8,128,768]{2,1,0:T(8,128)(2,1)} %get-tuple-element.10.v_ref, bf16[4,8,32,768]{3,2,1,0:T(8,128)(2,1)} %bitcast.10, bf16[768,768]{1,0:T(8,128)(2,1)} %wo_ref.3), custom_call_target="tpu_custom_call" | custom-call | flops 1811939328 | bytes 8000000 | tf_op jit(solution)/shard_map/row_update/pallas_call | solution.py:302
  97.6 2.4 %fusion = (bf16[1,512,768]{2,1,0:T(8,128)(2,1)}, bf16[1,512,768]{2,1,0:T(8,128)(2,1)S(1)}) fusion(bf16[2,512,768]{2,1,0:T(8,128)(2,1)} %row_update.1), kind=kLoop, calls=%fused_computation | loop fusion | bytes 3145728 | tf_op jit(solution)/shard_map/slice | solution.py:317
  100.0 22.0 %all_to_all.49 = bf16[32,16,768]{2,1,0:T(8,128)(2,1)} all-to-all(bf16[32,16,768]{2,1,0:T(8,128)(2,1)S(1)} %bitcast.8), channel_id=1, replica_groups=mesh['pair'=4,'core'=2,'res'=4] {'pair','core','res'}, dimensions={0} | all-to-all | bytes 1572864 | tf_op jit(solution)/shard_map/all_to_all | solution.py:316
  122.0 4.3 %all-to-all-start.5 = ((bf16[32,16,768]{2,1,0:T(8,128)(2,1)}), bf16[32,16,768]{2,1,0:T(8,128)(2,1)S(1)}, u32[]{:S(2)}, u32[]{:S(2)}) async-start(bf16[32,16,768]{2,1,0:T(8,128)(2,1)} %bitcast.6), calls=%async_computation.5 | async-start | bytes 1572864 | tf_op jit(solution)/shard_map/all_to_all | solution.py:316
  126.3 8.2 %column_update.2 = bf16[8,2,32,768]{3,2,1,0:T(8,128)(2,1)} custom-call(bf16[512,768]{1,0:T(8,128)(2,1)} %bitcast.13, bf16[768,768]{1,0:T(8,128)(2,1)} %wq_ref.5, bf16[768,768]{1,0:T(8,128)(2,1)} %wk_ref.5, bf16[768,768]{1,0:T(8,128)(2,1)} %wv_ref.5, bf16[768,768]{1,0:T(8,128)(2,1)} %wo_ref.5), custom_call_target="tpu_custom_call" | custom-call | flops 3019898880 | bytes 8000000 | tf_op jit(solution)/shard_map/column_update/pallas_call | solution.py:319
  134.6 11.4 %all-to-all-done.5 = bf16[32,16,768]{2,1,0:T(8,128)(2,1)S(1)} async-done(((bf16[32,16,768]{2,1,0:T(8,128)(2,1)}), bf16[32,16,768]{2,1,0:T(8,128)(2,1)S(1)}, u32[]{:S(2)}, u32[]{:S(2)}) %all-to-all-start.5) | async-done | bytes 786464 | tf_op jit(solution)/shard_map/all_to_all | solution.py:316
  145.9 3.8 %all-to-all-start.4 = ((bf16[8,2,32,768]{3,2,1,0:T(8,128)(2,1)}), bf16[8,2,32,768]{3,2,1,0:T(8,128)(2,1)S(1)}, u32[]{:S(2)}, u32[]{:S(2)}) async-start(bf16[8,2,32,768]{3,2,1,0:T(8,128)(2,1)} %column_update.2), calls=%async_computation.4 | async-start | bytes 1572864 | tf_op jit(solution)/shard_map/all_to_all | solution.py:328
  149.8 8.2 %column_update.3 = bf16[8,2,32,768]{3,2,1,0:T(8,128)(2,1)} custom-call(bf16[512,768]{1,0:T(8,128)(2,1)} %bitcast.12, bf16[768,768]{1,0:T(8,128)(2,1)} %wq_ref.5, bf16[768,768]{1,0:T(8,128)(2,1)} %wk_ref.5, bf16[768,768]{1,0:T(8,128)(2,1)} %wv_ref.5, bf16[768,768]{1,0:T(8,128)(2,1)} %wo_ref.5), custom_call_target="tpu_custom_call" | custom-call | flops 3019898880 | bytes 8000000 | tf_op jit(solution)/shard_map/column_update/pallas_call | solution.py:319
  158.0 4.4 %all-to-all-done.4.refs_0_ = bf16[8,2,32,768]{3,2,1,0:T(8,128)(2,1)S(1)} async-done(((bf16[8,2,32,768]{3,2,1,0:T(8,128)(2,1)}), bf16[8,2,32,768]{3,2,1,0:T(8,128)(2,1)S(1)}, u32[]{:S(2)}, u32[]{:S(2)}) %all-to-all-start.4) | async-done | bytes 786464 | tf_op jit(solution)/shard_map/all_to_all | solution.py:328
  162.4 16.7 %all_to_all.50.refs_1_ = bf16[8,2,32,768]{3,2,1,0:T(8,128)(2,1)} all-to-all(bf16[8,2,32,768]{3,2,1,0:T(8,128)(2,1)} %column_update.3), channel_id=1, replica_groups=mesh['pair'=4,'core'=2,'res'=4] {'pair','core'}, dimensions={0} | all-to-all | bytes 1572864 | tf_op jit(solution)/shard_map/all_to_all | solution.py:328
  179.1 3.2 %assemble.1 = bf16[32,32,768]{2,1,0:T(8,128)(2,1)} custom-call(bf16[8,2,32,768]{3,2,1,0:T(8,128)(2,1)} %copy-done, bf16[8,2,32,768]{3,2,1,0:T(8,128)(2,1)} %all_to_all.50.refs_1_), custom_call_target="tpu_custom_call" | custom-call | tf_op jit(solution)/shard_map/assemble/pallas_call | solution.py:333
  (8 shorter events, 0.0 us)
Async XLA Ops:
  0.0 43.3 %all-to-all-start = ((bf16[32,32,768]{2,1,0:T(8,128)(2,1)}), bf16[32,32,768]{2,1,0:T(8,128)(2,1)S(1)}, u32[]{:S(2)}, u32[]{:S(2)}) async-start(bf16[32,32,768]{2,1,0:T(8,128)(2,1)} %param.9), calls=%async_computation | async-start | bytes 3145728 | tf_op jit(solution)/shard_map/all_to_all | solution.py:262
  43.3 1.1 copy-start.1
  54.0 1.9 %collective-permute-start = (f32[3,128,256]{2,1,0:T(8,128)}, f32[3,128,256]{2,1,0:T(8,128)S(1)}, u32[]{:S(2)}, u32[]{:S(2)}) collective-permute-start(f32[3,128,256]{2,1,0:T(8,128)} %get-tuple-element.9), channel_id=1, source_target_pairs={{0,4},{4,0},{1,5},{5,1},{2,6},{6,2},{3,7},{7,3},{8,12},{12,8},{9,1... | collective-permute-start | bytes 1179656 | tf_op jit(solution)/shard_map/ppermute | solution.py:288
  89.1 1.4 copy-start.3
  89.1 1.4 collective-permute-start.1
  90.5 0.7 copy-start.4
  122.0 24.0 %all-to-all-start.5 = ((bf16[32,16,768]{2,1,0:T(8,128)(2,1)}), bf16[32,16,768]{2,1,0:T(8,128)(2,1)S(1)}, u32[]{:S(2)}, u32[]{:S(2)}) async-start(bf16[32,16,768]{2,1,0:T(8,128)(2,1)} %bitcast.6), calls=%async_computation.5 | async-start | bytes 1572864 | tf_op jit(solution)/shard_map/all_to_all | solution.py:316
  145.9 3.8 %copy-start.2 = (bf16[32,16,768]{2,1,0:T(8,128)(2,1)}, bf16[32,16,768]{2,1,0:T(8,128)(2,1)S(1)}, u32[]{:S(2)}) copy-start(bf16[32,16,768]{2,1,0:T(8,128)(2,1)S(1)} %all-to-all-done.5) | copy-start | bytes 2359300
  145.9 16.4 %all-to-all-start.4 = ((bf16[8,2,32,768]{3,2,1,0:T(8,128)(2,1)}), bf16[8,2,32,768]{3,2,1,0:T(8,128)(2,1)S(1)}, u32[]{:S(2)}, u32[]{:S(2)}) async-start(bf16[8,2,32,768]{3,2,1,0:T(8,128)(2,1)} %column_update.2), calls=%async_computation.4 | async-start | bytes 1572864 | tf_op jit(solution)/shard_map/all_to_all | solution.py:328
  162.4 16.8 %copy-start = (bf16[8,2,32,768]{3,2,1,0:T(8,128)(2,1)}, bf16[8,2,32,768]{3,2,1,0:T(8,128)(2,1)S(1)}, u32[]{:S(2)}) copy-start(bf16[8,2,32,768]{3,2,1,0:T(8,128)(2,1)S(1)} %all-to-all-done.4.refs_0_) | copy-start | bytes 2359300

commit v2 on v1

v2 whole, which is shorter than its diff:
```python
import functools
import math

import jax
import jax.numpy as jnp
from jax import lax
from jax.experimental import pallas as pl
from jax.experimental.pallas import tpu as pltpu
from jax.sharding import Mesh
from jax.sharding import PartitionSpec as P

HEADS = 12
CORES = 2
SLOT = 16
VMEM_BYTES = 32 * 1024 * 1024

BF16 = jnp.bfloat16
F32 = jnp.float32


def normalize(values):
    center = values - jnp.mean(values, axis=-1, keepdims=True)
    spread = jnp.mean(center * center, axis=-1, keepdims=True)
    return (center * lax.rsqrt(spread + 1e-05)).astype(BF16)


def dot(left, right):
    return jnp.dot(left, right, preferred_element_type=F32)


def dot_nt(left, right):
    return lax.dot_general(left, right, (((1,), (1,)), ((), ())), preferred_element_type=F32)


def head_masks(width, head_dim):
    lane = lax.broadcasted_iota(jnp.int32, (1, width), 1)
    first = (lax.rem(lane, 2 * head_dim) < head_dim).astype(F32)
    return first.astype(BF16), (1.0 - first).astype(BF16)


def permutation(size, source):
    wanted = source(lax.broadcasted_iota(jnp.int32, (size, size), 0))
    return (wanted == lax.broadcasted_iota(jnp.int32, (size, size), 1)).astype(F32).astype(BF16)


def row_project(at_ref, x_ref, wq_ref, wk_ref, wv_ref, *refs):
    q_ref, k_ref, v_ref, kept_ref = refs[-4:]
    rows, block, width = x_ref.shape
    x = x_ref[...]
    kept_ref[...] = x
    normed = normalize(x.astype(F32).reshape(rows * block, width))
    for weight_ref, ref in ((wq_ref, q_ref), (wk_ref, k_ref), (wv_ref, v_ref)):
        ref[...] = dot(normed, weight_ref[...]).astype(BF16).reshape(rows, block, width)


def row_scores(block, chunks, base_ref, q_ref, k_ref, tied_ref):
    rows, cols, pair = q_ref.shape
    first, second = head_masks(pair, pair // 2)
    q = jnp.concatenate([q_ref[row] for row in range(rows)], axis=1)
    keys = jnp.concatenate(
        [
            jnp.concatenate([k_ref[row] * mask for row in range(rows)], axis=1)
            for mask in (first, second)
        ],
        axis=0,
    )
    score = dot_nt(q, keys).reshape(cols // block, block, 2 * cols)
    at = 0
    pieces = []
    for piece in chunks:
        pieces.append(score[:, at : at + piece].reshape(-1, 2 * cols))
        at += piece
    tied_ref[0] = jnp.concatenate(pieces, axis=0)


def row_softmax(scale, parts_ref, prob_ref):
    tied = parts_ref[0]
    for at in range(1, parts_ref.shape[0]):
        tied = tied + parts_ref[at]
    tied = tied * scale
    cols = tied.shape[1] // 2
    halves = []
    for half in (tied[:, :cols], tied[:, cols:]):
        top = jnp.exp(half - jnp.max(half, axis=-1, keepdims=True))
        halves.append(top / jnp.sum(top, axis=-1, keepdims=True))
    prob = jnp.concatenate(halves, axis=1).astype(BF16)
    for at in range(prob_ref.shape[0]):
        prob_ref[at] = prob


def row_update(seq_size, parts, chunks, core_ref, mine_ref, other_ref, v_ref, x_ref, wo_ref, *refs):
    mid_refs, o_ref = refs[:-1], refs[-1]
    rows, cols, width = x_ref.shape
    head_dim = width // HEADS
    pair = 2 * head_dim
    half_pairs = HEADS // 2 // CORES
    masks = head_masks(pair, head_dim)

    for prob_ref, low in ((mine_ref, core_ref[0]), (other_ref, 1 - core_ref[0])):
        for at in range(half_pairs):
            lanes = pl.ds(pl.multiple_of((low * half_pairs + at) * pair, pair), pair)
            prob = prob_ref[at]
            for row in range(0, rows, 2):
                fields = [v_ref[row + step, :, lanes] for step in range(2)]
                values = jnp.concatenate(
                    [
                        jnp.concatenate([field * mask for field in fields], axis=1)
                        for mask in masks
                    ],
                    axis=0,
                )
                result = dot(prob, values).astype(BF16)
                o_ref[row, :, lanes] = result[:, :pair]
                o_ref[row + 1, :, lanes] = result[:, pair:]

    at = 0
    for piece, mid_ref in zip(chunks, mid_refs, strict=True):
        tokens = rows * parts * piece
        inner = piece // seq_size

        def source(token):
            row = lax.rem(token, rows)
            rest = lax.div(token, rows)
            step = lax.rem(rest, inner)
            rest = lax.div(rest, inner)
            part = lax.rem(rest, parts)
            owner = lax.div(rest, parts)
            return (row * parts + part) * piece + owner * inner + step

        attended = o_ref[:, at * parts : (at + piece) * parts, :].reshape(tokens, width)
        residual = x_ref[...].astype(F32).reshape(rows, parts, cols // parts, width)
        residual = residual[:, :, at : at + piece].reshape(tokens, width)
        mid = residual + dot(attended, wo_ref[...])
        mid_ref[...] = dot(permutation(tokens, source), mid.astype(BF16)).astype(BF16)
        at += piece


def column_update(
    at_once, rows, seq_ref, mid_ref, wq_ref, wk_ref, wv_ref, wo_ref, *refs
):
    out_refs, o_ref, updated_ref = refs[:-2], refs[-2], refs[-1]
    total, width = mid_ref.shape
    all_rows = total // at_once
    head_dim = width // HEADS
    pair = 2 * head_dim
    scale = head_dim ** (-0.5)

    mid = mid_ref[...].astype(F32)
    if at_once > 1:
        mid = mid.reshape(all_rows // rows, at_once, rows, width)
        mid = jnp.concatenate(
            [mid[:, at].reshape(all_rows, width) for at in range(at_once)], axis=0
        )
    normed = normalize(mid)
    q = (dot(normed, wq_ref[...]).astype(BF16) * scale).astype(BF16)
    k = dot(normed, wk_ref[...]).astype(BF16)
    v = dot(normed, wv_ref[...]).astype(BF16)
    masks = head_masks(pair, head_dim)
    ones = [jnp.broadcast_to(mask, (all_rows, pair)) for mask in masks]

    for at in range(at_once):
        own = slice(at * all_rows, (at + 1) * all_rows)
        for head in range(HEADS // 2):
            lanes = slice(head * pair, (head + 1) * pair)
            keys = jnp.concatenate([k[own, lanes] * mask for mask in masks], axis=0)
            score = dot_nt(q[own, lanes], keys)
            tops = []
            for half in (score[:, :all_rows], score[:, all_rows:]):
                tops.append(jnp.exp(half - jnp.max(half, axis=-1, keepdims=True)).astype(BF16))
            values = jnp.concatenate(
                [
                    jnp.concatenate([v[own, lanes] * mask, one], axis=1)
                    for mask, one in zip(masks, ones, strict=True)
                ],
                axis=0,
            )
            result = dot(jnp.concatenate(tops, axis=1), values)
            o_ref[own, lanes] = (result[:, :pair] / result[:, pair:]).astype(BF16)

    update = dot(o_ref[...], wo_ref[...]).astype(BF16).astype(F32)
    updated_ref[...] = (mid + update).astype(BF16).reshape(at_once, all_rows, width)
    for step, out_ref in enumerate(out_refs):
        kept = out_ref.shape[1]
        owner = lax.bitwise_xor(seq_ref[0], step)
        out_ref[...] = updated_ref[:, pl.ds(pl.multiple_of(owner * kept, kept), kept), :]


def assemble(seq_size, pieces, seq_ref, *refs):
    out_ref = refs[-1]
    rows, cols, width = out_ref.shape
    tokens = rows * cols

    def source(token):
        row = lax.div(token, cols)
        col = lax.rem(token, cols)
        at, base = 0, jnp.zeros_like(token)
        for piece in pieces:
            inner = piece // seq_size
            local = col - at
            owner = lax.bitwise_xor(lax.div(local, inner), seq_ref[0])
            here = (at + owner * inner + lax.rem(local, inner)) * rows + row
            base = jnp.where((local >= 0) & (local < piece), here, base)
            at += piece
        return base

    gathered = jnp.concatenate(
        [ref[...].reshape(-1, width) for ref in refs[: seq_size * len(pieces)]], axis=0
    )
    moved = dot(permutation(tokens, source), gathered)
    out_ref[...] = moved.astype(BF16).reshape(rows, cols, width)


def whole(shape):
    return pl.BlockSpec(shape, lambda *_: (0,) * len(shape))


def params():
    return pltpu.CompilerParams(vmem_limit_bytes=VMEM_BYTES)


def cost(flops, moved, special=0):
    return pl.CostEstimate(flops=int(flops), bytes_accessed=int(moved), transcendentals=int(special))


def on_device(
    states, row_query, row_key, row_value, row_out, col_query, col_key, col_value, col_out
):
    rows, block, width = states.shape
    pairs_size, res_size = lax.axis_size("pair"), lax.axis_size("res")
    seq_size = pairs_size * CORES
    all_rows, cols = rows * seq_size, block * res_size
    head_dim = width // HEADS
    pair = 2 * head_dim
    own_rows = rows // res_size
    half_pairs = HEADS // 2 // CORES
    core = lax.axis_index("core").astype(jnp.int32)
    seq = lax.axis_index("pair").astype(jnp.int32) * CORES + core
    part = lax.axis_index("res").astype(jnp.int32)
    swap = [(0, 1), (1, 0)]
    smem = pl.BlockSpec(memory_space=pltpu.SMEM)
    vmem = pl.BlockSpec(memory_space=pltpu.VMEM)
    anywhere = pl.BlockSpec(memory_space=pl.ANY)
    inner_all = block // seq_size
    chunks = [SLOT]
    while sum(chunks) < block:
        chunks.append(seq_size)

    def across(field, step):
        return lax.ppermute(field, "res", [(at, at ^ step) for at in range(res_size)])

    def around(field, step):
        return lax.ppermute(
            field, ("pair", "core"), [(at, at ^ step) for at in range(seq_size)]
        )

    blocks = [states]
    for step in range(1, res_size):
        share = lax.dynamic_slice_in_dim(states, (part ^ step) * own_rows, own_rows, axis=0)
        blocks.append(across(share, step))
    share_spec = pl.BlockSpec((own_rows, block, width), lambda g, at: (0, at[0], 0))
    fields = []
    for step, field in enumerate(blocks):
        place = (part ^ step).reshape(1)
        source = (lambda g, at: (at[0], 0, 0)) if step == 0 else (lambda g, at: (0, 0, 0))
        fields = pl.pallas_call(
            row_project,
            grid_spec=pltpu.PrefetchScalarGridSpec(
                num_scalar_prefetch=1,
                grid=(1,),
                in_specs=[pl.BlockSpec((own_rows, block, width), source)]
                + [whole((width, width))] * 3
                + [anywhere] * len(fields),
                out_specs=[share_spec] * 4,
            ),
            out_shape=[jax.ShapeDtypeStruct((own_rows, cols, width), BF16)] * 4,
            input_output_aliases={5 + at: at for at in range(len(fields))},
            compiler_params=params(),
            cost_estimate=cost(6 * own_rows * block * width * width, 6e6),
            name="row_project",
        )(place, field, row_query, row_key, row_value, *fields)
    q, k, v, x = fields

    def scores(base):
        spec = pl.BlockSpec((own_rows, cols, pair), lambda g, at: (0, 0, at[0] + g))
        return pl.pallas_call(
            functools.partial(row_scores, block, chunks),
            grid_spec=pltpu.PrefetchScalarGridSpec(
                num_scalar_prefetch=1,
                grid=(half_pairs,),
                in_specs=[spec, spec],
                out_specs=pl.BlockSpec((1, cols, 2 * cols), lambda g, at: (g, 0, 0)),
            ),
            out_shape=jax.ShapeDtypeStruct((half_pairs, cols, 2 * cols), F32),
            compiler_params=params(),
            cost_estimate=cost(4 * own_rows * cols * cols * pair * half_pairs, 2e6),
            name="row_scores",
        )(base.reshape(1), q, k)

    other = lax.ppermute(scores((1 - core) * half_pairs), "core", swap)
    mine = scores(core * half_pairs)
    shares = pairs_size * res_size
    partial = (mine + other).reshape(shares, half_pairs * cols // shares, 2 * cols)
    partial = lax.all_to_all(partial, ("pair", "res"), split_axis=0, concat_axis=0, tiled=True)
    prob = pl.pallas_call(
        functools.partial(row_softmax, head_dim ** (-0.5) / math.sqrt(all_rows)),
        out_shape=jax.ShapeDtypeStruct(partial.shape, BF16),
        compiler_params=params(),
        name="row_softmax",
    )(partial)
    prob = lax.all_to_all(prob, ("pair", "res"), split_axis=0, concat_axis=0, tiled=True)
    prob = prob.reshape(half_pairs, cols, 2 * cols)
    prob_other = lax.ppermute(prob, "core", swap)

    mids = pl.pallas_call(
        functools.partial(row_update, seq_size, res_size, chunks),
        in_specs=[smem] + [vmem] * 5,
        out_shape=[
            jax.ShapeDtypeStruct((own_rows * res_size * piece, width), BF16) for piece in chunks
        ],
        scratch_shapes=[pltpu.VMEM((own_rows, cols, width), BF16)],
        compiler_params=params(),
        cost_estimate=cost(3 * own_rows * cols * width * width, 8e6),
        name="row_update",
    )(core.reshape(1), prob, prob_other, v, x, row_out)

    home = []
    for piece, mid in zip(chunks, mids, strict=True):
        at_once = piece // seq_size
        tokens = mid.shape[0]
        moved = lax.all_to_all(
            mid, ("pair", "core", "res"), split_axis=0, concat_axis=0, tiled=True
        )
        updated = pl.pallas_call(
            functools.partial(column_update, at_once, own_rows),
            in_specs=[smem] + [vmem] * 5,
            out_shape=[jax.ShapeDtypeStruct((at_once, rows, width), BF16)] * seq_size,
            scratch_shapes=[
                pltpu.VMEM((tokens, width), BF16),
                pltpu.VMEM((at_once, all_rows, width), BF16),
            ],
            compiler_params=params(),
            cost_estimate=cost(10 * tokens * width * width, 8e6, tokens * all_rows * HEADS),
            name="column_update",
        )(seq.reshape(1), moved, col_query, col_key, col_value, col_out)
        home.append(
            [updated[0]] + [around(updated[step], step) for step in range(1, seq_size)]
        )

    row_step = 16
    out = []
    at = 0
    for slot in range(block // SLOT):
        pieces = []
        parts = []
        while sum(pieces) < SLOT:
            pieces.append(chunks[at])
            parts += home[at]
            at += 1
        out = [
            pl.pallas_call(
                functools.partial(assemble, seq_size, pieces),
                grid=(rows // row_step,),
                in_specs=[smem]
                + [
                    pl.BlockSpec((field.shape[0], row_step, width), lambda g: (0, g, 0))
                    for field in parts
                ]
                + [anywhere] * len(out),
                out_specs=pl.BlockSpec((row_step, SLOT, width), lambda g, slot=slot: (g, slot, 0)),
                out_shape=jax.ShapeDtypeStruct((rows, block, width), BF16),
                input_output_aliases={1 + len(parts): 0} if out else {},
                compiler_params=params(),
                name="assemble",
            )(seq.reshape(1), *parts, *out)
        ]
    return out[0]


def solution(mesh):
    seq_size, res_size = mesh.devices.shape
    split = Mesh(
        mesh.devices.reshape(seq_size // CORES, CORES, res_size), ("pair", "core", "res")
    )
    placed = P(("pair", "core"), "res", None)
    return jax.shard_map(
        on_device,
        mesh=split,
        in_specs=(placed,) + (P(),) * 8,
        out_specs=placed,
        check_vma=False,
    )
```

time: 183 us -> 175 us (0.956)
  waiting for transfers between devices: 56.1 us -> 28.1 us
  starting transfers between devices: 14.5 us -> 30.9 us
  local copies, waits for them, and re-layouts: 4.16 us -> 15.5 us
  Pallas kernels: 37.5 us -> 26.9 us
  blocking collectives: 68.9 us -> 71.2 us
    all_to_all x3 -> x1, waiting for transfers between devices: 52.7 us -> 0.01 us  [on_device(): lax.all_to_all(mid, ('pair', 'core', 'res'), split_axis=0, concat_axis=0,...]
    ppermute x1 -> x25, starting transfers between devices: 0.01 us -> 26.4 us  [the longest x21 20.8 us: around(): lax.ppermute(field, ('pair', 'core'), [(at, at ^ step) for at in range(se...]
    ppermute x1 -> x25, waiting for transfers between devices: 1.93 us -> 26.6 us  [the longest x3 18.7 us: across(): lax.ppermute(field, 'res', [(at, at ^ step) for at in range(res_size)])]
    unnamed x10 -> x36, local copies, waits for them, and re-layouts: 1.81 us -> 13.2 us
    all_to_all x3 -> x1, starting transfers between devices: 14.5 us -> 4.54 us  [on_device(): lax.all_to_all(mid, ('pair', 'core', 'res'), split_axis=0, concat_axis=0,...]
    pallas_call x5 -> x12, Pallas kernels: 35.7 us -> 26.7 us  [the longest x3 10.9 us: on_device(): pl.pallas_call(functools.partial(column_update, at_once, own_rows), in_sp...]
    all_to_all x1, blocking collectives: 18.3 us -> 22.8 us  [on_device(): lax.all_to_all(partial, ('pair', 'res'), split_axis=0, concat_axis=0, til...]
    slice x1 -> x0, local copies, waits for them, and re-layouts: 2.35 us -> none  [on_device(): mid[chunk]]
  transfers between devices with their start and end apart: 5 -> 27, of which waited for: 5 -> 10; matrix products, arithmetic and copies ran while one was open for 0% -> 0% of each run, Pallas kernels for 9% -> 11%
where the time goes in v2:
time: 175 us; the launch traced here: 174 us
  blocking collectives  71.2 us (41%)
  starting transfers between devices  30.9 us (18%)
  waiting for transfers between devices  28.1 us (16%)
  Pallas kernels  26.9 us (15%)
  local copies, waits for them, and re-layouts  15.5 us (9%)
    all_to_all x2, blocking collectives, on_device(): lax.all_to_all(mid, ('pair', 'core', 'res'), split_axis=0, concat_axis=0,...  36.9 us
    all_to_all x1, blocking collectives, on_device(): lax.all_to_all(partial, ('pair', 'res'), split_axis=0, concat_axis=0, til...  22.8 us
    ppermute x21, starting transfers between devices, around(): lax.ppermute(field, ('pair', 'core'), [(at, at ^ step) for at in range(se...  20.8 us
    ppermute x3, waiting for transfers between devices, across(): lax.ppermute(field, 'res', [(at, at ^ step) for at in range(res_size)])  18.7 us
    unnamed x36, local copies, waits for them, and re-layouts  13.2 us
    all_to_all x1, blocking collectives, on_device(): lax.all_to_all(prob, ('pair', 'res'), split_axis=0, concat_axis=0, tiled=...  11.5 us
    pallas_call x3, Pallas kernels, on_device(): pl.pallas_call(functools.partial(column_update, at_once, own_rows), in_sp...  10.9 us
    ppermute x21, waiting for transfers between devices, around(): lax.ppermute(field, ('pair', 'core'), [(at, at ^ step) for at in range(se...  7.45 us
  transfers between devices with their start and end apart: 27, of which 10 were waited for; matrix products, arithmetic and copies ran while one was open for 0% of the time, Pallas kernels for 11%

profile of v2, /device:TPU:0, one launch (start us, length us, event | category | flops | bytes accessed | tf_op | source)
XLA Modules:
  0.0 174.2 jit_solution(16293086258791422623)
XLA Ops:
  0.0 2.3 %constant_dynamic-slice_fusion = (bf16[8,32,768]{2,1,0:T(8,128)(2,1)}, bf16[8,32,768]{2,1,0:T(8,128)(2,1)}, bf16[8,32,768]{2,1,0:T(8,128)(2,1)}) fusion(bf16[32,32,768]{2,1,0:T(8,128)(2,1)} %x_ref.1, s32[]{:T(128)S(6)} %select_n.11, s32[]{:T(128)S(6)} %select_n.10, s32[]{:T(128)S(6)} %select_n.9), kind=kLoop, calls=%fused_computation | loop fusion | bytes 2359308 | tf_op jit(solution)/shard_map/dynamic_slice | solution.py:258
  2.3 3.0 %collective-permute-start.2 = (bf16[8,32,768]{2,1,0:T(8,128)(2,1)}, bf16[8,32,768]{2,1,0:T(8,128)(2,1)}, u32[]{:S(2)}, u32[]{:S(2)}) collective-permute-start(bf16[8,32,768]{2,1,0:T(8,128)(2,1)} %get-tuple-element.91), channel_id=1, source_target_pairs={{0,1},{1,0},{2,3},{3,2},{4,5},{5,4},{6,7},{7,6},{8,9},{9,8},{10,11... | collective-permute-start | bytes 1179656 | tf_op jit(solution)/shard_map/ppermute | solution.py:249
  5.3 2.6 %collective-permute-start.1 = (bf16[8,32,768]{2,1,0:T(8,128)(2,1)}, bf16[8,32,768]{2,1,0:T(8,128)(2,1)}, u32[]{:S(2)}, u32[]{:S(2)}) collective-permute-start(bf16[8,32,768]{2,1,0:T(8,128)(2,1)} %get-tuple-element.92), channel_id=1, source_target_pairs={{0,2},{1,3},{2,0},{3,1},{4,6},{5,7},{6,4},{7,5},{8,10},{9,11},{10,... | collective-permute-start | bytes 1179656 | tf_op jit(solution)/shard_map/ppermute | solution.py:249
  14.4 8.0 %collective-permute-done.2.x_ref = bf16[8,32,768]{2,1,0:T(8,128)(2,1)} collective-permute-done((bf16[8,32,768]{2,1,0:T(8,128)(2,1)}, bf16[8,32,768]{2,1,0:T(8,128)(2,1)}, u32[]{:S(2)}, u32[]{:S(2)}) %collective-permute-start.2) | collective-permute-done | bytes 393248 | tf_op jit(solution)/shard_map/ppermute | solution.py:249
  22.4 2.3 %row_project.5 = (bf16[8,128,768]{2,1,0:T(8,128)(2,1)S(1)}, bf16[8,128,768]{2,1,0:T(8,128)(2,1)S(1)}, bf16[8,128,768]{2,1,0:T(8,128)(2,1)S(1)}, bf16[8,128,768]{2,1,0:T(8,128)(2,1)S(1)}) custom-call(s32[1]{0:T(128)} %bitcast.5.at_ref, ...), custom_call_target="tpu_custom_call", output_to_operand_aliasing={{0}: (5, {}), {1}: (6, {}), {2}: (7, {}), {3}: (8, {})} | custom-call | flops 905969664 | bytes 6000000 | tf_op jit(solution)/shard_map/row_project/pallas_call | solution.py:265
  24.7 10.7 %collective-permute-done.1.x_ref = bf16[8,32,768]{2,1,0:T(8,128)(2,1)} collective-permute-done((bf16[8,32,768]{2,1,0:T(8,128)(2,1)}, bf16[8,32,768]{2,1,0:T(8,128)(2,1)}, u32[]{:S(2)}, u32[]{:S(2)}) %collective-permute-start.1) | collective-permute-done | bytes 393248 | tf_op jit(solution)/shard_map/ppermute | solution.py:249
  35.4 2.3 %row_project.6 = (bf16[8,128,768]{2,1,0:T(8,128)(2,1)S(1)}, bf16[8,128,768]{2,1,0:T(8,128)(2,1)S(1)}, bf16[8,128,768]{2,1,0:T(8,128)(2,1)S(1)}, bf16[8,128,768]{2,1,0:T(8,128)(2,1)S(1)}) custom-call(s32[1]{0:T(128)} %bitcast.4.at_ref, ...), custom_call_target="tpu_custom_call", output_to_operand_aliasing={{0}: (5, {}), {1}: (6, {}), {2}: (7, {}), {3}: (8, {})} | custom-call | flops 905969664 | bytes 6000000 | tf_op jit(solution)/shard_map/row_project/pallas_call | solution.py:265
  43.9 22.8 %all_to_all.43.parts_ref = f32[16,24,256]{2,1,0:T(8,128)S(1)} all-to-all(f32[16,24,256]{2,1,0:T(8,128)S(1)} %bitcast.23), channel_id=1, replica_groups=mesh['pair'=4,'core'=2,'res'=4] {'pair','res'}, dimensions={0} | all-to-all | bytes 786432 | tf_op jit(solution)/shard_map/all_to_all | solution.py:303
  66.9 11.5 %all_to_all.44 = bf16[16,24,256]{2,1,0:T(8,128)(2,1)S(1)} all-to-all(bf16[16,24,256]{2,1,0:T(8,128)(2,1)S(1)} %row_softmax.1), channel_id=1, replica_groups=mesh['pair'=4,'core'=2,'res'=4] {'pair','res'}, dimensions={0} | all-to-all | bytes 393216 | tf_op jit(solution)/shard_map/all_to_all | solution.py:310
  79.9 3.3 %row_update.1 = (bf16[512,768]{1,0:T(8,128)(2,1)S(1)}, bf16[256,768]{1,0:T(8,128)(2,1)}, bf16[256,768]{1,0:T(8,128)(2,1)S(1)}) custom-call(s32[1]{0:T(128)} %bitcast.1.core_ref, bf16[3,128,256]{2,1,0:T(8,128)(2,1)S(1)} %bitcast.22, bf16[3,128,256]{2,1,0:T(8,128)(2,1)S(1)} %collective-permute-done.4.other_ref, bf16[8,128,768]{2,1,0:T(8,128)(2,1)S(1)} %copy-done.6, ...), custom_call_target="tpu_custom_call" | custom-call | flops 1811939328 | bytes 8000000 | tf_op jit(solution)/shard_map/row_update/pallas_call | solution.py:314
  83.2 13.7 %all_to_all.45 = bf16[32,8,768]{2,1,0:T(8,128)(2,1)S(1)} all-to-all(bf16[32,8,768]{2,1,0:T(8,128)(2,1)S(1)} %bitcast.20), channel_id=1, replica_groups=mesh['pair'=4,'core'=2,'res'=4] {'pair','core','res'}, dimensions={0} | all-to-all | bytes 786432 | tf_op jit(solution)/shard_map/all_to_all | solution.py:330
  96.8 23.2 %all_to_all.46 = bf16[32,16,768]{2,1,0:T(8,128)(2,1)S(1)} all-to-all(bf16[32,16,768]{2,1,0:T(8,128)(2,1)S(1)} %bitcast.17), channel_id=1, replica_groups=mesh['pair'=4,'core'=2,'res'=4] {'pair','core','res'}, dimensions={0} | all-to-all | bytes 1572864 | tf_op jit(solution)/shard_map/all_to_all | solution.py:330
  120.1 4.5 %all-to-all-start.2 = ((bf16[32,8,768]{2,1,0:T(8,128)(2,1)}), bf16[32,8,768]{2,1,0:T(8,128)(2,1)S(1)}, u32[]{:S(2)}, u32[]{:S(2)}) async-start(bf16[32,8,768]{2,1,0:T(8,128)(2,1)} %bitcast.10), calls=%async_computation.2 | async-start | bytes 786432 | tf_op jit(solution)/shard_map/all_to_all | solution.py:330
  128.5 3.3 %column_update.4 = (bf16[1,32,768]{2,1,0:T(8,128)(2,1)S(1)}, bf16[1,32,768]{2,1,0:T(8,128)(2,1)S(1)}, bf16[1,32,768]{2,1,0:T(8,128)(2,1)S(1)}, bf16[1,32,768]{2,...) custom-call(s32[1]{0:T(128)} %bitcast.seq_ref, ...), custom_call_target="tpu_custom_call" | custom-call | flops 1509949440 | bytes 8000000 | tf_op jit(solution)/shard_map/column_update/pallas_call | solution.py:333
  131.9 1.7 collective-permute-start.13
  133.7 1.6 collective-permute-start.15
  135.4 4.8 %column_update.5 = (bf16[2,32,768]{2,1,0:T(8,128)(2,1)S(1)}, bf16[2,32,768]{2,1,0:T(8,128)(2,1)S(1)}, bf16[2,32,768]{2,1,0:T(8,128)(2,1)S(1)}, bf16[2,32,768]{2,...) custom-call(s32[1]{0:T(128)} %bitcast.seq_ref, ...), custom_call_target="tpu_custom_call" | custom-call | flops 3019898880 | bytes 8000000 | tf_op jit(solution)/shard_map/column_update/pallas_call | solution.py:333
  140.2 2.6 %collective-permute-start.17 = (bf16[1,32,768]{2,1,0:T(8,128)(2,1)}, bf16[1,32,768]{2,1,0:T(8,128)(2,1)S(1)}, u32[]{:S(2)}, u32[]{:S(2)}) collective-permute-start(bf16[1,32,768]{2,1,0:T(8,128)(2,1)} %get-tuple-element.80), channel_id=1, source_target_pairs={{0,24},{4,28},{8,16},{12,20},{16,8},{20,12},{24,0},{28,4},{1,25},{... | collective-permute-start | bytes 147464 | tf_op jit(solution)/shard_map/ppermute | solution.py:252
  147.3 2.7 %column_update.3 = (bf16[1,32,768]{2,1,0:T(8,128)(2,1)S(1)}, bf16[1,32,768]{2,1,0:T(8,128)(2,1)S(1)}, bf16[1,32,768]{2,1,0:T(8,128)(2,1)S(1)}, bf16[1,32,768]{2,...) custom-call(s32[1]{0:T(128)} %bitcast.seq_ref, ...), custom_call_target="tpu_custom_call" | custom-call | flops 1509949440 | bytes 8000000 | tf_op jit(solution)/shard_map/column_update/pallas_call | solution.py:333
  151.3 1.5 collective-permute-start.10
  154.7 1.6 collective-permute-start.21
  156.3 1.9 %collective-permute-start.22 = (bf16[2,32,768]{2,1,0:T(8,128)(2,1)S(1)}, bf16[2,32,768]{2,1,0:T(8,128)(2,1)S(1)}, u32[]{:S(2)}, u32[]{:S(2)}) collective-permute-start(bf16[2,32,768]{2,1,0:T(8,128)(2,1)S(1)} %get-tuple-element.87), channel_id=1, source_target_pairs={{0,16},{4,20},{8,24},{12,28},{16,0},{20,4},{24,8},{28,12},{1,17},{... | collective-permute-start | bytes 294920 | tf_op jit(solution)/shard_map/ppermute | solution.py:252
  158.2 2.0 %collective-permute-start.24 = (bf16[2,32,768]{2,1,0:T(8,128)(2,1)S(1)}, bf16[2,32,768]{2,1,0:T(8,128)(2,1)S(1)}, u32[]{:S(2)}, u32[]{:S(2)}) collective-permute-start(bf16[2,32,768]{2,1,0:T(8,128)(2,1)S(1)} %get-tuple-element.89), channel_id=1, source_target_pairs={{0,24},{4,28},{8,16},{12,20},{16,8},{20,12},{24,0},{28,4},{1,25},{... | collective-permute-start | bytes 294920 | tf_op jit(solution)/shard_map/ppermute | solution.py:252
  162.4 4.9 %collective-permute-done.23.refs_5_ = bf16[2,32,768]{2,1,0:T(8,128)(2,1)S(1)} collective-permute-done((bf16[2,32,768]{2,1,0:T(8,128)(2,1)S(1)}, bf16[2,32,768]{2,1,0:T(8,128)(2,1)S(1)}, u32[]{:S(2)}, u32[]{:S(2)}) %collective-permute-start.23) | collective-permute-done | bytes 98336 | tf_op jit(solution)/shard_map/ppermute | solution.py:252
  (85 shorter events, 35.2 us)
Async XLA Ops:
  2.3 20.1 %collective-permute-start.2 = (bf16[8,32,768]{2,1,0:T(8,128)(2,1)}, bf16[8,32,768]{2,1,0:T(8,128)(2,1)}, u32[]{:S(2)}, u32[]{:S(2)}) collective-permute-start(bf16[8,32,768]{2,1,0:T(8,128)(2,1)} %get-tuple-element.91), channel_id=1, source_target_pairs={{0,1},{1,0},{2,3},{3,2},{4,5},{5,4},{6,7},{7,6},{8,9},{9,8},{10,11... | collective-permute-start | bytes 1179656 | tf_op jit(solution)/shard_map/ppermute | solution.py:249
  5.3 30.1 %collective-permute-start.1 = (bf16[8,32,768]{2,1,0:T(8,128)(2,1)}, bf16[8,32,768]{2,1,0:T(8,128)(2,1)}, u32[]{:S(2)}, u32[]{:S(2)}) collective-permute-start(bf16[8,32,768]{2,1,0:T(8,128)(2,1)} %get-tuple-element.92), channel_id=1, source_target_pairs={{0,2},{1,3},{2,0},{3,1},{4,6},{5,7},{6,4},{7,5},{8,10},{9,11},{10,... | collective-permute-start | bytes 1179656 | tf_op jit(solution)/shard_map/ppermute | solution.py:249
  7.9 29.8 %collective-permute-start = (bf16[8,32,768]{2,1,0:T(8,128)(2,1)}, bf16[8,32,768]{2,1,0:T(8,128)(2,1)S(1)}, u32[]{:S(2)}, u32[]{:S(2)}) collective-permute-start(bf16[8,32,768]{2,1,0:T(8,128)(2,1)} %get-tuple-element.93), channel_id=1, source_target_pairs={{0,3},{1,2},{2,1},{3,0},{4,7},{5,6},{6,5},{7,4},{8,11},{9,10},{10,... | collective-permute-start | bytes 1179656 | tf_op jit(solution)/shard_map/ppermute | solution.py:249
  120.1 23.4 %all-to-all-start.2 = ((bf16[32,8,768]{2,1,0:T(8,128)(2,1)}), bf16[32,8,768]{2,1,0:T(8,128)(2,1)S(1)}, u32[]{:S(2)}, u32[]{:S(2)}) async-start(bf16[32,8,768]{2,1,0:T(8,128)(2,1)} %bitcast.10), calls=%async_computation.2 | async-start | bytes 786432 | tf_op jit(solution)/shard_map/all_to_all | solution.py:330
  131.8 8.4 %collective-permute-start.12 = (bf16[1,32,768]{2,1,0:T(8,128)(2,1)S(1)}, bf16[1,32,768]{2,1,0:T(8,128)(2,1)S(1)}, u32[]{:S(2)}, u32[]{:S(2)}) collective-permute-start(bf16[1,32,768]{2,1,0:T(8,128)(2,1)S(1)} %get-tuple-element.75), channel_id=1, source_target_pairs={{0,4},{4,0},{8,12},{12,8},{16,20},{20,16},{24,28},{28,24},{1,5},{5... | collective-permute-start | bytes 147464 | tf_op jit(solution)/shard_map/ppermute | solution.py:252
  131.9 11.0 %collective-permute-start.13 = (bf16[1,32,768]{2,1,0:T(8,128)(2,1)S(1)}, bf16[1,32,768]{2,1,0:T(8,128)(2,1)S(1)}, u32[]{:S(2)}, u32[]{:S(2)}) collective-permute-start(bf16[1,32,768]{2,1,0:T(8,128)(2,1)S(1)} %get-tuple-element.76), channel_id=1, source_target_pairs={{0,8},{4,12},{8,0},{12,4},{16,24},{20,28},{24,16},{28,20},{1,9},{5... | collective-permute-start | bytes 147464 | tf_op jit(solution)/shard_map/ppermute | solution.py:252
  133.6 9.4 %collective-permute-start.14 = (bf16[1,32,768]{2,1,0:T(8,128)(2,1)S(1)}, bf16[1,32,768]{2,1,0:T(8,128)(2,1)S(1)}, u32[]{:S(2)}, u32[]{:S(2)}) collective-permute-start(bf16[1,32,768]{2,1,0:T(8,128)(2,1)S(1)} %get-tuple-element.77), channel_id=1, source_target_pairs={{0,12},{4,8},{8,4},{12,0},{16,28},{20,24},{24,20},{28,16},{1,13},{... | collective-permute-start | bytes 147464 | tf_op jit(solution)/shard_map/ppermute | solution.py:252
  133.7 16.4 %collective-permute-start.15 = (bf16[1,32,768]{2,1,0:T(8,128)(2,1)}, bf16[1,32,768]{2,1,0:T(8,128)(2,1)S(1)}, u32[]{:S(2)}, u32[]{:S(2)}) collective-permute-start(bf16[1,32,768]{2,1,0:T(8,128)(2,1)} %get-tuple-element.78), channel_id=1, source_target_pairs={{0,16},{4,20},{8,24},{12,28},{16,0},{20,4},{24,8},{28,12},{1,17},{... | collective-permute-start | bytes 147464 | tf_op jit(solution)/shard_map/ppermute | solution.py:252
  135.3 16.1 %collective-permute-start.16 = (bf16[1,32,768]{2,1,0:T(8,128)(2,1)}, bf16[1,32,768]{2,1,0:T(8,128)(2,1)S(1)}, u32[]{:S(2)}, u32[]{:S(2)}) collective-permute-start(bf16[1,32,768]{2,1,0:T(8,128)(2,1)} %get-tuple-element.79), channel_id=1, source_target_pairs={{0,20},{4,16},{8,28},{12,24},{16,4},{20,0},{24,12},{28,8},{1,21},{... | collective-permute-start | bytes 147464 | tf_op jit(solution)/shard_map/ppermute | solution.py:252
  140.2 12.6 %collective-permute-start.17 = (bf16[1,32,768]{2,1,0:T(8,128)(2,1)}, bf16[1,32,768]{2,1,0:T(8,128)(2,1)S(1)}, u32[]{:S(2)}, u32[]{:S(2)}) collective-permute-start(bf16[1,32,768]{2,1,0:T(8,128)(2,1)} %get-tuple-element.80), channel_id=1, source_target_pairs={{0,24},{4,28},{8,16},{12,20},{16,8},{20,12},{24,0},{28,4},{1,25},{... | collective-permute-start | bytes 147464 | tf_op jit(solution)/shard_map/ppermute | solution.py:252
  142.9 15.4 %collective-permute-start.19 = (bf16[2,32,768]{2,1,0:T(8,128)(2,1)S(1)}, bf16[2,32,768]{2,1,0:T(8,128)(2,1)S(1)}, u32[]{:S(2)}, u32[]{:S(2)}) collective-permute-start(bf16[2,32,768]{2,1,0:T(8,128)(2,1)S(1)} %get-tuple-element.84), channel_id=1, source_target_pairs={{0,4},{4,0},{8,12},{12,8},{16,20},{20,16},{24,28},{28,24},{1,5},{5... | collective-permute-start | bytes 294920 | tf_op jit(solution)/shard_map/ppermute | solution.py:252
  142.9 17.3 %collective-permute-start.20 = (bf16[2,32,768]{2,1,0:T(8,128)(2,1)S(1)}, bf16[2,32,768]{2,1,0:T(8,128)(2,1)S(1)}, u32[]{:S(2)}, u32[]{:S(2)}) collective-permute-start(bf16[2,32,768]{2,1,0:T(8,128)(2,1)S(1)} %get-tuple-element.85), channel_id=1, source_target_pairs={{0,8},{4,12},{8,0},{12,4},{16,24},{20,28},{24,16},{28,20},{1,9},{5... | collective-permute-start | bytes 294920 | tf_op jit(solution)/shard_map/ppermute | solution.py:252
  150.0 4.7 %collective-permute-start.18 = (bf16[1,32,768]{2,1,0:T(8,128)(2,1)S(1)}, bf16[1,32,768]{2,1,0:T(8,128)(2,1)S(1)}, u32[]{:S(2)}, u32[]{:S(2)}) collective-permute-start(bf16[1,32,768]{2,1,0:T(8,128)(2,1)S(1)} %get-tuple-element.81), channel_id=1, source_target_pairs={{0,28},{4,24},{8,20},{12,16},{16,12},{20,8},{24,4},{28,0},{1,29},{... | collective-permute-start | bytes 147464 | tf_op jit(solution)/shard_map/ppermute | solution.py:252
  151.3 5.0 %collective-permute-start.10 = (bf16[1,32,768]{2,1,0:T(8,128)(2,1)S(1)}, bf16[1,32,768]{2,1,0:T(8,128)(2,1)S(1)}, u32[]{:S(2)}, u32[]{:S(2)}) collective-permute-start(bf16[1,32,768]{2,1,0:T(8,128)(2,1)S(1)} %get-tuple-element.71), channel_id=1, source_target_pairs={{0,24},{4,28},{8,16},{12,20},{16,8},{20,12},{24,0},{28,4},{1,25},{... | collective-permute-start | bytes 147464 | tf_op jit(solution)/shard_map/ppermute | solution.py:252
  152.8 5.4 %collective-permute-start.11 = (bf16[1,32,768]{2,1,0:T(8,128)(2,1)S(1)}, bf16[1,32,768]{2,1,0:T(8,128)(2,1)S(1)}, u32[]{:S(2)}, u32[]{:S(2)}) collective-permute-start(bf16[1,32,768]{2,1,0:T(8,128)(2,1)S(1)} %get-tuple-element.72), channel_id=1, source_target_pairs={{0,28},{4,24},{8,20},{12,16},{16,12},{20,8},{24,4},{28,0},{1,29},{... | collective-permute-start | bytes 147464 | tf_op jit(solution)/shard_map/ppermute | solution.py:252
  154.7 6.0 %collective-permute-start.21 = (bf16[2,32,768]{2,1,0:T(8,128)(2,1)S(1)}, bf16[2,32,768]{2,1,0:T(8,128)(2,1)S(1)}, u32[]{:S(2)}, u32[]{:S(2)}) collective-permute-start(bf16[2,32,768]{2,1,0:T(8,128)(2,1)S(1)} %get-tuple-element.86), channel_id=1, source_target_pairs={{0,12},{4,8},{8,4},{12,0},{16,28},{20,24},{24,20},{28,16},{1,13},{... | collective-permute-start | bytes 294920 | tf_op jit(solution)/shard_map/ppermute | solution.py:252
  156.3 5.0 %collective-permute-start.22 = (bf16[2,32,768]{2,1,0:T(8,128)(2,1)S(1)}, bf16[2,32,768]{2,1,0:T(8,128)(2,1)S(1)}, u32[]{:S(2)}, u32[]{:S(2)}) collective-permute-start(bf16[2,32,768]{2,1,0:T(8,128)(2,1)S(1)} %get-tuple-element.87), channel_id=1, source_target_pairs={{0,16},{4,20},{8,24},{12,28},{16,0},{20,4},{24,8},{28,12},{1,17},{... | collective-permute-start | bytes 294920 | tf_op jit(solution)/shard_map/ppermute | solution.py:252
  158.2 9.1 %collective-permute-start.23 = (bf16[2,32,768]{2,1,0:T(8,128)(2,1)S(1)}, bf16[2,32,768]{2,1,0:T(8,128)(2,1)S(1)}, u32[]{:S(2)}, u32[]{:S(2)}) collective-permute-start(bf16[2,32,768]{2,1,0:T(8,128)(2,1)S(1)} %get-tuple-element.88), channel_id=1, source_target_pairs={{0,20},{4,16},{8,28},{12,24},{16,4},{20,0},{24,12},{28,8},{1,21},{... | collective-permute-start | bytes 294920 | tf_op jit(solution)/shard_map/ppermute | solution.py:252
  158.2 9.9 %collective-permute-start.24 = (bf16[2,32,768]{2,1,0:T(8,128)(2,1)S(1)}, bf16[2,32,768]{2,1,0:T(8,128)(2,1)S(1)}, u32[]{:S(2)}, u32[]{:S(2)}) collective-permute-start(bf16[2,32,768]{2,1,0:T(8,128)(2,1)S(1)} %get-tuple-element.89), channel_id=1, source_target_pairs={{0,24},{4,28},{8,16},{12,20},{16,8},{20,12},{24,0},{28,4},{1,25},{... | collective-permute-start | bytes 294920 | tf_op jit(solution)/shard_map/ppermute | solution.py:252
  160.2 8.6 %collective-permute-start.25 = (bf16[2,32,768]{2,1,0:T(8,128)(2,1)S(1)}, bf16[2,32,768]{2,1,0:T(8,128)(2,1)S(1)}, u32[]{:S(2)}, u32[]{:S(2)}) collective-permute-start(bf16[2,32,768]{2,1,0:T(8,128)(2,1)S(1)} %get-tuple-element.90), channel_id=1, source_target_pairs={{0,28},{4,24},{8,20},{12,16},{16,12},{20,8},{24,4},{28,0},{1,29},{... | collective-permute-start | bytes 294920 | tf_op jit(solution)/shard_map/ppermute | solution.py:252
  160.7 10.4 %collective-permute-start.5 = (bf16[1,32,768]{2,1,0:T(8,128)(2,1)S(1)}, bf16[1,32,768]{2,1,0:T(8,128)(2,1)S(1)}, u32[]{:S(2)}, u32[]{:S(2)}) collective-permute-start(bf16[1,32,768]{2,1,0:T(8,128)(2,1)S(1)} %get-tuple-element.66), channel_id=1, source_target_pairs={{0,4},{4,0},{8,12},{12,8},{16,20},{20,16},{24,28},{28,24},{1,5},{5... | collective-permute-start | bytes 147464 | tf_op jit(solution)/shard_map/ppermute | solution.py:252
  161.3 9.8 %collective-permute-start.6 = (bf16[1,32,768]{2,1,0:T(8,128)(2,1)S(1)}, bf16[1,32,768]{2,1,0:T(8,128)(2,1)S(1)}, u32[]{:S(2)}, u32[]{:S(2)}) collective-permute-start(bf16[1,32,768]{2,1,0:T(8,128)(2,1)S(1)} %get-tuple-element.67), channel_id=1, source_target_pairs={{0,8},{4,12},{8,0},{12,4},{16,24},{20,28},{24,16},{28,20},{1,9},{5... | collective-permute-start | bytes 147464 | tf_op jit(solution)/shard_map/ppermute | solution.py:252
  168.2 4.6 %collective-permute-start.8 = (bf16[1,32,768]{2,1,0:T(8,128)(2,1)S(1)}, bf16[1,32,768]{2,1,0:T(8,128)(2,1)S(1)}, u32[]{:S(2)}, u32[]{:S(2)}) collective-permute-start(bf16[1,32,768]{2,1,0:T(8,128)(2,1)S(1)} %get-tuple-element.69), channel_id=1, source_target_pairs={{0,16},{4,20},{8,24},{12,28},{16,0},{20,4},{24,8},{28,12},{1,17},{... | collective-permute-start | bytes 147464 | tf_op jit(solution)/shard_map/ppermute | solution.py:252
  168.8 4.0 %collective-permute-start.9 = (bf16[1,32,768]{2,1,0:T(8,128)(2,1)S(1)}, bf16[1,32,768]{2,1,0:T(8,128)(2,1)S(1)}, u32[]{:S(2)}, u32[]{:S(2)}) collective-permute-start(bf16[1,32,768]{2,1,0:T(8,128)(2,1)S(1)} %get-tuple-element.70), channel_id=1, source_target_pairs={{0,20},{4,16},{8,28},{12,24},{16,4},{20,0},{24,12},{28,8},{1,21},{... | collective-permute-start | bytes 147464 | tf_op jit(solution)/shard_map/ppermute | solution.py:252
  (21 other events, 198.0 us)

commit v3 on v2

--- a/solution.py
+++ b/solution.py
@@ -12,7 +12,8 @@
 HEADS = 12
 CORES = 2
 SLOT = 16
-VMEM_BYTES = 32 * 1024 * 1024
+VMEM_BYTES = 24 * 1024 * 1024
+FULL_VMEM_BYTES = 64_000_000
 
 BF16 = jnp.bfloat16
 F32 = jnp.float32
@@ -41,6 +42,27 @@
 def permutation(size, source):
     wanted = source(lax.broadcasted_iota(jnp.int32, (size, size), 0))
     return (wanted == lax.broadcasted_iota(jnp.int32, (size, size), 1)).astype(F32).astype(BF16)
+
+
+def row_shares(part_ref, states_any, *refs):
+    out_refs, (held_ref, in_sems, out_sems) = refs[:-3], refs[-3:]
+    rows = held_ref.shape[1]
+    arrivals, departures = [], []
+    for at, out_ref in enumerate(out_refs):
+        owner = lax.bitwise_xor(part_ref[0], at + 1)
+        arrivals.append(
+            pltpu.make_async_copy(
+                states_any.at[pl.ds(owner * rows, rows)], held_ref.at[at], in_sems.at[at]
+            )
+        )
+        departures.append(pltpu.make_async_copy(held_ref.at[at], out_ref, out_sems.at[at]))
+    for copy in arrivals:
+        copy.start()
+    for arrival, departure in zip(arrivals, departures, strict=True):
+        arrival.wait()
+        departure.start()
+    for copy in departures:
+        copy.wait()
 
 
 def row_project(at_ref, x_ref, wq_ref, wk_ref, wv_ref, *refs):
@@ -88,8 +110,7 @@
         prob_ref[at] = prob
 
 
-def row_update(seq_size, parts, chunks, core_ref, mine_ref, other_ref, v_ref, x_ref, wo_ref, *refs):
-    mid_refs, o_ref = refs[:-1], refs[-1]
+def row_update(seq_size, parts, chunks, core_ref, mine_ref, other_ref, v_ref, x_ref, wo_ref, mid_ref, o_ref):
     rows, cols, width = x_ref.shape
     head_dim = width // HEADS
     pair = 2 * head_dim
@@ -114,7 +135,8 @@
                 o_ref[row + 1, :, lanes] = result[:, pair:]
 
     at = 0
-    for piece, mid_ref in zip(chunks, mid_refs, strict=True):
+    step_at = 0
+    for piece in chunks:
         tokens = rows * parts * piece
         inner = piece // seq_size
 
@@ -131,26 +153,21 @@
         residual = x_ref[...].astype(F32).reshape(rows, parts, cols // parts, width)
         residual = residual[:, :, at : at + piece].reshape(tokens, width)
         mid = residual + dot(attended, wo_ref[...])
-        mid_ref[...] = dot(permutation(tokens, source), mid.astype(BF16)).astype(BF16)
+        moved = dot(permutation(tokens, source), mid.astype(BF16)).astype(BF16)
+        mid_ref[:, step_at : step_at + inner] = moved.reshape(-1, inner, rows, width)
         at += piece
-
-
-def column_update(
-    at_once, rows, seq_ref, mid_ref, wq_ref, wk_ref, wv_ref, wo_ref, *refs
-):
+        step_at += inner
+
+
+def column_update(first_at, seq_ref, mid_ref, wq_ref, wk_ref, wv_ref, wo_ref, *refs):
     out_refs, o_ref, updated_ref = refs[:-2], refs[-2], refs[-1]
-    total, width = mid_ref.shape
-    all_rows = total // at_once
+    at_once, all_rows, width = updated_ref.shape
     head_dim = width // HEADS
     pair = 2 * head_dim
     scale = head_dim ** (-0.5)
 
-    mid = mid_ref[...].astype(F32)
-    if at_once > 1:
-        mid = mid.reshape(all_rows // rows, at_once, rows, width)
-        mid = jnp.concatenate(
-            [mid[:, at].reshape(all_rows, width) for at in range(at_once)], axis=0
-        )
+    mid = mid_ref[:, first_at : first_at + at_once].astype(F32)
+    mid = jnp.concatenate([mid[:, at].reshape(all_rows, width) for at in range(at_once)], axis=0)
     normed = normalize(mid)
     q = (dot(normed, wq_ref[...]).astype(BF16) * scale).astype(BF16)
     k = dot(normed, wk_ref[...]).astype(BF16)
@@ -179,10 +196,17 @@
 
     update = dot(o_ref[...], wo_ref[...]).astype(BF16).astype(F32)
     updated_ref[...] = (mid + update).astype(BF16).reshape(at_once, all_rows, width)
+    kept = out_refs[0].shape[2]
     for step, out_ref in enumerate(out_refs):
-        kept = out_ref.shape[1]
-        owner = lax.bitwise_xor(seq_ref[0], step)
-        out_ref[...] = updated_ref[:, pl.ds(pl.multiple_of(owner * kept, kept), kept), :]
+        for other in range(CORES):
+            owner = lax.bitwise_xor(seq_ref[0], step * CORES + other)
+            out_ref[other] = updated_ref[:, pl.ds(pl.multiple_of(owner * kept, kept), kept), :]
+
+
+def in_order(refs, at, pairs_size):
+    straight = refs[at * (pairs_size + 1) : at * (pairs_size + 1) + pairs_size]
+    crossed = refs[at * (pairs_size + 1) + pairs_size]
+    return [field for step in range(pairs_size) for field in (straight[step][0], crossed[step])]
 
 
 def assemble(seq_size, pieces, seq_ref, *refs):
@@ -204,7 +228,12 @@
         return base
 
     gathered = jnp.concatenate(
-        [ref[...].reshape(-1, width) for ref in refs[: seq_size * len(pieces)]], axis=0
+        [
+            field.reshape(-1, width)
+            for at in range(len(pieces))
+            for field in in_order(refs, at, seq_size // CORES)
+        ],
+        axis=0,
     )
     moved = dot(permutation(tokens, source), gathered)
     out_ref[...] = moved.astype(BF16).reshape(rows, cols, width)
@@ -214,8 +243,8 @@
     return pl.BlockSpec(shape, lambda *_: (0,) * len(shape))
 
 
-def params():
-    return pltpu.CompilerParams(vmem_limit_bytes=VMEM_BYTES)
+def params(limit=VMEM_BYTES):
+    return pltpu.CompilerParams(vmem_limit_bytes=limit)
 
 
 def cost(flops, moved, special=0):
@@ -240,27 +269,37 @@
     smem = pl.BlockSpec(memory_space=pltpu.SMEM)
     vmem = pl.BlockSpec(memory_space=pltpu.VMEM)
     anywhere = pl.BlockSpec(memory_space=pl.ANY)
-    inner_all = block // seq_size
-    chunks = [SLOT]
-    while sum(chunks) < block:
-        chunks.append(seq_size)
+    chunks = [SLOT] * (block // SLOT)
 
     def across(field, step):
         return lax.ppermute(field, "res", [(at, at ^ step) for at in range(res_size)])
 
     def around(field, step):
-        return lax.ppermute(
-            field, ("pair", "core"), [(at, at ^ step) for at in range(seq_size)]
-        )
-
-    blocks = [states]
-    for step in range(1, res_size):
-        share = lax.dynamic_slice_in_dim(states, (part ^ step) * own_rows, own_rows, axis=0)
-        blocks.append(across(share, step))
+        return lax.ppermute(field, "pair", [(at, at ^ step) for at in range(pairs_size)])
+
+    shares = pl.pallas_call(
+        row_shares,
+        in_specs=[smem, anywhere],
+        out_specs=[anywhere] * (res_size - 1),
+        out_shape=[jax.ShapeDtypeStruct((own_rows, block, width), BF16)] * (res_size - 1),
+        scratch_shapes=[
+            pltpu.VMEM((res_size - 1, own_rows, block, width), BF16),
+            pltpu.SemaphoreType.DMA((res_size - 1,)),
+            pltpu.SemaphoreType.DMA((res_size - 1,)),
+        ],
+        compiler_params=params(FULL_VMEM_BYTES),
+        name="row_shares",
+    )(part.reshape(1), states)
+    blocks = [states] + [across(share, step + 1) for step, share in enumerate(shares)]
+    halves = ((1 - core) * half_pairs).reshape(1), (core * half_pairs).reshape(1)
+    places = [(part ^ step).reshape(1) for step in range(res_size)]
+    own, halves, core_place, place, places = lax.optimization_barrier(
+        (blocks[0], halves, core.reshape(1), seq.reshape(1), places)
+    )
+    blocks[0] = own
     share_spec = pl.BlockSpec((own_rows, block, width), lambda g, at: (0, at[0], 0))
     fields = []
     for step, field in enumerate(blocks):
-        place = (part ^ step).reshape(1)
         source = (lambda g, at: (at[0], 0, 0)) if step == 0 else (lambda g, at: (0, 0, 0))
         fields = pl.pallas_call(
             row_project,
@@ -277,7 +316,7 @@
             compiler_params=params(),
             cost_estimate=cost(6 * own_rows * block * width * width, 6e6),
             name="row_project",
-        )(place, field, row_query, row_key, row_value, *fields)
+        )(places[step], field, row_query, row_key, row_value, *fields)
     q, k, v, x = fields
 
     def scores(base):
@@ -294,12 +333,12 @@
             compiler_params=params(),
             cost_estimate=cost(4 * own_rows * cols * cols * pair * half_pairs, 2e6),
             name="row_scores",
-        )(base.reshape(1), q, k)
-
-    other = lax.ppermute(scores((1 - core) * half_pairs), "core", swap)
-    mine = scores(core * half_pairs)
-    shares = pairs_size * res_size
-    partial = (mine + other).reshape(shares, half_pairs * cols // shares, 2 * cols)
+        )(base, q, k)
+
+    other = lax.ppermute(scores(halves[0]), "core", swap)
+    mine = scores(halves[1])
+    owners = pairs_size * res_size
+    partial = (mine + other).reshape(owners, half_pairs * cols // owners, 2 * cols)
     partial = lax.all_to_all(partial, ("pair", "res"), split_axis=0, concat_axis=0, tiled=True)
     prob = pl.pallas_call(
         functools.partial(row_softmax, head_dim ** (-0.5) / math.sqrt(all_rows)),
@@ -311,29 +350,28 @@
     prob = prob.reshape(half_pairs, cols, 2 * cols)
     prob_other = lax.ppermute(prob, "core", swap)
 
-    mids = pl.pallas_call(
+    mid = pl.pallas_call(
         functools.partial(row_update, seq_size, res_size, chunks),
         in_specs=[smem] + [vmem] * 5,
-        out_shape=[
-            jax.ShapeDtypeStruct((own_rows * res_size * piece, width), BF16) for piece in chunks
-        ],
+        out_shape=jax.ShapeDtypeStruct(
+            (seq_size * res_size, block // seq_size, own_rows, width), BF16
+        ),
         scratch_shapes=[pltpu.VMEM((own_rows, cols, width), BF16)],
         compiler_params=params(),
         cost_estimate=cost(3 * own_rows * cols * width * width, 8e6),
         name="row_update",
-    )(core.reshape(1), prob, prob_other, v, x, row_out)
-
+    )(core_place, prob, prob_other, v, x, row_out)
+
+    moved = lax.all_to_all(mid, ("pair", "core", "res"), split_axis=0, concat_axis=0, tiled=True)
     home = []
-    for piece, mid in zip(chunks, mids, strict=True):
+    first_at = 0
+    for piece in chunks:
         at_once = piece // seq_size
-        tokens = mid.shape[0]
-        moved = lax.all_to_all(
-            mid, ("pair", "core", "res"), split_axis=0, concat_axis=0, tiled=True
-        )
+        tokens = at_once * all_rows
         updated = pl.pallas_call(
-            functools.partial(column_update, at_once, own_rows),
+            functools.partial(column_update, first_at),
             in_specs=[smem] + [vmem] * 5,
-            out_shape=[jax.ShapeDtypeStruct((at_once, rows, width), BF16)] * seq_size,
+            out_shape=[jax.ShapeDtypeStruct((CORES, at_once, rows, width), BF16)] * pairs_size,
             scratch_shapes=[
                 pltpu.VMEM((tokens, width), BF16),
                 pltpu.VMEM((at_once, all_rows, width), BF16),
@@ -341,20 +379,21 @@
             compiler_params=params(),
             cost_estimate=cost(10 * tokens * width * width, 8e6, tokens * all_rows * HEADS),
             name="column_update",
-        )(seq.reshape(1), moved, col_query, col_key, col_value, col_out)
-        home.append(
-            [updated[0]] + [around(updated[step], step) for step in range(1, seq_size)]
-        )
+        )(place, moved, col_query, col_key, col_value, col_out)
+        first_at += at_once
+        arrived = [updated[0]] + [around(updated[step], step) for step in range(1, pairs_size)]
+        crossed = lax.ppermute(jnp.stack([field[1] for field in arrived]), "core", swap)
+        home.append(arrived + [crossed])
 
     row_step = 16
     out = []
     at = 0
     for slot in range(block // SLOT):
-        pieces = []
-        parts = []
+        pieces, parts, counts = [], [], []
         while sum(pieces) < SLOT:
             pieces.append(chunks[at])
             parts += home[at]
+            counts += [1] * pairs_size + [pairs_size]
             at += 1
         out = [
             pl.pallas_call(
@@ -362,8 +401,8 @@
                 grid=(rows // row_step,),
                 in_specs=[smem]
                 + [
-                    pl.BlockSpec((field.shape[0], row_step, width), lambda g: (0, g, 0))
-                    for field in parts
+                    pl.BlockSpec((count, field.shape[1], row_step, width), lambda g: (0, 0, g, 0))
+                    for field, count in zip(parts, counts, strict=True)
                 ]
                 + [anywhere] * len(out),
                 out_specs=pl.BlockSpec((row_step, SLOT, width), lambda g, slot=slot: (g, slot, 0)),
@@ -371,7 +410,7 @@
                 input_output_aliases={1 + len(parts): 0} if out else {},
                 compiler_params=params(),
                 name="assemble",
-            )(seq.reshape(1), *parts, *out)
+            )(place, *parts, *out)
         ]
     return out[0]
 

time: 175 us -> 151 us (0.86)
  starting transfers between devices: 30.9 us -> 13 us
  local copies, waits for them, and re-layouts: 15.5 us -> 4.05 us
  waiting for transfers between devices: 28.1 us -> 32.6 us
  blocking collectives: 71.2 us -> 74.7 us
    ppermute x22 -> x9, starting transfers between devices: 20.8 us -> 7.35 us  [the longest x6 7.11 us: around(): lax.ppermute(field, 'pair', [(at, at ^ step) for at in range(pairs_size)])]
    unnamed x36 -> x22, local copies, waits for them, and re-layouts: 13.2 us -> 3.99 us
    all_to_all x1 -> x0, starting transfers between devices: 4.54 us -> none  [on_device(): lax.all_to_all(mid, ('pair', 'core', 'res'), split_axis=0, concat_axis=0,...]
    ppermute x22 -> x9, waiting for transfers between devices: 7.97 us -> 10.4 us  [the longest x6 9.72 us: around(): lax.ppermute(field, 'pair', [(at, at ^ step) for at in range(pairs_size)])]
    dynamic_slice x1 -> x0, local copies, waits for them, and re-layouts: 2.28 us -> none  [on_device(): lax.dynamic_slice_in_dim(states, (part ^ step) * own_rows, own_rows, axis=0)]
    ppermute x3, waiting for transfers between devices: 18.7 us -> 20.8 us  [across(): lax.ppermute(field, 'res', [(at, at ^ step) for at in range(res_size)])]
    pallas_call x4, Pallas kernels: 7.22 us -> 5.23 us  [on_device(): pl.pallas_call(row_project, grid_spec=pltpu.PrefetchScalarGridSpec(num_sc...]
    all_to_all x2 -> x1, blocking collectives: 36.9 us -> 38.7 us  [on_device(): lax.all_to_all(mid, ('pair', 'core', 'res'), split_axis=0, concat_axis=0,...]
  transfers between devices with their start and end apart: 27 -> 13, of which waited for: 10 -> 8; matrix products, arithmetic and copies ran while one was open for 0% -> 0% of each run, Pallas kernels for 11% -> 8%
where the time goes in v3:
time: 151 us
  blocking collectives  74.7 us (49%)
  waiting for transfers between devices  32.6 us (22%)
  Pallas kernels  25.7 us (17%)
  starting transfers between devices  13 us (9%)
  local copies, waits for them, and re-layouts  4.05 us (3%)
    all_to_all x1, blocking collectives, on_device(): lax.all_to_all(mid, ('pair', 'core', 'res'), split_axis=0, concat_axis=0,...  38.7 us
    all_to_all x1, blocking collectives, on_device(): lax.all_to_all(partial, ('pair', 'res'), split_axis=0, concat_axis=0, til...  24.1 us
    ppermute x3, waiting for transfers between devices, across(): lax.ppermute(field, 'res', [(at, at ^ step) for at in range(res_size)])  20.8 us
    all_to_all x1, blocking collectives, on_device(): lax.all_to_all(prob, ('pair', 'res'), split_axis=0, concat_axis=0, tiled=...  11.9 us
    ppermute x6, waiting for transfers between devices, around(): lax.ppermute(field, 'pair', [(at, at ^ step) for at in range(pairs_size)])  9.72 us
    pallas_call x2, Pallas kernels, on_device(): pl.pallas_call(functools.partial(column_update, first_at), in_specs=[smem...  9.65 us
    ppermute x6, starting transfers between devices, around(): lax.ppermute(field, 'pair', [(at, at ^ step) for at in range(pairs_size)])  7.11 us
    ppermute x3, starting transfers between devices, across(): lax.ppermute(field, 'res', [(at, at ^ step) for at in range(res_size)])  5.68 us
  transfers between devices with their start and end apart: 13, of which 8 were waited for; matrix products, arithmetic and copies ran while one was open for 0% of the time, Pallas kernels for 8%

profile of v3, /device:TPU:0, one launch (start us, length us, event | category | flops | bytes accessed | tf_op | source)
XLA Modules:
  0.0 150.5 jit_solution(13667262774484461564)
XLA Ops:
  0.0 2.2 %row_shares.1 = (bf16[8,32,768]{2,1,0:T(8,128)(2,1)}, bf16[8,32,768]{2,1,0:T(8,128)(2,1)}, bf16[8,32,768]{2,1,0:T(8,128)(2,1)}) custom-call(s32[1]{0:T(128)} %bitcast.4.part_ref.at_ref, bf16[32,32,768]{2,1,0:T(8,128)(2,1)} %x_ref), custom_call_target="tpu_custom_call" | custom-call | tf_op jit(solution)/shard_map/row_shares/pallas_call | solution.py:280
  2.2 3.1 %collective-permute-start.2 = (bf16[8,32,768]{2,1,0:T(8,128)(2,1)}, bf16[8,32,768]{2,1,0:T(8,128)(2,1)S(1)}, u32[]{:S(2)}, u32[]{:S(2)}) collective-permute-start(bf16[8,32,768]{2,1,0:T(8,128)(2,1)} %get-tuple-element.49), channel_id=1, source_target_pairs={{0,1},{1,0},{2,3},{3,2},{4,5},{5,4},{6,7},{7,6},{8,9},{9,8},{10,11... | collective-permute-start | bytes 1179656 | tf_op jit(solution)/shard_map/ppermute | solution.py:275
  5.3 2.6 %collective-permute-start.1 = (bf16[8,32,768]{2,1,0:T(8,128)(2,1)}, bf16[8,32,768]{2,1,0:T(8,128)(2,1)S(1)}, u32[]{:S(2)}, u32[]{:S(2)}) collective-permute-start(bf16[8,32,768]{2,1,0:T(8,128)(2,1)} %get-tuple-element.47), channel_id=1, source_target_pairs={{0,2},{1,3},{2,0},{3,1},{4,6},{5,7},{6,4},{7,5},{8,10},{9,11},{10,... | collective-permute-start | bytes 1179656 | tf_op jit(solution)/shard_map/ppermute | solution.py:275
  10.4 1.4 copy-done.5
  13.1 9.1 %collective-permute-done.2.x_ref = bf16[8,32,768]{2,1,0:T(8,128)(2,1)S(1)} collective-permute-done((bf16[8,32,768]{2,1,0:T(8,128)(2,1)}, bf16[8,32,768]{2,1,0:T(8,128)(2,1)S(1)}, u32[]{:S(2)}, u32[]{:S(2)}) %collective-permute-start.2) | collective-permute-done | bytes 393248 | tf_op jit(solution)/shard_map/ppermute | solution.py:275
  22.2 1.3 row_project.5
  23.6 11.7 %collective-permute-done.1.x_ref = bf16[8,32,768]{2,1,0:T(8,128)(2,1)S(1)} collective-permute-done((bf16[8,32,768]{2,1,0:T(8,128)(2,1)}, bf16[8,32,768]{2,1,0:T(8,128)(2,1)S(1)}, u32[]{:S(2)}, u32[]{:S(2)}) %collective-permute-start.1) | collective-permute-done | bytes 393248 | tf_op jit(solution)/shard_map/ppermute | solution.py:275
  36.6 1.3 row_project.7
  37.9 1.3 row_scores.3
  39.3 1.3 row_scores.2
  41.1 24.1 %all_to_all.15.parts_ref = f32[16,24,256]{2,1,0:T(8,128)S(1)} all-to-all(f32[16,24,256]{2,1,0:T(8,128)S(1)} %bitcast.12), channel_id=1, replica_groups=mesh['pair'=4,'core'=2,'res'=4] {'pair','res'}, dimensions={0} | all-to-all | bytes 786432 | tf_op jit(solution)/shard_map/all_to_all | solution.py:342
  65.4 11.9 %all_to_all.16 = bf16[16,24,256]{2,1,0:T(8,128)(2,1)S(1)} all-to-all(bf16[16,24,256]{2,1,0:T(8,128)(2,1)S(1)} %row_softmax.1), channel_id=1, replica_groups=mesh['pair'=4,'core'=2,'res'=4] {'pair','res'}, dimensions={0} | all-to-all | bytes 393216 | tf_op jit(solution)/shard_map/all_to_all | solution.py:349
  77.3 1.4 collective-permute-done.4.other_ref
  78.8 3.0 %row_update.1 = bf16[32,4,8,768]{3,2,1,0:T(8,128)(2,1)S(1)} custom-call(s32[1]{0:T(128)} %bitcast.2.core_ref, bf16[3,128,256]{2,1,0:T(8,128)(2,1)S(1)} %bitcast.11, bf16[3,128,256]{2,1,0:T(8,128)(2,1)S(1)} %collective-permute-done.4.other_ref, bf16[8,128,768]{2,1,0:T(8,128)(2,1)S(1)} %get-tuple-element.67.v_ref, ...), custom_call_target="tpu_custom_call" | custom-call | flops 1811939328 | bytes 8000000 | tf_op jit(solution)/shard_map/row_update/pallas_call | solution.py:353
  81.8 38.7 %all_to_all.17.mid_ref = bf16[32,4,8,768]{3,2,1,0:T(8,128)(2,1)S(1)} all-to-all(bf16[32,4,8,768]{3,2,1,0:T(8,128)(2,1)S(1)} %row_update.1), channel_id=1, replica_groups=mesh['pair'=4,'core'=2,'res'=4] {'pair','core','res'}, dimensions={0} | all-to-all | bytes 3145728 | tf_op jit(solution)/shard_map/all_to_all | solution.py:365
  120.5 4.8 %column_update.3 = (bf16[2,2,32,768]{3,2,1,0:T(8,128)(2,1)S(1)}, bf16[2,2,32,768]{3,2,1,0:T(8,128)(2,1)S(1)}, bf16[2,2,32,768]{3,2,1,0:T(8,128)(2,1)S(1)}, bf16[2,2,32,768]{3,2,1,0:T(8,128)(2,1)S(1)}) custom-call(s32[1]{0:T(128)} %bitcast.3.seq_ref, bf16[32,4,8,768]{3,2,1,0:T(8,128)(2,1)S(1)} %all_to_all.17.mid_ref, bf16[768,768]{1,0:T(8,128)(2,1)S(1)} %copy-done.7, ...), custom_call_target="tpu_custom_call" | custom-call | flops 3019898880 | bytes 8000000 | tf_op jit(solution)/shard_map/column_update/pallas_call | solution.py:371
  125.4 1.5 %collective-permute-start.9 = (bf16[2,2,32,768]{3,2,1,0:T(8,128)(2,1)S(1)}, bf16[2,2,32,768]{3,2,1,0:T(8,128)(2,1)S(1)}, u32[]{:S(2)}, u32[]{:S(2)}) collective-permute-start(bf16[2,2,32,768]{3,2,1,0:T(8,128)(2,1)S(1)} %get-tuple-element.74), channel_id=1, source_target_pairs={{0,8},{8,0},{16,24},{24,16},{1,9},{9,1},{17,25},{25,17},{2,10},{10... | collective-permute-start | bytes 589832 | tf_op jit(solution)/shard_map/ppermute | solution.py:278
  128.9 4.8 %column_update.2 = (bf16[2,2,32,768]{3,2,1,0:T(8,128)(2,1)S(1)}, bf16[2,2,32,768]{3,2,1,0:T(8,128)(2,1)S(1)}, bf16[2,2,32,768]{3,2,1,0:T(8,128)(2,1)S(1)}, bf16[2,2,32,768]{3,2,1,0:T(8,128)(2,1)S(1)}) custom-call(s32[1]{0:T(128)} %bitcast.3.seq_ref, bf16[32,4,8,768]{3,2,1,0:T(8,128)(2,1)S(1)} %all_to_all.17.mid_ref, bf16[768,768]{1,0:T(8,128)(2,1)S(1)} %copy-done.7, ...), custom_call_target="tpu_custom_call" | custom-call | flops 3019898880 | bytes 8000000 | tf_op jit(solution)/shard_map/column_update/pallas_call | solution.py:371
  133.8 1.5 %collective-permute-start.5 = (bf16[2,2,32,768]{3,2,1,0:T(8,128)(2,1)S(1)}, bf16[2,2,32,768]{3,2,1,0:T(8,128)(2,1)S(1)}, u32[]{:S(2)}, u32[]{:S(2)}) collective-permute-start(bf16[2,2,32,768]{3,2,1,0:T(8,128)(2,1)S(1)} %get-tuple-element.70), channel_id=1, source_target_pairs={{0,8},{8,0},{16,24},{24,16},{1,9},{9,1},{17,25},{25,17},{2,10},{10... | collective-permute-start | bytes 589832 | tf_op jit(solution)/shard_map/ppermute | solution.py:278
  137.4 1.5 %collective-permute-done.10.refs_2_ = bf16[2,2,32,768]{3,2,1,0:T(8,128)(2,1)S(1)} collective-permute-done((bf16[2,2,32,768]{3,2,1,0:T(8,128)(2,1)S(1)}, bf16[2,2,32,768]{3,2,1,0:T(8,128)(2,1)S(1)}, u32[]{:S(2)}, u32[]{:S(2)}) %collective-permute-start.10) | collective-permute-done | bytes 196640 | tf_op jit(solution)/shard_map/ppermute | solution.py:278
  139.1 2.6 %collective-permute-done.5.refs_1_ = bf16[2,2,32,768]{3,2,1,0:T(8,128)(2,1)S(1)} collective-permute-done((bf16[2,2,32,768]{3,2,1,0:T(8,128)(2,1)S(1)}, bf16[2,2,32,768]{3,2,1,0:T(8,128)(2,1)S(1)}, u32[]{:S(2)}, u32[]{:S(2)}) %collective-permute-start.5) | collective-permute-done | bytes 196640 | tf_op jit(solution)/shard_map/ppermute | solution.py:278
  141.7 5.6 %collective-permute-done.6.refs_2_ = bf16[2,2,32,768]{3,2,1,0:T(8,128)(2,1)S(1)} collective-permute-done((bf16[2,2,32,768]{3,2,1,0:T(8,128)(2,1)S(1)}, bf16[2,2,32,768]{3,2,1,0:T(8,128)(2,1)S(1)}, u32[]{:S(2)}, u32[]{:S(2)}) %collective-permute-start.6) | collective-permute-done | bytes 196640 | tf_op jit(solution)/shard_map/ppermute | solution.py:278
  147.5 1.4 assemble.2.refs_5_
  149.2 1.4 assemble.3
  (51 shorter events, 10.6 us)
Async XLA Ops:
  0.0 7.9 %copy-start = (bf16[768,768]{1,0:T(8,128)(2,1)S(1)}, bf16[768,768]{1,0:T(8,128)(2,1)}, u32[]{:S(2)}) copy-start(bf16[768,768]{1,0:T(8,128)(2,1)} %wq_ref.9) | copy-start | bytes 3538948
  2.2 20.1 %collective-permute-start.2 = (bf16[8,32,768]{2,1,0:T(8,128)(2,1)}, bf16[8,32,768]{2,1,0:T(8,128)(2,1)S(1)}, u32[]{:S(2)}, u32[]{:S(2)}) collective-permute-start(bf16[8,32,768]{2,1,0:T(8,128)(2,1)} %get-tuple-element.49), channel_id=1, source_target_pairs={{0,1},{1,0},{2,3},{3,2},{4,5},{5,4},{6,7},{7,6},{8,9},{9,8},{10,11... | collective-permute-start | bytes 1179656 | tf_op jit(solution)/shard_map/ppermute | solution.py:275
  5.3 30.0 %collective-permute-start.1 = (bf16[8,32,768]{2,1,0:T(8,128)(2,1)}, bf16[8,32,768]{2,1,0:T(8,128)(2,1)S(1)}, u32[]{:S(2)}, u32[]{:S(2)}) collective-permute-start(bf16[8,32,768]{2,1,0:T(8,128)(2,1)} %get-tuple-element.47), channel_id=1, source_target_pairs={{0,2},{1,3},{2,0},{3,1},{4,6},{5,7},{6,4},{7,5},{8,10},{9,11},{10,... | collective-permute-start | bytes 1179656 | tf_op jit(solution)/shard_map/ppermute | solution.py:275
  7.8 28.7 %collective-permute-start = (bf16[8,32,768]{2,1,0:T(8,128)(2,1)}, bf16[8,32,768]{2,1,0:T(8,128)(2,1)S(1)}, u32[]{:S(2)}, u32[]{:S(2)}) collective-permute-start(bf16[8,32,768]{2,1,0:T(8,128)(2,1)} %get-tuple-element.45), channel_id=1, source_target_pairs={{0,3},{1,2},{2,1},{3,0},{4,7},{5,6},{6,5},{7,4},{8,11},{9,10},{10,... | collective-permute-start | bytes 1179656 | tf_op jit(solution)/shard_map/ppermute | solution.py:275
  7.9 1.3 copy-start.1
  9.1 1.3 copy-start.3
  10.4 1.4 copy-start.5
  11.8 10.4 %copy-start.2 = (bf16[768,768]{1,0:T(8,128)(2,1)S(1)}, bf16[768,768]{1,0:T(8,128)(2,1)}, u32[]{:S(2)}) copy-start(bf16[768,768]{1,0:T(8,128)(2,1)} %wk_ref.9) | copy-start | bytes 3538948
  11.8 10.4 %copy-start.4 = (bf16[768,768]{1,0:T(8,128)(2,1)S(1)}, bf16[768,768]{1,0:T(8,128)(2,1)}, u32[]{:S(2)}) copy-start(bf16[768,768]{1,0:T(8,128)(2,1)} %wv_ref.9) | copy-start | bytes 3538948
  39.2 1.8 %collective-permute-start.3 = (f32[3,128,256]{2,1,0:T(8,128)S(1)}, f32[3,128,256]{2,1,0:T(8,128)S(1)}, u32[]{:S(2)}, u32[]{:S(2)}) collective-permute-start(f32[3,128,256]{2,1,0:T(8,128)S(1)} %row_scores.3), channel_id=1, source_target_pairs={{0,4},{4,0},{1,5},{5,1},{2,6},{6,2},{3,7},{7,3},{8,12},{12,8},{9,1... | collective-permute-start | bytes 1179656 | tf_op jit(solution)/shard_map/ppermute | solution.py:338
  40.6 38.1 %copy-start.6 = (bf16[768,768]{1,0:T(8,128)(2,1)S(1)}, bf16[768,768]{1,0:T(8,128)(2,1)}, u32[]{:S(2)}) copy-start(bf16[768,768]{1,0:T(8,128)(2,1)} %wo_ref.3) | copy-start | bytes 3538948
  77.3 1.4 collective-permute-start.4
  78.8 41.8 %copy-start.9 = (bf16[768,768]{1,0:T(8,128)(2,1)S(1)}, bf16[768,768]{1,0:T(8,128)(2,1)}, u32[]{:S(2)}) copy-start(bf16[768,768]{1,0:T(8,128)(2,1)} %wv_ref.11) | copy-start | bytes 3538948
  78.8 41.8 %copy-start.10 = (bf16[768,768]{1,0:T(8,128)(2,1)S(1)}, bf16[768,768]{1,0:T(8,128)(2,1)}, u32[]{:S(2)}) copy-start(bf16[768,768]{1,0:T(8,128)(2,1)} %wo_ref.5) | copy-start | bytes 3538948
  81.8 38.7 %copy-start.7 = (bf16[768,768]{1,0:T(8,128)(2,1)S(1)}, bf16[768,768]{1,0:T(8,128)(2,1)}, u32[]{:S(2)}) copy-start(bf16[768,768]{1,0:T(8,128)(2,1)} %wq_ref.11) | copy-start | bytes 3538948
  81.8 38.7 %copy-start.8 = (bf16[768,768]{1,0:T(8,128)(2,1)S(1)}, bf16[768,768]{1,0:T(8,128)(2,1)}, u32[]{:S(2)}) copy-start(bf16[768,768]{1,0:T(8,128)(2,1)} %wk_ref.11) | copy-start | bytes 3538948
  125.4 11.2 %collective-permute-start.9 = (bf16[2,2,32,768]{3,2,1,0:T(8,128)(2,1)S(1)}, bf16[2,2,32,768]{3,2,1,0:T(8,128)(2,1)S(1)}, u32[]{:S(2)}, u32[]{:S(2)}) collective-permute-start(bf16[2,2,32,768]{3,2,1,0:T(8,128)(2,1)S(1)} %get-tuple-element.74), channel_id=1, source_target_pairs={{0,8},{8,0},{16,24},{24,16},{1,9},{9,1},{17,25},{25,17},{2,10},{10... | collective-permute-start | bytes 589832 | tf_op jit(solution)/shard_map/ppermute | solution.py:278
  126.9 12.0 %collective-permute-start.10 = (bf16[2,2,32,768]{3,2,1,0:T(8,128)(2,1)S(1)}, bf16[2,2,32,768]{3,2,1,0:T(8,128)(2,1)S(1)}, u32[]{:S(2)}, u32[]{:S(2)}) collective-permute-start(bf16[2,2,32,768]{3,2,1,0:T(8,128)(2,1)S(1)} %get-tuple-element.75), channel_id=1, source_target_pairs={{0,16},{8,24},{16,0},{24,8},{1,17},{9,25},{17,1},{25,9},{2,18},{10... | collective-permute-start | bytes 589832 | tf_op jit(solution)/shard_map/ppermute | solution.py:278
  128.2 10.7 %collective-permute-start.11 = (bf16[2,2,32,768]{3,2,1,0:T(8,128)(2,1)S(1)}, bf16[2,2,32,768]{3,2,1,0:T(8,128)(2,1)S(1)}, u32[]{:S(2)}, u32[]{:S(2)}) collective-permute-start(bf16[2,2,32,768]{3,2,1,0:T(8,128)(2,1)S(1)} %get-tuple-element.76), channel_id=1, source_target_pairs={{0,24},{8,16},{16,8},{24,0},{1,25},{9,17},{17,9},{25,1},{2,26},{10... | collective-permute-start | bytes 589832 | tf_op jit(solution)/shard_map/ppermute | solution.py:278
  133.8 7.9 %collective-permute-start.5 = (bf16[2,2,32,768]{3,2,1,0:T(8,128)(2,1)S(1)}, bf16[2,2,32,768]{3,2,1,0:T(8,128)(2,1)S(1)}, u32[]{:S(2)}, u32[]{:S(2)}) collective-permute-start(bf16[2,2,32,768]{3,2,1,0:T(8,128)(2,1)S(1)} %get-tuple-element.70), channel_id=1, source_target_pairs={{0,8},{8,0},{16,24},{24,16},{1,9},{9,1},{17,25},{25,17},{2,10},{10... | collective-permute-start | bytes 589832 | tf_op jit(solution)/shard_map/ppermute | solution.py:278
  135.3 12.0 %collective-permute-start.6 = (bf16[2,2,32,768]{3,2,1,0:T(8,128)(2,1)S(1)}, bf16[2,2,32,768]{3,2,1,0:T(8,128)(2,1)S(1)}, u32[]{:S(2)}, u32[]{:S(2)}) collective-permute-start(bf16[2,2,32,768]{3,2,1,0:T(8,128)(2,1)S(1)} %get-tuple-element.71), channel_id=1, source_target_pairs={{0,16},{8,24},{16,0},{24,8},{1,17},{9,25},{17,1},{25,9},{2,18},{10... | collective-permute-start | bytes 589832 | tf_op jit(solution)/shard_map/ppermute | solution.py:278
  136.6 10.7 %collective-permute-start.7 = (bf16[2,2,32,768]{3,2,1,0:T(8,128)(2,1)S(1)}, bf16[2,2,32,768]{3,2,1,0:T(8,128)(2,1)S(1)}, u32[]{:S(2)}, u32[]{:S(2)}) collective-permute-start(bf16[2,2,32,768]{3,2,1,0:T(8,128)(2,1)S(1)} %get-tuple-element.72), channel_id=1, source_target_pairs={{0,24},{8,16},{16,8},{24,0},{1,25},{9,17},{17,9},{25,1},{2,26},{10... | collective-permute-start | bytes 589832 | tf_op jit(solution)/shard_map/ppermute | solution.py:278
  139.0 8.5 %collective-permute-start.12 = (bf16[4,2,32,768]{3,2,1,0:T(8,128)(2,1)S(1)}, bf16[4,2,32,768]{3,2,1,0:T(8,128)(2,1)S(1)}, u32[]{:S(2)}, u32[]{:S(2)}) collective-permute-start(bf16[4,2,32,768]{3,2,1,0:T(8,128)(2,1)S(1)} %pad_maximum_fusion.1), channel_id=1, source_target_pairs={{0,4},{4,0},{1,5},{5,1},{2,6},{6,2},{3,7},{7,3},{8,12},{12,8},{9,1... | collective-permute-start | bytes 1179656 | tf_op jit(solution)/shard_map/ppermute | solution.py:385
  147.4 1.8 %collective-permute-start.8 = (bf16[4,2,32,768]{3,2,1,0:T(8,128)(2,1)S(1)}, bf16[4,2,32,768]{3,2,1,0:T(8,128)(2,1)S(1)}, u32[]{:S(2)}, u32[]{:S(2)}) collective-permute-start(bf16[4,2,32,768]{3,2,1,0:T(8,128)(2,1)S(1)} %pad_maximum_fusion), channel_id=1, source_target_pairs={{0,4},{4,0},{1,5},{5,1},{2,6},{6,2},{3,7},{7,3},{8,12},{12,8},{9,1... | collective-permute-start | bytes 1179656 | tf_op jit(solution)/shard_map/ppermute | solution.py:385

commit v4 on v3

--- a/solution.py
+++ b/solution.py
@@ -11,6 +11,7 @@
 
 HEADS = 12
 CORES = 2
+HALVES = 2
 SLOT = 16
 VMEM_BYTES = 24 * 1024 * 1024
 FULL_VMEM_BYTES = 64_000_000
@@ -67,39 +68,48 @@
 
 def row_project(at_ref, x_ref, wq_ref, wk_ref, wv_ref, *refs):
     q_ref, k_ref, v_ref, kept_ref = refs[-4:]
-    rows, block, width = x_ref.shape
-    x = x_ref[...]
-    kept_ref[...] = x
+    rows, cols, width = q_ref.shape
+    block = x_ref.shape[1]
+    x = x_ref[...] if x_ref.shape[0] == rows else x_ref[pl.ds(at_ref[0] * rows, rows)]
+    place = pl.ds(pl.multiple_of(at_ref[0] * block, block), block)
+    kept_ref[:, place, :] = x
     normed = normalize(x.astype(F32).reshape(rows * block, width))
     for weight_ref, ref in ((wq_ref, q_ref), (wk_ref, k_ref), (wv_ref, v_ref)):
-        ref[...] = dot(normed, weight_ref[...]).astype(BF16).reshape(rows, block, width)
+        ref[:, place, :] = dot(normed, weight_ref[...]).astype(BF16).reshape(rows, block, width)
 
 
 def row_scores(block, chunks, base_ref, q_ref, k_ref, tied_ref):
-    rows, cols, pair = q_ref.shape
-    first, second = head_masks(pair, pair // 2)
-    q = jnp.concatenate([q_ref[row] for row in range(rows)], axis=1)
-    keys = jnp.concatenate(
-        [
-            jnp.concatenate([k_ref[row] * mask for row in range(rows)], axis=1)
-            for mask in (first, second)
-        ],
-        axis=0,
-    )
-    score = dot_nt(q, keys).reshape(cols // block, block, 2 * cols)
-    at = 0
-    pieces = []
-    for piece in chunks:
-        pieces.append(score[:, at : at + piece].reshape(-1, 2 * cols))
-        at += piece
-    tied_ref[0] = jnp.concatenate(pieces, axis=0)
-
-
-def row_softmax(scale, parts_ref, prob_ref):
+    rows, cols, width = q_ref.shape
+    pair = 2 * (width // HEADS)
+    masks = head_masks(pair, pair // 2)
+    for step in range(tied_ref.shape[0]):
+        lanes = pl.ds(pl.multiple_of((base_ref[0] + step) * pair, pair), pair)
+        q = jnp.concatenate([q_ref[row, :, lanes] for row in range(rows)], axis=1)
+        keys = jnp.concatenate(
+            [
+                jnp.concatenate([k_ref[row, :, lanes] * mask for row in range(rows)], axis=1)
+                for mask in masks
+            ],
+            axis=0,
+        )
+        score = dot_nt(q, keys).reshape(cols // block, block, 2 * cols)
+        at = 0
+        pieces = []
+        for piece in chunks:
+            pieces.append(score[:, at : at + piece].reshape(-1, 2 * cols))
+            at += piece
+        tied_ref[step] = jnp.concatenate(pieces, axis=0)
+
+
+def row_sum(parts_ref, tied_ref):
     tied = parts_ref[0]
     for at in range(1, parts_ref.shape[0]):
         tied = tied + parts_ref[at]
-    tied = tied * scale
+    tied_ref[...] = tied
+
+
+def row_softmax(scale, mine_ref, other_ref, prob_ref):
+    tied = (mine_ref[...] + other_ref[...]) * scale
     cols = tied.shape[1] // 2
     halves = []
     for half in (tied[:, :cols], tied[:, cols:]):
@@ -255,7 +265,7 @@
     states, row_query, row_key, row_value, row_out, col_query, col_key, col_value, col_out
 ):
     rows, block, width = states.shape
-    pairs_size, res_size = lax.axis_size("pair"), lax.axis_size("res")
+    pairs_size, res_size = lax.axis_size("pair"), HALVES * lax.axis_size("inner")
     seq_size = pairs_size * CORES
     all_rows, cols = rows * seq_size, block * res_size
     head_dim = width // HEADS
@@ -264,7 +274,7 @@
     half_pairs = HEADS // 2 // CORES
     core = lax.axis_index("core").astype(jnp.int32)
     seq = lax.axis_index("pair").astype(jnp.int32) * CORES + core
-    part = lax.axis_index("res").astype(jnp.int32)
+    part = lax.axis_index(("half", "inner")).astype(jnp.int32)
     swap = [(0, 1), (1, 0)]
     smem = pl.BlockSpec(memory_space=pltpu.SMEM)
     vmem = pl.BlockSpec(memory_space=pltpu.VMEM)
@@ -272,7 +282,7 @@
     chunks = [SLOT] * (block // SLOT)
 
     def across(field, step):
-        return lax.ppermute(field, "res", [(at, at ^ step) for at in range(res_size)])
+        return lax.ppermute(field, ("half", "inner"), [(at, at ^ step) for at in range(res_size)])
 
     def around(field, step):
         return lax.ppermute(field, "pair", [(at, at ^ step) for at in range(pairs_size)])
@@ -297,20 +307,12 @@
         (blocks[0], halves, core.reshape(1), seq.reshape(1), places)
     )
     blocks[0] = own
-    share_spec = pl.BlockSpec((own_rows, block, width), lambda g, at: (0, at[0], 0))
     fields = []
     for step, field in enumerate(blocks):
-        source = (lambda g, at: (at[0], 0, 0)) if step == 0 else (lambda g, at: (0, 0, 0))
         fields = pl.pallas_call(
             row_project,
-            grid_spec=pltpu.PrefetchScalarGridSpec(
-                num_scalar_prefetch=1,
-                grid=(1,),
-                in_specs=[pl.BlockSpec((own_rows, block, width), source)]
-                + [whole((width, width))] * 3
-                + [anywhere] * len(fields),
-                out_specs=[share_spec] * 4,
-            ),
+            in_specs=[smem] + [vmem] * (4 + len(fields)),
+            out_specs=[vmem] * 4,
             out_shape=[jax.ShapeDtypeStruct((own_rows, cols, width), BF16)] * 4,
             input_output_aliases={5 + at: at for at in range(len(fields))},
             compiler_params=params(),
@@ -320,15 +322,10 @@
     q, k, v, x = fields
 
     def scores(base):
-        spec = pl.BlockSpec((own_rows, cols, pair), lambda g, at: (0, 0, at[0] + g))
         return pl.pallas_call(
             functools.partial(row_scores, block, chunks),
-            grid_spec=pltpu.PrefetchScalarGridSpec(
-                num_scalar_prefetch=1,
-                grid=(half_pairs,),
-                in_specs=[spec, spec],
-                out_specs=pl.BlockSpec((1, cols, 2 * cols), lambda g, at: (g, 0, 0)),
-            ),
+            in_specs=[smem, vmem, vmem],
+            out_specs=vmem,
             out_shape=jax.ShapeDtypeStruct((half_pairs, cols, 2 * cols), F32),
             compiler_params=params(),
             cost_estimate=cost(4 * own_rows * cols * cols * pair * half_pairs, 2e6),
@@ -337,16 +334,28 @@
 
     other = lax.ppermute(scores(halves[0]), "core", swap)
     mine = scores(halves[1])
-    owners = pairs_size * res_size
-    partial = (mine + other).reshape(owners, half_pairs * cols // owners, 2 * cols)
-    partial = lax.all_to_all(partial, ("pair", "res"), split_axis=0, concat_axis=0, tiled=True)
+    owners = pairs_size * (res_size // HALVES)
+    share = (owners, half_pairs * cols // owners, 2 * cols)
+    partial = lax.all_to_all(
+        (mine + other).reshape(share), ("pair", "inner"), split_axis=0, concat_axis=0, tiled=True
+    )
+    partial = pl.pallas_call(
+        row_sum,
+        in_specs=[vmem],
+        out_specs=vmem,
+        out_shape=jax.ShapeDtypeStruct(share[1:], F32),
+        compiler_params=params(),
+        name="row_sum",
+    )(partial)
     prob = pl.pallas_call(
         functools.partial(row_softmax, head_dim ** (-0.5) / math.sqrt(all_rows)),
-        out_shape=jax.ShapeDtypeStruct(partial.shape, BF16),
+        in_specs=[vmem, vmem],
+        out_specs=vmem,
+        out_shape=jax.ShapeDtypeStruct(share, BF16),
         compiler_params=params(),
         name="row_softmax",
-    )(partial)
-    prob = lax.all_to_all(prob, ("pair", "res"), split_axis=0, concat_axis=0, tiled=True)
+    )(partial, lax.ppermute(partial, "half", swap))
+    prob = lax.all_to_all(prob, ("pair", "inner"), split_axis=0, concat_axis=0, tiled=True)
     prob = prob.reshape(half_pairs, cols, 2 * cols)
     prob_other = lax.ppermute(prob, "core", swap)
 
@@ -362,7 +371,9 @@
         name="row_update",
     )(core_place, prob, prob_other, v, x, row_out)
 
-    moved = lax.all_to_all(mid, ("pair", "core", "res"), split_axis=0, concat_axis=0, tiled=True)
+    moved = lax.all_to_all(
+        mid, ("pair", "core", "half", "inner"), split_axis=0, concat_axis=0, tiled=True
+    )
     home = []
     first_at = 0
     for piece in chunks:
@@ -418,9 +429,10 @@
 def solution(mesh):
     seq_size, res_size = mesh.devices.shape
     split = Mesh(
-        mesh.devices.reshape(seq_size // CORES, CORES, res_size), ("pair", "core", "res")
-    )
-    placed = P(("pair", "core"), "res", None)
+        mesh.devices.reshape(seq_size // CORES, CORES, HALVES, res_size // HALVES),
+        ("pair", "core", "half", "inner"),
+    )
+    placed = P(("pair", "core"), ("half", "inner"), None)
     return jax.shard_map(
         on_device,
         mesh=split,

time: 151 us -> 147 us (0.974)
  blocking collectives: 74.7 us -> 65.6 us
  waiting for transfers between devices: 32.6 us -> 37.2 us
  starting transfers between devices: 13 us -> 14.7 us
    all_to_all x3, blocking collectives: 74.7 us -> 65.6 us  [the longest x1 38.7 us: on_device(): lax.all_to_all(mid, ('pair', 'core', 'half', 'inner'), split_axis=0, conc...]
    ppermute x3 -> x4, waiting for transfers between devices: 20.8 us -> 24.8 us  [the longest x3 20.8 us: across(): lax.ppermute(field, ('half', 'inner'), [(at, at ^ step) for at in range(r...]
    ppermute x3 -> x4, starting transfers between devices: 5.68 us -> 7.32 us  [the longest x3 5.68 us: across(): lax.ppermute(field, ('half', 'inner'), [(at, at ^ step) for at in range(r...]
    pallas_call x6 -> x7, Pallas kernels: 7.87 us -> 6.61 us  [the longest x4 5.22 us: on_device(): pl.pallas_call(row_project, in_specs=[smem] + [vmem] * (4 + len(fields)),...]
  transfers between devices with their start and end apart: 13 -> 14, of which waited for: 8 -> 9; matrix products, arithmetic and copies ran while one was open for 0% -> 0% of each run, Pallas kernels for 8% -> 7%
where the time goes in v4:
time: 147 us; the launch traced here: 146 us
  blocking collectives  65.6 us (45%)
  waiting for transfers between devices  37.2 us (25%)
  Pallas kernels  24.4 us (17%)
  starting transfers between devices  14.7 us (10%)
  local copies, waits for them, and re-layouts  4.05 us (3%)
    all_to_all x1, blocking collectives, on_device(): lax.all_to_all(mid, ('pair', 'core', 'half', 'inner'), split_axis=0, conc...  38.7 us
    ppermute x3, waiting for transfers between devices, across(): lax.ppermute(field, ('half', 'inner'), [(at, at ^ step) for at in range(r...  20.8 us
    all_to_all x1, blocking collectives, on_device(): lax.all_to_all((mine + other).reshape(share), ('pair', 'inner'), split_ax...  17.9 us
    ppermute x6, waiting for transfers between devices, around(): lax.ppermute(field, 'pair', [(at, at ^ step) for at in range(pairs_size)])  9.73 us
    pallas_call x2, Pallas kernels, on_device(): pl.pallas_call(functools.partial(column_update, first_at), in_specs=[smem...  9.65 us
    all_to_all x1, blocking collectives, on_device(): lax.all_to_all(prob, ('pair', 'inner'), split_axis=0, concat_axis=0, tile...  9.02 us
    ppermute x6, starting transfers between devices, around(): lax.ppermute(field, 'pair', [(at, at ^ step) for at in range(pairs_size)])  7.11 us
    ppermute x3, starting transfers between devices, across(): lax.ppermute(field, ('half', 'inner'), [(at, at ^ step) for at in range(r...  5.68 us
  transfers between devices with their start and end apart: 14, of which 9 were waited for; matrix products, arithmetic and copies ran while one was open for 0% of the time, Pallas kernels for 7%

profile of v4, /device:TPU:0, one launch (start us, length us, event | category | flops | bytes accessed | tf_op | source)
XLA Modules:
  0.0 146.4 jit_solution(1745036722027109687)
XLA Ops:
  0.0 2.2 %row_shares.1 = (bf16[8,32,768]{2,1,0:T(8,128)(2,1)}, bf16[8,32,768]{2,1,0:T(8,128)(2,1)}, bf16[8,32,768]{2,1,0:T(8,128)(2,1)}) custom-call(s32[1]{0:T(128)} %bitcast.4.part_ref.at_ref, bf16[32,32,768]{2,1,0:T(8,128)(2,1)} %x_ref), custom_call_target="tpu_custom_call" | custom-call | tf_op jit(solution)/shard_map/row_shares/pallas_call | solution.py:290
  2.2 3.1 %collective-permute-start.2 = (bf16[8,32,768]{2,1,0:T(8,128)(2,1)}, bf16[8,32,768]{2,1,0:T(8,128)(2,1)S(1)}, u32[]{:S(2)}, u32[]{:S(2)}) collective-permute-start(bf16[8,32,768]{2,1,0:T(8,128)(2,1)} %get-tuple-element.49), channel_id=1, source_target_pairs={{0,1},{1,0},{2,3},{3,2},{4,5},{5,4},{6,7},{7,6},{8,9},{9,8},{10,11... | collective-permute-start | bytes 1179656 | tf_op jit(solution)/shard_map/ppermute | solution.py:285
  5.3 2.6 %collective-permute-start.1 = (bf16[8,32,768]{2,1,0:T(8,128)(2,1)}, bf16[8,32,768]{2,1,0:T(8,128)(2,1)S(1)}, u32[]{:S(2)}, u32[]{:S(2)}) collective-permute-start(bf16[8,32,768]{2,1,0:T(8,128)(2,1)} %get-tuple-element.47), channel_id=1, source_target_pairs={{0,2},{1,3},{2,0},{3,1},{4,6},{5,7},{6,4},{7,5},{8,10},{9,11},{10,... | collective-permute-start | bytes 1179656 | tf_op jit(solution)/shard_map/ppermute | solution.py:285
  10.4 1.4 copy-done.5
  11.8 1.3 row_project.4
  13.1 9.1 %collective-permute-done.2.x_ref = bf16[8,32,768]{2,1,0:T(8,128)(2,1)S(1)} collective-permute-done((bf16[8,32,768]{2,1,0:T(8,128)(2,1)}, bf16[8,32,768]{2,1,0:T(8,128)(2,1)S(1)}, u32[]{:S(2)}, u32[]{:S(2)}) %collective-permute-start.2) | collective-permute-done | bytes 393248 | tf_op jit(solution)/shard_map/ppermute | solution.py:285
  23.6 11.7 %collective-permute-done.1.x_ref = bf16[8,32,768]{2,1,0:T(8,128)(2,1)S(1)} collective-permute-done((bf16[8,32,768]{2,1,0:T(8,128)(2,1)}, bf16[8,32,768]{2,1,0:T(8,128)(2,1)S(1)}, u32[]{:S(2)}, u32[]{:S(2)}) %collective-permute-start.1) | collective-permute-done | bytes 393248 | tf_op jit(solution)/shard_map/ppermute | solution.py:285
  36.6 1.3 row_project.7
  40.4 17.9 %all_to_all.15.parts_ref = f32[8,48,256]{2,1,0:T(8,128)S(1)} all-to-all(f32[8,48,256]{2,1,0:T(8,128)S(1)} %bitcast.12), channel_id=1, replica_groups=mesh['pair'=4,'core'=2,'half'=2,'inner'=2] {'pair','inner'}, dimensions={0} | all-to-all | bytes 786432 | tf_op jit(solution)/shard_map/all_to_all | solution.py:339
  58.3 1.6 %collective-permute-start.4 = (f32[48,256]{1,0:T(8,128)S(1)}, f32[48,256]{1,0:T(8,128)S(1)}, u32[]{:S(2)}, u32[]{:S(2)}) collective-permute-start(f32[48,256]{1,0:T(8,128)S(1)} %row_sum.1.mine_ref), channel_id=1, source_target_pairs={{0,2},{2,0},{1,3},{3,1},{4,6},{6,4},{5,7},{7,5},{8,10},{10,8},{9,1... | collective-permute-start | bytes 147464 | tf_op jit(solution)/shard_map/ppermute | solution.py:357
  60.0 3.9 %collective-permute-done.4.other_ref = f32[48,256]{1,0:T(8,128)S(1)} collective-permute-done((f32[48,256]{1,0:T(8,128)S(1)}, f32[48,256]{1,0:T(8,128)S(1)}, u32[]{:S(2)}, u32[]{:S(2)}) %collective-permute-start.4) | collective-permute-done | bytes 49184 | tf_op jit(solution)/shard_map/ppermute | solution.py:357
  64.1 9.0 %all_to_all.16 = bf16[8,48,256]{2,1,0:T(8,128)(2,1)S(1)} all-to-all(bf16[8,48,256]{2,1,0:T(8,128)(2,1)S(1)} %row_softmax.1), channel_id=1, replica_groups=mesh['pair'=4,'core'=2,'half'=2,'inner'=2] {'pair','inner'}, dimensions={0} | all-to-all | bytes 393216 | tf_op jit(solution)/shard_map/all_to_all | solution.py:358
  73.1 1.4 collective-permute-done.5.other_ref
  74.6 3.0 %row_update.1 = bf16[32,4,8,768]{3,2,1,0:T(8,128)(2,1)S(1)} custom-call(s32[1]{0:T(128)} %bitcast.2.core_ref, bf16[3,128,256]{2,1,0:T(8,128)(2,1)S(1)} %bitcast.11, bf16[3,128,256]{2,1,0:T(8,128)(2,1)S(1)} %collective-permute-done.5.other_ref, bf16[8,128,768]{2,1,0:T(8,128)(2,1)S(1)} %get-tuple-element.67.v_ref, ...), custom_call_target="tpu_custom_call" | custom-call | flops 1811939328 | bytes 8000000 | tf_op jit(solution)/shard_map/row_update/pallas_call | solution.py:362
  77.6 38.7 %all_to_all.17.mid_ref = bf16[32,4,8,768]{3,2,1,0:T(8,128)(2,1)S(1)} all-to-all(bf16[32,4,8,768]{3,2,1,0:T(8,128)(2,1)S(1)} %row_update.1), channel_id=1, replica_groups=mesh['pair'=4,'core'=2,'half'=2,'inner'=2] {'pair','core','half','inner'}, dimensions={0} | all-to-all | bytes 3145728 | tf_op jit(solution)/shard_map/all_to_all | solution.py:374
  116.3 4.8 %column_update.3 = (bf16[2,2,32,768]{3,2,1,0:T(8,128)(2,1)S(1)}, bf16[2,2,32,768]{3,2,1,0:T(8,128)(2,1)S(1)}, bf16[2,2,32,768]{3,2,1,0:T(8,128)(2,1)S(1)}, bf16[2,2,32,768]{3,2,1,0:T(8,128)(2,1)S(1)}) custom-call(s32[1]{0:T(128)} %bitcast.3.seq_ref, bf16[32,4,8,768]{3,2,1,0:T(8,128)(2,1)S(1)} %all_to_all.17.mid_ref, bf16[768,768]{1,0:T(8,128)(2,1)S(1)} %copy-done.7, ...), custom_call_target="tpu_custom_call" | custom-call | flops 3019898880 | bytes 8000000 | tf_op jit(solution)/shard_map/column_update/pallas_call | solution.py:382
  121.2 1.5 %collective-permute-start.10 = (bf16[2,2,32,768]{3,2,1,0:T(8,128)(2,1)S(1)}, bf16[2,2,32,768]{3,2,1,0:T(8,128)(2,1)S(1)}, u32[]{:S(2)}, u32[]{:S(2)}) collective-permute-start(bf16[2,2,32,768]{3,2,1,0:T(8,128)(2,1)S(1)} %get-tuple-element.74), channel_id=1, source_target_pairs={{0,8},{8,0},{16,24},{24,16},{1,9},{9,1},{17,25},{25,17},{2,10},{10... | collective-permute-start | bytes 589832 | tf_op jit(solution)/shard_map/ppermute | solution.py:288
  124.7 4.8 %column_update.2 = (bf16[2,2,32,768]{3,2,1,0:T(8,128)(2,1)S(1)}, bf16[2,2,32,768]{3,2,1,0:T(8,128)(2,1)S(1)}, bf16[2,2,32,768]{3,2,1,0:T(8,128)(2,1)S(1)}, bf16[2,2,32,768]{3,2,1,0:T(8,128)(2,1)S(1)}) custom-call(s32[1]{0:T(128)} %bitcast.3.seq_ref, bf16[32,4,8,768]{3,2,1,0:T(8,128)(2,1)S(1)} %all_to_all.17.mid_ref, bf16[768,768]{1,0:T(8,128)(2,1)S(1)} %copy-done.7, ...), custom_call_target="tpu_custom_call" | custom-call | flops 3019898880 | bytes 8000000 | tf_op jit(solution)/shard_map/column_update/pallas_call | solution.py:382
  129.6 1.6 %collective-permute-start.6 = (bf16[2,2,32,768]{3,2,1,0:T(8,128)(2,1)S(1)}, bf16[2,2,32,768]{3,2,1,0:T(8,128)(2,1)S(1)}, u32[]{:S(2)}, u32[]{:S(2)}) collective-permute-start(bf16[2,2,32,768]{3,2,1,0:T(8,128)(2,1)S(1)} %get-tuple-element.70), channel_id=1, source_target_pairs={{0,8},{8,0},{16,24},{24,16},{1,9},{9,1},{17,25},{25,17},{2,10},{10... | collective-permute-start | bytes 589832 | tf_op jit(solution)/shard_map/ppermute | solution.py:288
  133.2 1.6 %collective-permute-done.11.refs_2_ = bf16[2,2,32,768]{3,2,1,0:T(8,128)(2,1)S(1)} collective-permute-done((bf16[2,2,32,768]{3,2,1,0:T(8,128)(2,1)S(1)}, bf16[2,2,32,768]{3,2,1,0:T(8,128)(2,1)S(1)}, u32[]{:S(2)}, u32[]{:S(2)}) %collective-permute-start.11) | collective-permute-done | bytes 196640 | tf_op jit(solution)/shard_map/ppermute | solution.py:288
  134.9 2.6 %collective-permute-done.6.refs_1_ = bf16[2,2,32,768]{3,2,1,0:T(8,128)(2,1)S(1)} collective-permute-done((bf16[2,2,32,768]{3,2,1,0:T(8,128)(2,1)S(1)}, bf16[2,2,32,768]{3,2,1,0:T(8,128)(2,1)S(1)}, u32[]{:S(2)}, u32[]{:S(2)}) %collective-permute-start.6) | collective-permute-done | bytes 196640 | tf_op jit(solution)/shard_map/ppermute | solution.py:288
  137.5 5.6 %collective-permute-done.7.refs_2_ = bf16[2,2,32,768]{3,2,1,0:T(8,128)(2,1)S(1)} collective-permute-done((bf16[2,2,32,768]{3,2,1,0:T(8,128)(2,1)S(1)}, bf16[2,2,32,768]{3,2,1,0:T(8,128)(2,1)S(1)}, u32[]{:S(2)}, u32[]{:S(2)}) %collective-permute-start.7) | collective-permute-done | bytes 196640 | tf_op jit(solution)/shard_map/ppermute | solution.py:288
  143.3 1.4 assemble.2.refs_5_
  145.0 1.4 assemble.3
  (54 shorter events, 12.5 us)
Async XLA Ops:
  0.0 7.9 %copy-start = (bf16[768,768]{1,0:T(8,128)(2,1)S(1)}, bf16[768,768]{1,0:T(8,128)(2,1)}, u32[]{:S(2)}) copy-start(bf16[768,768]{1,0:T(8,128)(2,1)} %wq_ref.9) | copy-start | bytes 3538948
  2.2 20.1 %collective-permute-start.2 = (bf16[8,32,768]{2,1,0:T(8,128)(2,1)}, bf16[8,32,768]{2,1,0:T(8,128)(2,1)S(1)}, u32[]{:S(2)}, u32[]{:S(2)}) collective-permute-start(bf16[8,32,768]{2,1,0:T(8,128)(2,1)} %get-tuple-element.49), channel_id=1, source_target_pairs={{0,1},{1,0},{2,3},{3,2},{4,5},{5,4},{6,7},{7,6},{8,9},{9,8},{10,11... | collective-permute-start | bytes 1179656 | tf_op jit(solution)/shard_map/ppermute | solution.py:285
  5.3 30.0 %collective-permute-start.1 = (bf16[8,32,768]{2,1,0:T(8,128)(2,1)}, bf16[8,32,768]{2,1,0:T(8,128)(2,1)S(1)}, u32[]{:S(2)}, u32[]{:S(2)}) collective-permute-start(bf16[8,32,768]{2,1,0:T(8,128)(2,1)} %get-tuple-element.47), channel_id=1, source_target_pairs={{0,2},{1,3},{2,0},{3,1},{4,6},{5,7},{6,4},{7,5},{8,10},{9,11},{10,... | collective-permute-start | bytes 1179656 | tf_op jit(solution)/shard_map/ppermute | solution.py:285
  7.8 28.7 %collective-permute-start = (bf16[8,32,768]{2,1,0:T(8,128)(2,1)}, bf16[8,32,768]{2,1,0:T(8,128)(2,1)S(1)}, u32[]{:S(2)}, u32[]{:S(2)}) collective-permute-start(bf16[8,32,768]{2,1,0:T(8,128)(2,1)} %get-tuple-element.45), channel_id=1, source_target_pairs={{0,3},{1,2},{2,1},{3,0},{4,7},{5,6},{6,5},{7,4},{8,11},{9,10},{10,... | collective-permute-start | bytes 1179656 | tf_op jit(solution)/shard_map/ppermute | solution.py:285
  7.9 1.3 copy-start.1
  10.4 1.4 copy-start.5
  11.8 10.4 %copy-start.2 = (bf16[768,768]{1,0:T(8,128)(2,1)S(1)}, bf16[768,768]{1,0:T(8,128)(2,1)}, u32[]{:S(2)}) copy-start(bf16[768,768]{1,0:T(8,128)(2,1)} %wk_ref.9) | copy-start | bytes 3538948
  11.8 10.4 %copy-start.4 = (bf16[768,768]{1,0:T(8,128)(2,1)S(1)}, bf16[768,768]{1,0:T(8,128)(2,1)}, u32[]{:S(2)}) copy-start(bf16[768,768]{1,0:T(8,128)(2,1)} %wv_ref.9) | copy-start | bytes 3538948
  38.6 1.8 %collective-permute-start.3 = (f32[3,128,256]{2,1,0:T(8,128)S(1)}, f32[3,128,256]{2,1,0:T(8,128)S(1)}, u32[]{:S(2)}, u32[]{:S(2)}) collective-permute-start(f32[3,128,256]{2,1,0:T(8,128)S(1)} %row_scores.3), channel_id=1, source_target_pairs={{0,4},{4,0},{1,5},{5,1},{2,6},{6,2},{3,7},{7,3},{8,12},{12,8},{9,1... | collective-permute-start | bytes 1179656 | tf_op jit(solution)/shard_map/ppermute | solution.py:335
  39.4 35.2 %copy-start.6 = (bf16[768,768]{1,0:T(8,128)(2,1)S(1)}, bf16[768,768]{1,0:T(8,128)(2,1)}, u32[]{:S(2)}) copy-start(bf16[768,768]{1,0:T(8,128)(2,1)} %wo_ref.3) | copy-start | bytes 3538948
  58.3 5.6 %collective-permute-start.4 = (f32[48,256]{1,0:T(8,128)S(1)}, f32[48,256]{1,0:T(8,128)S(1)}, u32[]{:S(2)}, u32[]{:S(2)}) collective-permute-start(f32[48,256]{1,0:T(8,128)S(1)} %row_sum.1.mine_ref), channel_id=1, source_target_pairs={{0,2},{2,0},{1,3},{3,1},{4,6},{6,4},{5,7},{7,5},{8,10},{10,8},{9,1... | collective-permute-start | bytes 147464 | tf_op jit(solution)/shard_map/ppermute | solution.py:357
  73.1 1.4 collective-permute-start.5
  74.6 41.8 %copy-start.9 = (bf16[768,768]{1,0:T(8,128)(2,1)S(1)}, bf16[768,768]{1,0:T(8,128)(2,1)}, u32[]{:S(2)}) copy-start(bf16[768,768]{1,0:T(8,128)(2,1)} %wv_ref.11) | copy-start | bytes 3538948
  74.6 41.8 %copy-start.10 = (bf16[768,768]{1,0:T(8,128)(2,1)S(1)}, bf16[768,768]{1,0:T(8,128)(2,1)}, u32[]{:S(2)}) copy-start(bf16[768,768]{1,0:T(8,128)(2,1)} %wo_ref.5) | copy-start | bytes 3538948
  77.6 38.7 %copy-start.7 = (bf16[768,768]{1,0:T(8,128)(2,1)S(1)}, bf16[768,768]{1,0:T(8,128)(2,1)}, u32[]{:S(2)}) copy-start(bf16[768,768]{1,0:T(8,128)(2,1)} %wq_ref.11) | copy-start | bytes 3538948
  77.6 38.7 %copy-start.8 = (bf16[768,768]{1,0:T(8,128)(2,1)S(1)}, bf16[768,768]{1,0:T(8,128)(2,1)}, u32[]{:S(2)}) copy-start(bf16[768,768]{1,0:T(8,128)(2,1)} %wk_ref.11) | copy-start | bytes 3538948
  121.2 11.2 %collective-permute-start.10 = (bf16[2,2,32,768]{3,2,1,0:T(8,128)(2,1)S(1)}, bf16[2,2,32,768]{3,2,1,0:T(8,128)(2,1)S(1)}, u32[]{:S(2)}, u32[]{:S(2)}) collective-permute-start(bf16[2,2,32,768]{3,2,1,0:T(8,128)(2,1)S(1)} %get-tuple-element.74), channel_id=1, source_target_pairs={{0,8},{8,0},{16,24},{24,16},{1,9},{9,1},{17,25},{25,17},{2,10},{10... | collective-permute-start | bytes 589832 | tf_op jit(solution)/shard_map/ppermute | solution.py:288
  122.7 12.0 %collective-permute-start.11 = (bf16[2,2,32,768]{3,2,1,0:T(8,128)(2,1)S(1)}, bf16[2,2,32,768]{3,2,1,0:T(8,128)(2,1)S(1)}, u32[]{:S(2)}, u32[]{:S(2)}) collective-permute-start(bf16[2,2,32,768]{3,2,1,0:T(8,128)(2,1)S(1)} %get-tuple-element.75), channel_id=1, source_target_pairs={{0,16},{8,24},{16,0},{24,8},{1,17},{9,25},{17,1},{25,9},{2,18},{10... | collective-permute-start | bytes 589832 | tf_op jit(solution)/shard_map/ppermute | solution.py:288
  124.0 10.7 %collective-permute-start.12 = (bf16[2,2,32,768]{3,2,1,0:T(8,128)(2,1)S(1)}, bf16[2,2,32,768]{3,2,1,0:T(8,128)(2,1)S(1)}, u32[]{:S(2)}, u32[]{:S(2)}) collective-permute-start(bf16[2,2,32,768]{3,2,1,0:T(8,128)(2,1)S(1)} %get-tuple-element.76), channel_id=1, source_target_pairs={{0,24},{8,16},{16,8},{24,0},{1,25},{9,17},{17,9},{25,1},{2,26},{10... | collective-permute-start | bytes 589832 | tf_op jit(solution)/shard_map/ppermute | solution.py:288
  129.6 7.9 %collective-permute-start.6 = (bf16[2,2,32,768]{3,2,1,0:T(8,128)(2,1)S(1)}, bf16[2,2,32,768]{3,2,1,0:T(8,128)(2,1)S(1)}, u32[]{:S(2)}, u32[]{:S(2)}) collective-permute-start(bf16[2,2,32,768]{3,2,1,0:T(8,128)(2,1)S(1)} %get-tuple-element.70), channel_id=1, source_target_pairs={{0,8},{8,0},{16,24},{24,16},{1,9},{9,1},{17,25},{25,17},{2,10},{10... | collective-permute-start | bytes 589832 | tf_op jit(solution)/shard_map/ppermute | solution.py:288
  131.1 12.0 %collective-permute-start.7 = (bf16[2,2,32,768]{3,2,1,0:T(8,128)(2,1)S(1)}, bf16[2,2,32,768]{3,2,1,0:T(8,128)(2,1)S(1)}, u32[]{:S(2)}, u32[]{:S(2)}) collective-permute-start(bf16[2,2,32,768]{3,2,1,0:T(8,128)(2,1)S(1)} %get-tuple-element.71), channel_id=1, source_target_pairs={{0,16},{8,24},{16,0},{24,8},{1,17},{9,25},{17,1},{25,9},{2,18},{10... | collective-permute-start | bytes 589832 | tf_op jit(solution)/shard_map/ppermute | solution.py:288
  132.4 10.7 %collective-permute-start.8 = (bf16[2,2,32,768]{3,2,1,0:T(8,128)(2,1)S(1)}, bf16[2,2,32,768]{3,2,1,0:T(8,128)(2,1)S(1)}, u32[]{:S(2)}, u32[]{:S(2)}) collective-permute-start(bf16[2,2,32,768]{3,2,1,0:T(8,128)(2,1)S(1)} %get-tuple-element.72), channel_id=1, source_target_pairs={{0,24},{8,16},{16,8},{24,0},{1,25},{9,17},{17,9},{25,1},{2,26},{10... | collective-permute-start | bytes 589832 | tf_op jit(solution)/shard_map/ppermute | solution.py:288
  134.8 8.5 %collective-permute-start.13 = (bf16[4,2,32,768]{3,2,1,0:T(8,128)(2,1)S(1)}, bf16[4,2,32,768]{3,2,1,0:T(8,128)(2,1)S(1)}, u32[]{:S(2)}, u32[]{:S(2)}) collective-permute-start(bf16[4,2,32,768]{3,2,1,0:T(8,128)(2,1)S(1)} %pad_maximum_fusion.1), channel_id=1, source_target_pairs={{0,4},{4,0},{1,5},{5,1},{2,6},{6,2},{3,7},{7,3},{8,12},{12,8},{9,1... | collective-permute-start | bytes 1179656 | tf_op jit(solution)/shard_map/ppermute | solution.py:396
  143.2 1.8 %collective-permute-start.9 = (bf16[4,2,32,768]{3,2,1,0:T(8,128)(2,1)S(1)}, bf16[4,2,32,768]{3,2,1,0:T(8,128)(2,1)S(1)}, u32[]{:S(2)}, u32[]{:S(2)}) collective-permute-start(bf16[4,2,32,768]{3,2,1,0:T(8,128)(2,1)S(1)} %pad_maximum_fusion), channel_id=1, source_target_pairs={{0,4},{4,0},{1,5},{5,1},{2,6},{6,2},{3,7},{7,3},{8,12},{12,8},{9,1... | collective-permute-start | bytes 1179656 | tf_op jit(solution)/shard_map/ppermute | solution.py:396
  (1 other events, 1.3 us)

commit v5 on v4

--- a/solution.py
+++ b/solution.py
@@ -41,8 +41,13 @@
 
 
 def permutation(size, source):
-    wanted = source(lax.broadcasted_iota(jnp.int32, (size, size), 0))
-    return (wanted == lax.broadcasted_iota(jnp.int32, (size, size), 1)).astype(F32).astype(BF16)
+    wanted = source(lax.broadcasted_iota(jnp.int32, (size, 1), 0))
+    found = lax.broadcasted_iota(jnp.int32, (size, size), 1) == wanted
+    return found.astype(F32).astype(BF16)
+
+
+def parted(number, size):
+    return lax.shift_right_logical(number, size.bit_length() - 1), lax.bitwise_and(number, size - 1)
 
 
 def row_shares(part_ref, states_any, *refs):
@@ -66,15 +71,16 @@
         copy.wait()
 
 
-def row_project(at_ref, x_ref, wq_ref, wk_ref, wv_ref, *refs):
-    q_ref, k_ref, v_ref, kept_ref = refs[-4:]
-    rows, cols, width = q_ref.shape
+def row_project(count, kept, at_ref, x_ref, *refs):
+    weight_refs, out_refs = refs[:count], refs[len(refs) - count - kept :]
+    rows, _, width = out_refs[0].shape
     block = x_ref.shape[1]
     x = x_ref[...] if x_ref.shape[0] == rows else x_ref[pl.ds(at_ref[0] * rows, rows)]
     place = pl.ds(pl.multiple_of(at_ref[0] * block, block), block)
-    kept_ref[:, place, :] = x
+    if kept:
+        out_refs[count][:, place, :] = x
     normed = normalize(x.astype(F32).reshape(rows * block, width))
-    for weight_ref, ref in ((wq_ref, q_ref), (wk_ref, k_ref), (wv_ref, v_ref)):
+    for weight_ref, ref in zip(weight_refs, out_refs[:count], strict=True):
         ref[:, place, :] = dot(normed, weight_ref[...]).astype(BF16).reshape(rows, block, width)
 
 
@@ -120,30 +126,28 @@
         prob_ref[at] = prob
 
 
-def row_update(seq_size, parts, chunks, core_ref, mine_ref, other_ref, v_ref, x_ref, wo_ref, mid_ref, o_ref):
-    rows, cols, width = x_ref.shape
-    head_dim = width // HEADS
-    pair = 2 * head_dim
-    half_pairs = HEADS // 2 // CORES
-    masks = head_masks(pair, head_dim)
-
-    for prob_ref, low in ((mine_ref, core_ref[0]), (other_ref, 1 - core_ref[0])):
-        for at in range(half_pairs):
-            lanes = pl.ds(pl.multiple_of((low * half_pairs + at) * pair, pair), pair)
-            prob = prob_ref[at]
-            for row in range(0, rows, 2):
-                fields = [v_ref[row + step, :, lanes] for step in range(2)]
-                values = jnp.concatenate(
-                    [
-                        jnp.concatenate([field * mask for field in fields], axis=1)
-                        for mask in masks
-                    ],
-                    axis=0,
-                )
-                result = dot(prob, values).astype(BF16)
-                o_ref[row, :, lanes] = result[:, :pair]
-                o_ref[row + 1, :, lanes] = result[:, pair:]
-
+def row_attend(low_ref, prob_ref, v_ref, o_ref):
+    rows, _, width = v_ref.shape
+    pair = 2 * (width // HEADS)
+    masks = head_masks(pair, pair // 2)
+    for at in range(prob_ref.shape[0]):
+        lanes = pl.ds(pl.multiple_of((low_ref[0] + at) * pair, pair), pair)
+        prob = prob_ref[at]
+        for row in range(0, rows, 2):
+            fields = [v_ref[row + step, :, lanes] for step in range(2)]
+            values = jnp.concatenate(
+                [jnp.concatenate([field * mask for field in fields], axis=1) for mask in masks],
+                axis=0,
+            )
+            result = dot(prob, values).astype(BF16)
+            o_ref[row, :, lanes] = result[:, :pair]
+            o_ref[row + 1, :, lanes] = result[:, pair:]
+
+
+def row_update(seq_size, parts, chunks, low_ref, prob_ref, v_ref, x_ref, wo_ref, *refs):
+    mid_ref, o_ref = refs[-2:]
+    row_attend(low_ref, prob_ref, v_ref, o_ref)
+    rows, cols, width = o_ref.shape
     at = 0
     step_at = 0
     for piece in chunks:
@@ -151,12 +155,9 @@
         inner = piece // seq_size
 
         def source(token):
-            row = lax.rem(token, rows)
-            rest = lax.div(token, rows)
-            step = lax.rem(rest, inner)
-            rest = lax.div(rest, inner)
-            part = lax.rem(rest, parts)
-            owner = lax.div(rest, parts)
+            rest, row = parted(token, rows)
+            rest, step = parted(rest, inner)
+            owner, part = parted(rest, parts)
             return (row * parts + part) * piece + owner * inner + step
 
         attended = o_ref[:, at * parts : (at + piece) * parts, :].reshape(tokens, width)
@@ -225,14 +226,14 @@
     tokens = rows * cols
 
     def source(token):
-        row = lax.div(token, cols)
-        col = lax.rem(token, cols)
+        row, col = parted(token, cols)
         at, base = 0, jnp.zeros_like(token)
         for piece in pieces:
             inner = piece // seq_size
             local = col - at
-            owner = lax.bitwise_xor(lax.div(local, inner), seq_ref[0])
-            here = (at + owner * inner + lax.rem(local, inner)) * rows + row
+            owner, step = parted(local, inner)
+            owner = lax.bitwise_xor(owner, seq_ref[0])
+            here = (at + owner * inner + step) * rows + row
             base = jnp.where((local >= 0) & (local < piece), here, base)
             at += piece
         return base
@@ -303,23 +304,28 @@
     blocks = [states] + [across(share, step + 1) for step, share in enumerate(shares)]
     halves = ((1 - core) * half_pairs).reshape(1), (core * half_pairs).reshape(1)
     places = [(part ^ step).reshape(1) for step in range(res_size)]
-    own, halves, core_place, place, places = lax.optimization_barrier(
-        (blocks[0], halves, core.reshape(1), seq.reshape(1), places)
+    own, halves, place, places = lax.optimization_barrier(
+        (blocks[0], halves, seq.reshape(1), places)
     )
     blocks[0] = own
+    def projected(step, weights, fields, kept):
+        count = len(weights) + kept
+        return pl.pallas_call(
+            functools.partial(row_project, len(weights), kept),
+            in_specs=[smem] + [vmem] * (1 + len(weights) + len(fields)),
+            out_specs=[vmem] * count,
+            out_shape=[jax.ShapeDtypeStruct((own_rows, cols, width), BF16)] * count,
+            input_output_aliases={2 + len(weights) + at: at for at in range(len(fields))},
+            compiler_params=params(),
+            cost_estimate=cost(2 * len(weights) * own_rows * block * width * width, 6e6),
+            name="row_project",
+        )(places[step], blocks[step], *weights, *fields)
+
+    last = res_size - 1
     fields = []
-    for step, field in enumerate(blocks):
-        fields = pl.pallas_call(
-            row_project,
-            in_specs=[smem] + [vmem] * (4 + len(fields)),
-            out_specs=[vmem] * 4,
-            out_shape=[jax.ShapeDtypeStruct((own_rows, cols, width), BF16)] * 4,
-            input_output_aliases={5 + at: at for at in range(len(fields))},
-            compiler_params=params(),
-            cost_estimate=cost(6 * own_rows * block * width * width, 6e6),
-            name="row_project",
-        )(places[step], field, row_query, row_key, row_value, *fields)
-    q, k, v, x = fields
+    for step in range(last):
+        fields = projected(step, [row_query, row_key, row_value], fields, 1)
+    q, k = projected(last, [row_query, row_key], fields[:2], 0)
 
     def scores(base):
         return pl.pallas_call(
@@ -347,6 +353,8 @@
         compiler_params=params(),
         name="row_sum",
     )(partial)
+    partial, fields = lax.optimization_barrier((partial, fields[2:]))
+    v, x = projected(last, [row_value], fields, 1)
     prob = pl.pallas_call(
         functools.partial(row_softmax, head_dim ** (-0.5) / math.sqrt(all_rows)),
         in_specs=[vmem, vmem],
@@ -355,21 +363,35 @@
         compiler_params=params(),
         name="row_softmax",
     )(partial, lax.ppermute(partial, "half", swap))
+    prob, v = lax.optimization_barrier((prob, v))
     prob = lax.all_to_all(prob, ("pair", "inner"), split_axis=0, concat_axis=0, tiled=True)
     prob = prob.reshape(half_pairs, cols, 2 * cols)
     prob_other = lax.ppermute(prob, "core", swap)
 
-    mid = pl.pallas_call(
+    attended = pl.pallas_call(
+        row_attend,
+        in_specs=[smem, vmem, vmem],
+        out_specs=vmem,
+        out_shape=jax.ShapeDtypeStruct((own_rows, cols, width), BF16),
+        compiler_params=params(),
+        cost_estimate=cost(2 * own_rows * cols * cols * width, 3e6),
+        name="row_attend",
+    )(halves[1], prob, v)
+    mid, _ = pl.pallas_call(
         functools.partial(row_update, seq_size, res_size, chunks),
         in_specs=[smem] + [vmem] * 5,
-        out_shape=jax.ShapeDtypeStruct(
-            (seq_size * res_size, block // seq_size, own_rows, width), BF16
-        ),
-        scratch_shapes=[pltpu.VMEM((own_rows, cols, width), BF16)],
+        out_specs=[vmem, vmem],
+        out_shape=[
+            jax.ShapeDtypeStruct(
+                (seq_size * res_size, block // seq_size, own_rows, width), BF16
+            ),
+            jax.ShapeDtypeStruct((own_rows, cols, width), BF16),
+        ],
+        input_output_aliases={5: 1},
         compiler_params=params(),
-        cost_estimate=cost(3 * own_rows * cols * width * width, 8e6),
+        cost_estimate=cost(2 * own_rows * cols * width * (width + cols), 8e6),
         name="row_update",
-    )(core_place, prob, prob_other, v, x, row_out)
+    )(halves[0], prob_other, v, x, row_out, attended)
 
     moved = lax.all_to_all(
         mid, ("pair", "core", "half", "inner"), split_axis=0, concat_axis=0, tiled=True

time: 147 us -> 146 us (level)
    pallas_call x4 -> x6, Pallas kernels: 5.22 us -> 6.01 us  [the longest x5 5.6 us: projected(): pl.pallas_call(functools.partial(row_project, len(weights), kept), in_spe...]
    unnamed x22 -> x20, local copies, waits for them, and re-layouts: 3.99 us -> 3.98 us
  transfers between devices with their start and end apart: 14 -> 14, of which waited for: 9 -> 9; matrix products, arithmetic and copies ran while one was open for 0% -> 0% of each run, Pallas kernels for 7% -> 8%
where the time goes in v5:
time: 146 us
  blocking collectives  65.6 us (45%)
  waiting for transfers between devices  36.1 us (25%)
  Pallas kernels  24.9 us (17%)
  starting transfers between devices  14.7 us (10%)
  local copies, waits for them, and re-layouts  4.04 us (3%)
    all_to_all x1, blocking collectives, on_device(): lax.all_to_all(mid, ('pair', 'core', 'half', 'inner'), split_axis=0, conc...  38.7 us
    ppermute x3, waiting for transfers between devices, across(): lax.ppermute(field, ('half', 'inner'), [(at, at ^ step) for at in range(r...  20.8 us
    all_to_all x1, blocking collectives, on_device(): lax.all_to_all((mine + other).reshape(share), ('pair', 'inner'), split_ax...  17.9 us
    ppermute x6, waiting for transfers between devices, around(): lax.ppermute(field, 'pair', [(at, at ^ step) for at in range(pairs_size)])  9.72 us
    pallas_call x2, Pallas kernels, on_device(): pl.pallas_call(functools.partial(column_update, first_at), in_specs=[smem...  9.65 us
    all_to_all x1, blocking collectives, on_device(): lax.all_to_all(prob, ('pair', 'inner'), split_axis=0, concat_axis=0, tile...  9.02 us
    ppermute x6, starting transfers between devices, around(): lax.ppermute(field, 'pair', [(at, at ^ step) for at in range(pairs_size)])  7.11 us
    ppermute x3, starting transfers between devices, across(): lax.ppermute(field, ('half', 'inner'), [(at, at ^ step) for at in range(r...  5.68 us
  transfers between devices with their start and end apart: 14, of which 9 were waited for; matrix products, arithmetic and copies ran while one was open for 0% of the time, Pallas kernels for 8%

profile of v5, /device:TPU:0, one launch (start us, length us, event | category | flops | bytes accessed | tf_op | source)
XLA Modules:
  0.0 145.8 jit_solution(5130510984885117581)
XLA Ops:
  0.0 2.2 %row_shares.1 = (bf16[8,32,768]{2,1,0:T(8,128)(2,1)}, bf16[8,32,768]{2,1,0:T(8,128)(2,1)}, bf16[8,32,768]{2,1,0:T(8,128)(2,1)}) custom-call(s32[1]{0:T(128)} %bitcast.3.part_ref.at_ref, bf16[32,32,768]{2,1,0:T(8,128)(2,1)} %x_ref), custom_call_target="tpu_custom_call" | custom-call | tf_op jit(solution)/shard_map/row_shares/pallas_call | solution.py:291
  2.2 3.1 %collective-permute-start.2 = (bf16[8,32,768]{2,1,0:T(8,128)(2,1)}, bf16[8,32,768]{2,1,0:T(8,128)(2,1)S(1)}, u32[]{:S(2)}, u32[]{:S(2)}) collective-permute-start(bf16[8,32,768]{2,1,0:T(8,128)(2,1)} %get-tuple-element.54), channel_id=1, source_target_pairs={{0,1},{1,0},{2,3},{3,2},{4,5},{5,4},{6,7},{7,6},{8,9},{9,8},{10,11... | collective-permute-start | bytes 1179656 | tf_op jit(solution)/shard_map/ppermute | solution.py:286
  5.3 2.6 %collective-permute-start.1 = (bf16[8,32,768]{2,1,0:T(8,128)(2,1)}, bf16[8,32,768]{2,1,0:T(8,128)(2,1)S(1)}, u32[]{:S(2)}, u32[]{:S(2)}) collective-permute-start(bf16[8,32,768]{2,1,0:T(8,128)(2,1)} %get-tuple-element.52), channel_id=1, source_target_pairs={{0,2},{1,3},{2,0},{3,1},{4,6},{5,7},{6,4},{7,5},{8,10},{9,11},{10,... | collective-permute-start | bytes 1179656 | tf_op jit(solution)/shard_map/ppermute | solution.py:286
  10.4 1.4 copy-done.4
  11.8 1.3 row_project.5
  13.1 9.1 %collective-permute-done.2.x_ref = bf16[8,32,768]{2,1,0:T(8,128)(2,1)S(1)} collective-permute-done((bf16[8,32,768]{2,1,0:T(8,128)(2,1)}, bf16[8,32,768]{2,1,0:T(8,128)(2,1)S(1)}, u32[]{:S(2)}, u32[]{:S(2)}) %collective-permute-start.2) | collective-permute-done | bytes 393248 | tf_op jit(solution)/shard_map/ppermute | solution.py:286
  22.2 1.3 row_project.6
  23.6 11.7 %collective-permute-done.1.x_ref = bf16[8,32,768]{2,1,0:T(8,128)(2,1)S(1)} collective-permute-done((bf16[8,32,768]{2,1,0:T(8,128)(2,1)}, bf16[8,32,768]{2,1,0:T(8,128)(2,1)S(1)}, u32[]{:S(2)}, u32[]{:S(2)}) %collective-permute-start.1) | collective-permute-done | bytes 393248 | tf_op jit(solution)/shard_map/ppermute | solution.py:286
  35.3 1.3 row_project.7
  40.1 17.9 %all_to_all.15.parts_ref = f32[8,48,256]{2,1,0:T(8,128)S(1)} all-to-all(f32[8,48,256]{2,1,0:T(8,128)S(1)} %bitcast.11), channel_id=1, replica_groups=mesh['pair'=4,'core'=2,'half'=2,'inner'=2] {'pair','inner'}, dimensions={0} | all-to-all | bytes 786432 | tf_op jit(solution)/shard_map/all_to_all | solution.py:345
  58.0 1.6 %collective-permute-start.4 = (f32[48,256]{1,0:T(8,128)S(1)}, f32[48,256]{1,0:T(8,128)S(1)}, u32[]{:S(2)}, u32[]{:S(2)}) collective-permute-start(f32[48,256]{1,0:T(8,128)S(1)} %row_sum.1.mine_ref), channel_id=1, source_target_pairs={{0,2},{2,0},{1,3},{3,1},{4,6},{6,4},{5,7},{7,5},{8,10},{10,8},{9,1... | collective-permute-start | bytes 147464 | tf_op jit(solution)/shard_map/ppermute | solution.py:365
  60.3 3.3 %collective-permute-done.4.other_ref = f32[48,256]{1,0:T(8,128)S(1)} collective-permute-done((f32[48,256]{1,0:T(8,128)S(1)}, f32[48,256]{1,0:T(8,128)S(1)}, u32[]{:S(2)}, u32[]{:S(2)}) %collective-permute-start.4) | collective-permute-done | bytes 49184 | tf_op jit(solution)/shard_map/ppermute | solution.py:365
  63.8 9.0 %all_to_all.16 = bf16[8,48,256]{2,1,0:T(8,128)(2,1)S(1)} all-to-all(bf16[8,48,256]{2,1,0:T(8,128)(2,1)S(1)} %row_softmax.1), channel_id=1, replica_groups=mesh['pair'=4,'core'=2,'half'=2,'inner'=2] {'pair','inner'}, dimensions={0} | all-to-all | bytes 393216 | tf_op jit(solution)/shard_map/all_to_all | solution.py:367
  74.3 2.7 %row_update.1 = (bf16[32,4,8,768]{3,2,1,0:T(8,128)(2,1)S(1)}, bf16[8,128,768]{2,1,0:T(8,128)(2,1)S(1)}) custom-call(s32[1]{0:T(128)} %bitcast.base_ref.low_ref, bf16[3,128,256]{2,1,0:T(8,128)(2,1)S(1)} %collective-permute-done.5.prob_ref, bf16[8,128,768]{2,1,0:T(8,128)(2,1)S(1)} %get-tuple-element.76.v_ref, ...), custom_call_target="tpu_custom_call", output_to_operand_aliasing={{1}: (5, {})} | custom-call | flops 1409286144 | bytes 8000000 | tf_op jit(solution)/shard_map/row_update/pallas_call | solution.py:380
  77.0 38.7 %all_to_all.17.mid_ref = bf16[32,4,8,768]{3,2,1,0:T(8,128)(2,1)S(1)} all-to-all(bf16[32,4,8,768]{3,2,1,0:T(8,128)(2,1)S(1)} %get-tuple-element.78), channel_id=1, replica_groups=mesh['pair'=4,'core'=2,'half'=2,'inner'=2] {'pair','core','half','inner'}, dimensions={0} | all-to-all | bytes 3145728 | tf_op jit(solution)/shard_map/all_to_all | solution.py:396
  115.8 4.8 %column_update.3 = (bf16[2,2,32,768]{3,2,1,0:T(8,128)(2,1)S(1)}, bf16[2,2,32,768]{3,2,1,0:T(8,128)(2,1)S(1)}, bf16[2,2,32,768]{3,2,1,0:T(8,128)(2,1)S(1)}, bf16[2,2,32,768]{3,2,1,0:T(8,128)(2,1)S(1)}) custom-call(s32[1]{0:T(128)} %bitcast.2.seq_ref, bf16[32,4,8,768]{3,2,1,0:T(8,128)(2,1)S(1)} %all_to_all.17.mid_ref, bf16[768,768]{1,0:T(8,128)(2,1)S(1)} %copy-done.6, ...), custom_call_target="tpu_custom_call" | custom-call | flops 3019898880 | bytes 8000000 | tf_op jit(solution)/shard_map/column_update/pallas_call | solution.py:404
  120.6 1.5 %collective-permute-start.10 = (bf16[2,2,32,768]{3,2,1,0:T(8,128)(2,1)S(1)}, bf16[2,2,32,768]{3,2,1,0:T(8,128)(2,1)S(1)}, u32[]{:S(2)}, u32[]{:S(2)}) collective-permute-start(bf16[2,2,32,768]{3,2,1,0:T(8,128)(2,1)S(1)} %get-tuple-element.84), channel_id=1, source_target_pairs={{0,8},{8,0},{16,24},{24,16},{1,9},{9,1},{17,25},{25,17},{2,10},{10... | collective-permute-start | bytes 589832 | tf_op jit(solution)/shard_map/ppermute | solution.py:289
  124.1 4.8 %column_update.2 = (bf16[2,2,32,768]{3,2,1,0:T(8,128)(2,1)S(1)}, bf16[2,2,32,768]{3,2,1,0:T(8,128)(2,1)S(1)}, bf16[2,2,32,768]{3,2,1,0:T(8,128)(2,1)S(1)}, bf16[2,2,32,768]{3,2,1,0:T(8,128)(2,1)S(1)}) custom-call(s32[1]{0:T(128)} %bitcast.2.seq_ref, bf16[32,4,8,768]{3,2,1,0:T(8,128)(2,1)S(1)} %all_to_all.17.mid_ref, bf16[768,768]{1,0:T(8,128)(2,1)S(1)} %copy-done.6, ...), custom_call_target="tpu_custom_call" | custom-call | flops 3019898880 | bytes 8000000 | tf_op jit(solution)/shard_map/column_update/pallas_call | solution.py:404
  129.0 1.5 %collective-permute-start.6 = (bf16[2,2,32,768]{3,2,1,0:T(8,128)(2,1)S(1)}, bf16[2,2,32,768]{3,2,1,0:T(8,128)(2,1)S(1)}, u32[]{:S(2)}, u32[]{:S(2)}) collective-permute-start(bf16[2,2,32,768]{3,2,1,0:T(8,128)(2,1)S(1)} %get-tuple-element.80), channel_id=1, source_target_pairs={{0,8},{8,0},{16,24},{24,16},{1,9},{9,1},{17,25},{25,17},{2,10},{10... | collective-permute-start | bytes 589832 | tf_op jit(solution)/shard_map/ppermute | solution.py:289
  132.6 1.5 %collective-permute-done.11.refs_2_ = bf16[2,2,32,768]{3,2,1,0:T(8,128)(2,1)S(1)} collective-permute-done((bf16[2,2,32,768]{3,2,1,0:T(8,128)(2,1)S(1)}, bf16[2,2,32,768]{3,2,1,0:T(8,128)(2,1)S(1)}, u32[]{:S(2)}, u32[]{:S(2)}) %collective-permute-start.11) | collective-permute-done | bytes 196640 | tf_op jit(solution)/shard_map/ppermute | solution.py:289
  134.3 2.6 %collective-permute-done.6.refs_1_ = bf16[2,2,32,768]{3,2,1,0:T(8,128)(2,1)S(1)} collective-permute-done((bf16[2,2,32,768]{3,2,1,0:T(8,128)(2,1)S(1)}, bf16[2,2,32,768]{3,2,1,0:T(8,128)(2,1)S(1)}, u32[]{:S(2)}, u32[]{:S(2)}) %collective-permute-start.6) | collective-permute-done | bytes 196640 | tf_op jit(solution)/shard_map/ppermute | solution.py:289
  136.9 5.6 %collective-permute-done.7.refs_2_ = bf16[2,2,32,768]{3,2,1,0:T(8,128)(2,1)S(1)} collective-permute-done((bf16[2,2,32,768]{3,2,1,0:T(8,128)(2,1)S(1)}, bf16[2,2,32,768]{3,2,1,0:T(8,128)(2,1)S(1)}, u32[]{:S(2)}, u32[]{:S(2)}) %collective-permute-start.7) | collective-permute-done | bytes 196640 | tf_op jit(solution)/shard_map/ppermute | solution.py:289
  142.7 1.4 assemble.2.refs_5_
  144.4 1.4 assemble.3
  (54 shorter events, 13.1 us)
Async XLA Ops:
  0.0 7.9 %copy-start = (bf16[768,768]{1,0:T(8,128)(2,1)S(1)}, bf16[768,768]{1,0:T(8,128)(2,1)}, u32[]{:S(2)}) copy-start(bf16[768,768]{1,0:T(8,128)(2,1)} %refs_0_.9) | copy-start | bytes 3538948
  2.2 20.1 %collective-permute-start.2 = (bf16[8,32,768]{2,1,0:T(8,128)(2,1)}, bf16[8,32,768]{2,1,0:T(8,128)(2,1)S(1)}, u32[]{:S(2)}, u32[]{:S(2)}) collective-permute-start(bf16[8,32,768]{2,1,0:T(8,128)(2,1)} %get-tuple-element.54), channel_id=1, source_target_pairs={{0,1},{1,0},{2,3},{3,2},{4,5},{5,4},{6,7},{7,6},{8,9},{9,8},{10,11... | collective-permute-start | bytes 1179656 | tf_op jit(solution)/shard_map/ppermute | solution.py:286
  5.3 30.0 %collective-permute-start.1 = (bf16[8,32,768]{2,1,0:T(8,128)(2,1)}, bf16[8,32,768]{2,1,0:T(8,128)(2,1)S(1)}, u32[]{:S(2)}, u32[]{:S(2)}) collective-permute-start(bf16[8,32,768]{2,1,0:T(8,128)(2,1)} %get-tuple-element.52), channel_id=1, source_target_pairs={{0,2},{1,3},{2,0},{3,1},{4,6},{5,7},{6,4},{7,5},{8,10},{9,11},{10,... | collective-permute-start | bytes 1179656 | tf_op jit(solution)/shard_map/ppermute | solution.py:286
  7.8 28.7 %collective-permute-start = (bf16[8,32,768]{2,1,0:T(8,128)(2,1)}, bf16[8,32,768]{2,1,0:T(8,128)(2,1)S(1)}, u32[]{:S(2)}, u32[]{:S(2)}) collective-permute-start(bf16[8,32,768]{2,1,0:T(8,128)(2,1)} %get-tuple-element.50), channel_id=1, source_target_pairs={{0,3},{1,2},{2,1},{3,0},{4,7},{5,6},{6,5},{7,4},{8,11},{9,10},{10,... | collective-permute-start | bytes 1179656 | tf_op jit(solution)/shard_map/ppermute | solution.py:286
  7.9 1.3 copy-start.1
  9.1 1.3 copy-start.3
  10.4 1.4 copy-start.4
  11.8 10.4 %copy-start.2 = (bf16[768,768]{1,0:T(8,128)(2,1)S(1)}, bf16[768,768]{1,0:T(8,128)(2,1)}, u32[]{:S(2)}) copy-start(bf16[768,768]{1,0:T(8,128)(2,1)} %refs_0_.8) | copy-start | bytes 3538948
  38.3 1.8 %collective-permute-start.3 = (f32[3,128,256]{2,1,0:T(8,128)S(1)}, f32[3,128,256]{2,1,0:T(8,128)S(1)}, u32[]{:S(2)}, u32[]{:S(2)}) collective-permute-start(f32[3,128,256]{2,1,0:T(8,128)S(1)} %row_scores.3), channel_id=1, source_target_pairs={{0,4},{4,0},{1,5},{5,1},{2,6},{6,2},{3,7},{7,3},{8,12},{12,8},{9,1... | collective-permute-start | bytes 1179656 | tf_op jit(solution)/shard_map/ppermute | solution.py:341
  58.0 5.6 %collective-permute-start.4 = (f32[48,256]{1,0:T(8,128)S(1)}, f32[48,256]{1,0:T(8,128)S(1)}, u32[]{:S(2)}, u32[]{:S(2)}) collective-permute-start(f32[48,256]{1,0:T(8,128)S(1)} %row_sum.1.mine_ref), channel_id=1, source_target_pairs={{0,2},{2,0},{1,3},{3,1},{4,6},{6,4},{5,7},{7,5},{8,10},{10,8},{9,1... | collective-permute-start | bytes 147464 | tf_op jit(solution)/shard_map/ppermute | solution.py:365
  72.8 1.4 copy-start.5
  72.8 1.4 collective-permute-start.5
  74.3 41.5 %copy-start.8 = (bf16[768,768]{1,0:T(8,128)(2,1)S(1)}, bf16[768,768]{1,0:T(8,128)(2,1)}, u32[]{:S(2)}) copy-start(bf16[768,768]{1,0:T(8,128)(2,1)} %wv_ref.3) | copy-start | bytes 3538948
  74.3 41.5 %copy-start.9 = (bf16[768,768]{1,0:T(8,128)(2,1)S(1)}, bf16[768,768]{1,0:T(8,128)(2,1)}, u32[]{:S(2)}) copy-start(bf16[768,768]{1,0:T(8,128)(2,1)} %wo_ref.5) | copy-start | bytes 3538948
  77.0 38.7 %copy-start.6 = (bf16[768,768]{1,0:T(8,128)(2,1)S(1)}, bf16[768,768]{1,0:T(8,128)(2,1)}, u32[]{:S(2)}) copy-start(bf16[768,768]{1,0:T(8,128)(2,1)} %wq_ref.3) | copy-start | bytes 3538948
  77.0 38.7 %copy-start.7 = (bf16[768,768]{1,0:T(8,128)(2,1)S(1)}, bf16[768,768]{1,0:T(8,128)(2,1)}, u32[]{:S(2)}) copy-start(bf16[768,768]{1,0:T(8,128)(2,1)} %wk_ref.3) | copy-start | bytes 3538948
  120.6 11.2 %collective-permute-start.10 = (bf16[2,2,32,768]{3,2,1,0:T(8,128)(2,1)S(1)}, bf16[2,2,32,768]{3,2,1,0:T(8,128)(2,1)S(1)}, u32[]{:S(2)}, u32[]{:S(2)}) collective-permute-start(bf16[2,2,32,768]{3,2,1,0:T(8,128)(2,1)S(1)} %get-tuple-element.84), channel_id=1, source_target_pairs={{0,8},{8,0},{16,24},{24,16},{1,9},{9,1},{17,25},{25,17},{2,10},{10... | collective-permute-start | bytes 589832 | tf_op jit(solution)/shard_map/ppermute | solution.py:289
  122.1 12.0 %collective-permute-start.11 = (bf16[2,2,32,768]{3,2,1,0:T(8,128)(2,1)S(1)}, bf16[2,2,32,768]{3,2,1,0:T(8,128)(2,1)S(1)}, u32[]{:S(2)}, u32[]{:S(2)}) collective-permute-start(bf16[2,2,32,768]{3,2,1,0:T(8,128)(2,1)S(1)} %get-tuple-element.85), channel_id=1, source_target_pairs={{0,16},{8,24},{16,0},{24,8},{1,17},{9,25},{17,1},{25,9},{2,18},{10... | collective-permute-start | bytes 589832 | tf_op jit(solution)/shard_map/ppermute | solution.py:289
  123.4 10.7 %collective-permute-start.12 = (bf16[2,2,32,768]{3,2,1,0:T(8,128)(2,1)S(1)}, bf16[2,2,32,768]{3,2,1,0:T(8,128)(2,1)S(1)}, u32[]{:S(2)}, u32[]{:S(2)}) collective-permute-start(bf16[2,2,32,768]{3,2,1,0:T(8,128)(2,1)S(1)} %get-tuple-element.86), channel_id=1, source_target_pairs={{0,24},{8,16},{16,8},{24,0},{1,25},{9,17},{17,9},{25,1},{2,26},{10... | collective-permute-start | bytes 589832 | tf_op jit(solution)/shard_map/ppermute | solution.py:289
  129.0 7.9 %collective-permute-start.6 = (bf16[2,2,32,768]{3,2,1,0:T(8,128)(2,1)S(1)}, bf16[2,2,32,768]{3,2,1,0:T(8,128)(2,1)S(1)}, u32[]{:S(2)}, u32[]{:S(2)}) collective-permute-start(bf16[2,2,32,768]{3,2,1,0:T(8,128)(2,1)S(1)} %get-tuple-element.80), channel_id=1, source_target_pairs={{0,8},{8,0},{16,24},{24,16},{1,9},{9,1},{17,25},{25,17},{2,10},{10... | collective-permute-start | bytes 589832 | tf_op jit(solution)/shard_map/ppermute | solution.py:289
  130.5 12.0 %collective-permute-start.7 = (bf16[2,2,32,768]{3,2,1,0:T(8,128)(2,1)S(1)}, bf16[2,2,32,768]{3,2,1,0:T(8,128)(2,1)S(1)}, u32[]{:S(2)}, u32[]{:S(2)}) collective-permute-start(bf16[2,2,32,768]{3,2,1,0:T(8,128)(2,1)S(1)} %get-tuple-element.81), channel_id=1, source_target_pairs={{0,16},{8,24},{16,0},{24,8},{1,17},{9,25},{17,1},{25,9},{2,18},{10... | collective-permute-start | bytes 589832 | tf_op jit(solution)/shard_map/ppermute | solution.py:289
  131.8 10.7 %collective-permute-start.8 = (bf16[2,2,32,768]{3,2,1,0:T(8,128)(2,1)S(1)}, bf16[2,2,32,768]{3,2,1,0:T(8,128)(2,1)S(1)}, u32[]{:S(2)}, u32[]{:S(2)}) collective-permute-start(bf16[2,2,32,768]{3,2,1,0:T(8,128)(2,1)S(1)} %get-tuple-element.82), channel_id=1, source_target_pairs={{0,24},{8,16},{16,8},{24,0},{1,25},{9,17},{17,9},{25,1},{2,26},{10... | collective-permute-start | bytes 589832 | tf_op jit(solution)/shard_map/ppermute | solution.py:289
  134.2 8.5 %collective-permute-start.13 = (bf16[4,2,32,768]{3,2,1,0:T(8,128)(2,1)S(1)}, bf16[4,2,32,768]{3,2,1,0:T(8,128)(2,1)S(1)}, u32[]{:S(2)}, u32[]{:S(2)}) collective-permute-start(bf16[4,2,32,768]{3,2,1,0:T(8,128)(2,1)S(1)} %pad_maximum_fusion.1), channel_id=1, source_target_pairs={{0,4},{4,0},{1,5},{5,1},{2,6},{6,2},{3,7},{7,3},{8,12},{12,8},{9,1... | collective-permute-start | bytes 1179656 | tf_op jit(solution)/shard_map/ppermute | solution.py:418
  142.6 1.8 %collective-permute-start.9 = (bf16[4,2,32,768]{3,2,1,0:T(8,128)(2,1)S(1)}, bf16[4,2,32,768]{3,2,1,0:T(8,128)(2,1)S(1)}, u32[]{:S(2)}, u32[]{:S(2)}) collective-permute-start(bf16[4,2,32,768]{3,2,1,0:T(8,128)(2,1)S(1)} %pad_maximum_fusion), channel_id=1, source_target_pairs={{0,4},{4,0},{1,5},{5,1},{2,6},{6,2},{3,7},{7,3},{8,12},{12,8},{9,1... | collective-permute-start | bytes 1179656 | tf_op jit(solution)/shard_map/ppermute | solution.py:418

commit v6 on v5

--- a/solution.py
+++ b/solution.py
@@ -217,12 +217,14 @@
 def in_order(refs, at, pairs_size):
     straight = refs[at * (pairs_size + 1) : at * (pairs_size + 1) + pairs_size]
     crossed = refs[at * (pairs_size + 1) + pairs_size]
-    return [field for step in range(pairs_size) for field in (straight[step][0], crossed[step])]
-
-
-def assemble(seq_size, pieces, seq_ref, *refs):
-    out_ref = refs[-1]
-    rows, cols, width = out_ref.shape
+    return [field for step in range(pairs_size) for field in (straight[step].at[0], crossed.at[step])]
+
+
+def assemble(seq_size, pieces, slot, seq_ref, *refs):
+    out_any, held_ref, sems = refs[-3:]
+    count = sems.shape[0]
+    rows, cols, width = held_ref.shape
+    rows = rows // count
     tokens = rows * cols
 
     def source(token):
@@ -238,20 +240,27 @@
             at += piece
         return base
 
-    gathered = jnp.concatenate(
-        [
-            field.reshape(-1, width)
-            for at in range(len(pieces))
-            for field in in_order(refs, at, seq_size // CORES)
-        ],
-        axis=0,
-    )
-    moved = dot(permutation(tokens, source), gathered)
-    out_ref[...] = moved.astype(BF16).reshape(rows, cols, width)
-
-
-def whole(shape):
-    return pl.BlockSpec(shape, lambda *_: (0,) * len(shape))
+    order = permutation(tokens, source)
+    copies = []
+    for step in range(count):
+        own = pl.ds(step * rows, rows)
+        gathered = jnp.concatenate(
+            [
+                field[:, own].reshape(-1, width)
+                for at in range(len(pieces))
+                for field in in_order(refs, at, seq_size // CORES)
+            ],
+            axis=0,
+        )
+        held_ref[own] = dot(order, gathered).astype(BF16).reshape(rows, cols, width)
+        copies.append(
+            pltpu.make_async_copy(
+                held_ref.at[own], out_any.at[own, pl.ds(slot * cols, cols)], sems.at[step]
+            )
+        )
+        copies[-1].start()
+    for copy in copies:
+        copy.wait()
 
 
 def params(limit=VMEM_BYTES):
@@ -301,7 +310,7 @@
         compiler_params=params(FULL_VMEM_BYTES),
         name="row_shares",
     )(part.reshape(1), states)
-    blocks = [states] + [across(share, step + 1) for step, share in enumerate(shares)]
+    blocks = [states, None] + [across(share, step + 2) for step, share in enumerate(shares[1:])]
     halves = ((1 - core) * half_pairs).reshape(1), (core * half_pairs).reshape(1)
     places = [(part ^ step).reshape(1) for step in range(res_size)]
     own, halves, place, places = lax.optimization_barrier(
@@ -321,10 +330,13 @@
             name="row_project",
         )(places[step], blocks[step], *weights, *fields)
 
-    last = res_size - 1
+    *early, last = [0, res_size - 1] + list(range(1, res_size - 1))
     fields = []
-    for step in range(last):
+    for step in early:
         fields = projected(step, [row_query, row_key, row_value], fields, 1)
+        if step == 0:
+            near, fields = lax.optimization_barrier((shares[0], fields))
+            blocks[1] = across(near, 1)
     q, k = projected(last, [row_query, row_key], fields[:2], 0)
 
     def scores(base):
@@ -418,29 +430,26 @@
         crossed = lax.ppermute(jnp.stack([field[1] for field in arrived]), "core", swap)
         home.append(arrived + [crossed])
 
-    row_step = 16
+    steps = 2
     out = []
     at = 0
     for slot in range(block // SLOT):
-        pieces, parts, counts = [], [], []
+        pieces, parts = [], []
         while sum(pieces) < SLOT:
             pieces.append(chunks[at])
             parts += home[at]
-            counts += [1] * pairs_size + [pairs_size]
             at += 1
         out = [
             pl.pallas_call(
-                functools.partial(assemble, seq_size, pieces),
-                grid=(rows // row_step,),
-                in_specs=[smem]
-                + [
-                    pl.BlockSpec((count, field.shape[1], row_step, width), lambda g: (0, 0, g, 0))
-                    for field, count in zip(parts, counts, strict=True)
-                ]
-                + [anywhere] * len(out),
-                out_specs=pl.BlockSpec((row_step, SLOT, width), lambda g, slot=slot: (g, slot, 0)),
+                functools.partial(assemble, seq_size, pieces, slot),
+                in_specs=[smem] + [vmem] * len(parts) + [anywhere] * len(out),
+                out_specs=anywhere,
                 out_shape=jax.ShapeDtypeStruct((rows, block, width), BF16),
                 input_output_aliases={1 + len(parts): 0} if out else {},
+                scratch_shapes=[
+                    pltpu.VMEM((rows, SLOT, width), BF16),
+                    pltpu.SemaphoreType.DMA((steps,)),
+                ],
                 compiler_params=params(),
                 name="assemble",
             )(place, *parts, *out)

time: 146 us -> 145 us (level)
  blocking collectives: 65.6 us -> 60.2 us
  waiting for transfers between devices: 36.1 us -> 39.8 us
    all_to_all x1, blocking collectives: 17.9 us -> 12.2 us  [on_device(): lax.all_to_all((mine + other).reshape(share), ('pair', 'inner'), split_ax...]
    ppermute x3, waiting for transfers between devices: 20.8 us -> 25.2 us  [across(): lax.ppermute(field, ('half', 'inner'), [(at, at ^ step) for at in range(r...]
    unnamed x20 -> x24, local copies, waits for them, and re-layouts: 3.98 us -> 3.99 us
  transfers between devices with their start and end apart: 14 -> 14, of which waited for: 9 -> 10; matrix products, arithmetic and copies ran while one was open for 0% -> 0% of each run, Pallas kernels for 8% -> 8%
where the time goes in v6:
time: 145 us
  blocking collectives  60.2 us (42%)
  waiting for transfers between devices  39.8 us (27%)
  Pallas kernels  24.5 us (17%)
  starting transfers between devices  15.7 us (11%)
  local copies, waits for them, and re-layouts  4.05 us (3%)
    all_to_all x1, blocking collectives, on_device(): lax.all_to_all(mid, ('pair', 'core', 'half', 'inner'), split_axis=0, conc...  39 us
    ppermute x3, waiting for transfers between devices, across(): lax.ppermute(field, ('half', 'inner'), [(at, at ^ step) for at in range(r...  25.2 us
    all_to_all x1, blocking collectives, on_device(): lax.all_to_all((mine + other).reshape(share), ('pair', 'inner'), split_ax...  12.2 us
    ppermute x6, waiting for transfers between devices, around(): lax.ppermute(field, 'pair', [(at, at ^ step) for at in range(pairs_size)])  9.72 us
    pallas_call x2, Pallas kernels, on_device(): pl.pallas_call(functools.partial(column_update, first_at), in_specs=[smem...  9.65 us
    all_to_all x1, blocking collectives, on_device(): lax.all_to_all(prob, ('pair', 'inner'), split_axis=0, concat_axis=0, tile...  9.02 us
    ppermute x6, starting transfers between devices, around(): lax.ppermute(field, 'pair', [(at, at ^ step) for at in range(pairs_size)])  7.11 us
    ppermute x3, starting transfers between devices, across(): lax.ppermute(field, ('half', 'inner'), [(at, at ^ step) for at in range(r...  5.76 us
  transfers between devices with their start and end apart: 14, of which 10 were waited for; matrix products, arithmetic and copies ran while one was open for 0% of the time, Pallas kernels for 8%

profile of v6, /device:TPU:0, one launch (start us, length us, event | category | flops | bytes accessed | tf_op | source)
XLA Modules:
  0.0 144.8 jit_solution(11140547139123321591)
XLA Ops:
  0.0 2.2 %row_shares.1 = (bf16[8,32,768]{2,1,0:T(8,128)(2,1)}, bf16[8,32,768]{2,1,0:T(8,128)(2,1)}, bf16[8,32,768]{2,1,0:T(8,128)(2,1)}) custom-call(s32[1]{0:T(128)} %bitcast.3.part_ref.at_ref, bf16[32,32,768]{2,1,0:T(8,128)(2,1)} %x_ref), custom_call_target="tpu_custom_call" | custom-call | tf_op jit(solution)/shard_map/row_shares/pallas_call | solution.py:300
  2.2 5.1 %collective-permute-start.2 = (bf16[8,32,768]{2,1,0:T(8,128)(2,1)}, bf16[8,32,768]{2,1,0:T(8,128)(2,1)S(1)}, u32[]{:S(2)}, u32[]{:S(2)}) collective-permute-start(bf16[8,32,768]{2,1,0:T(8,128)(2,1)} %get-tuple-element.66), channel_id=1, source_target_pairs={{0,3},{1,2},{2,1},{3,0},{4,7},{5,6},{6,5},{7,4},{8,11},{9,10},{10,... | collective-permute-start | bytes 1179656 | tf_op jit(solution)/shard_map/ppermute | solution.py:295
  9.8 1.4 copy-done.4
  11.2 1.3 row_project.5
  13.2 4.3 %collective-permute-done.2.x_ref = bf16[8,32,768]{2,1,0:T(8,128)(2,1)S(1)} collective-permute-done((bf16[8,32,768]{2,1,0:T(8,128)(2,1)}, bf16[8,32,768]{2,1,0:T(8,128)(2,1)S(1)}, u32[]{:S(2)}, u32[]{:S(2)}) %collective-permute-start.2) | collective-permute-done | bytes 393248 | tf_op jit(solution)/shard_map/ppermute | solution.py:295
  17.5 1.3 row_project.6
  18.8 7.3 %collective-permute-done.1.x_ref = bf16[8,32,768]{2,1,0:T(8,128)(2,1)S(1)} collective-permute-done((bf16[8,32,768]{2,1,0:T(8,128)(2,1)S(1)}, bf16[8,32,768]{2,1,0:T(8,128)(2,1)S(1)}, u32[]{:S(2)}, u32[]{:S(2)}) %collective-permute-start.1) | collective-permute-done | bytes 393248 | tf_op jit(solution)/shard_map/ppermute | solution.py:295
  26.1 1.3 row_project.7
  27.4 13.6 %collective-permute-done.x_ref = bf16[8,32,768]{2,1,0:T(8,128)(2,1)S(1)} collective-permute-done((bf16[8,32,768]{2,1,0:T(8,128)(2,1)S(1)}, bf16[8,32,768]{2,1,0:T(8,128)(2,1)S(1)}, u32[]{:S(2)}, u32[]{:S(2)}) %collective-permute-start) | collective-permute-done | bytes 393248 | tf_op jit(solution)/shard_map/ppermute | solution.py:295
  44.6 12.2 %all_to_all.15.parts_ref = f32[8,48,256]{2,1,0:T(8,128)S(1)} all-to-all(f32[8,48,256]{2,1,0:T(8,128)S(1)} %bitcast.11), channel_id=1, replica_groups=mesh['pair'=4,'core'=2,'half'=2,'inner'=2] {'pair','inner'}, dimensions={0} | all-to-all | bytes 786432 | tf_op jit(solution)/shard_map/all_to_all | solution.py:357
  56.8 2.5 %collective-permute-start.4 = (f32[48,256]{1,0:T(8,128)S(1)}, f32[48,256]{1,0:T(8,128)S(1)}, u32[]{:S(2)}, u32[]{:S(2)}) collective-permute-start(f32[48,256]{1,0:T(8,128)S(1)} %row_sum.1.mine_ref), channel_id=1, source_target_pairs={{0,2},{2,0},{1,3},{3,1},{4,6},{6,4},{5,7},{7,5},{8,10},{10,8},{9,1... | collective-permute-start | bytes 147464 | tf_op jit(solution)/shard_map/ppermute | solution.py:377
  60.0 2.4 %collective-permute-done.4.other_ref = f32[48,256]{1,0:T(8,128)S(1)} collective-permute-done((f32[48,256]{1,0:T(8,128)S(1)}, f32[48,256]{1,0:T(8,128)S(1)}, u32[]{:S(2)}, u32[]{:S(2)}) %collective-permute-start.4) | collective-permute-done | bytes 49184 | tf_op jit(solution)/shard_map/ppermute | solution.py:377
  62.6 9.0 %all_to_all.16 = bf16[8,48,256]{2,1,0:T(8,128)(2,1)S(1)} all-to-all(bf16[8,48,256]{2,1,0:T(8,128)(2,1)S(1)} %row_softmax.1), channel_id=1, replica_groups=mesh['pair'=4,'core'=2,'half'=2,'inner'=2] {'pair','inner'}, dimensions={0} | all-to-all | bytes 393216 | tf_op jit(solution)/shard_map/all_to_all | solution.py:379
  73.0 2.7 %row_update.1 = (bf16[32,4,8,768]{3,2,1,0:T(8,128)(2,1)S(1)}, bf16[8,128,768]{2,1,0:T(8,128)(2,1)S(1)}) custom-call(s32[1]{0:T(128)} %bitcast.base_ref.low_ref, bf16[3,128,256]{2,1,0:T(8,128)(2,1)S(1)} %collective-permute-done.5.prob_ref, bf16[8,128,768]{2,1,0:T(8,128)(2,1)S(1)} %get-tuple-element.86.v_ref, ...), custom_call_target="tpu_custom_call", output_to_operand_aliasing={{1}: (5, {})} | custom-call | flops 1409286144 | bytes 8000000 | tf_op jit(solution)/shard_map/row_update/pallas_call | solution.py:392
  75.8 39.0 %all_to_all.17.mid_ref = bf16[32,4,8,768]{3,2,1,0:T(8,128)(2,1)S(1)} all-to-all(bf16[32,4,8,768]{3,2,1,0:T(8,128)(2,1)S(1)} %get-tuple-element.88), channel_id=1, replica_groups=mesh['pair'=4,'core'=2,'half'=2,'inner'=2] {'pair','core','half','inner'}, dimensions={0} | all-to-all | bytes 3145728 | tf_op jit(solution)/shard_map/all_to_all | solution.py:408
  114.8 4.8 %column_update.3 = (bf16[2,2,32,768]{3,2,1,0:T(8,128)(2,1)S(1)}, bf16[2,2,32,768]{3,2,1,0:T(8,128)(2,1)S(1)}, bf16[2,2,32,768]{3,2,1,0:T(8,128)(2,1)S(1)}, bf16[2,2,32,768]{3,2,1,0:T(8,128)(2,1)S(1)}) custom-call(s32[1]{0:T(128)} %bitcast.2.seq_ref, bf16[32,4,8,768]{3,2,1,0:T(8,128)(2,1)S(1)} %all_to_all.17.mid_ref, bf16[768,768]{1,0:T(8,128)(2,1)S(1)} %copy-done.6, ...), custom_call_target="tpu_custom_call" | custom-call | flops 3019898880 | bytes 8000000 | tf_op jit(solution)/shard_map/column_update/pallas_call | solution.py:416
  119.6 1.5 %collective-permute-start.10 = (bf16[2,2,32,768]{3,2,1,0:T(8,128)(2,1)S(1)}, bf16[2,2,32,768]{3,2,1,0:T(8,128)(2,1)S(1)}, u32[]{:S(2)}, u32[]{:S(2)}) collective-permute-start(bf16[2,2,32,768]{3,2,1,0:T(8,128)(2,1)S(1)} %get-tuple-element.94), channel_id=1, source_target_pairs={{0,8},{8,0},{16,24},{24,16},{1,9},{9,1},{17,25},{25,17},{2,10},{10... | collective-permute-start | bytes 589832 | tf_op jit(solution)/shard_map/ppermute | solution.py:298
  121.2 1.3 collective-permute-start.11
  123.2 4.8 %column_update.2 = (bf16[2,2,32,768]{3,2,1,0:T(8,128)(2,1)S(1)}, bf16[2,2,32,768]{3,2,1,0:T(8,128)(2,1)S(1)}, bf16[2,2,32,768]{3,2,1,0:T(8,128)(2,1)S(1)}, bf16[2,2,32,768]{3,2,1,0:T(8,128)(2,1)S(1)}) custom-call(s32[1]{0:T(128)} %bitcast.2.seq_ref, bf16[32,4,8,768]{3,2,1,0:T(8,128)(2,1)S(1)} %all_to_all.17.mid_ref, bf16[768,768]{1,0:T(8,128)(2,1)S(1)} %copy-done.6, ...), custom_call_target="tpu_custom_call" | custom-call | flops 3019898880 | bytes 8000000 | tf_op jit(solution)/shard_map/column_update/pallas_call | solution.py:416
  128.0 1.5 %collective-permute-start.6 = (bf16[2,2,32,768]{3,2,1,0:T(8,128)(2,1)S(1)}, bf16[2,2,32,768]{3,2,1,0:T(8,128)(2,1)S(1)}, u32[]{:S(2)}, u32[]{:S(2)}) collective-permute-start(bf16[2,2,32,768]{3,2,1,0:T(8,128)(2,1)S(1)} %get-tuple-element.90), channel_id=1, source_target_pairs={{0,8},{8,0},{16,24},{24,16},{1,9},{9,1},{17,25},{25,17},{2,10},{10... | collective-permute-start | bytes 589832 | tf_op jit(solution)/shard_map/ppermute | solution.py:298
  129.6 1.3 collective-permute-start.7
  131.6 1.5 %collective-permute-done.11.refs_2_ = bf16[2,2,32,768]{3,2,1,0:T(8,128)(2,1)S(1)} collective-permute-done((bf16[2,2,32,768]{3,2,1,0:T(8,128)(2,1)S(1)}, bf16[2,2,32,768]{3,2,1,0:T(8,128)(2,1)S(1)}, u32[]{:S(2)}, u32[]{:S(2)}) %collective-permute-start.11) | collective-permute-done | bytes 196640 | tf_op jit(solution)/shard_map/ppermute | solution.py:298
  133.3 2.6 %collective-permute-done.6.refs_1_ = bf16[2,2,32,768]{3,2,1,0:T(8,128)(2,1)S(1)} collective-permute-done((bf16[2,2,32,768]{3,2,1,0:T(8,128)(2,1)S(1)}, bf16[2,2,32,768]{3,2,1,0:T(8,128)(2,1)S(1)}, u32[]{:S(2)}, u32[]{:S(2)}) %collective-permute-start.6) | collective-permute-done | bytes 196640 | tf_op jit(solution)/shard_map/ppermute | solution.py:298
  135.9 5.6 %collective-permute-done.7.refs_2_ = bf16[2,2,32,768]{3,2,1,0:T(8,128)(2,1)S(1)} collective-permute-done((bf16[2,2,32,768]{3,2,1,0:T(8,128)(2,1)S(1)}, bf16[2,2,32,768]{3,2,1,0:T(8,128)(2,1)S(1)}, u32[]{:S(2)}, u32[]{:S(2)}) %collective-permute-start.7) | collective-permute-done | bytes 196640 | tf_op jit(solution)/shard_map/ppermute | solution.py:298
  (58 shorter events, 13.7 us)
Async XLA Ops:
  0.0 7.3 %copy-start = (bf16[768,768]{1,0:T(8,128)(2,1)S(1)}, bf16[768,768]{1,0:T(8,128)(2,1)}, u32[]{:S(2)}) copy-start(bf16[768,768]{1,0:T(8,128)(2,1)} %refs_0_.9) | copy-start | bytes 3538948
  2.2 15.3 %collective-permute-start.2 = (bf16[8,32,768]{2,1,0:T(8,128)(2,1)}, bf16[8,32,768]{2,1,0:T(8,128)(2,1)S(1)}, u32[]{:S(2)}, u32[]{:S(2)}) collective-permute-start(bf16[8,32,768]{2,1,0:T(8,128)(2,1)} %get-tuple-element.66), channel_id=1, source_target_pairs={{0,3},{1,2},{2,1},{3,0},{4,7},{5,6},{6,5},{7,4},{8,11},{9,10},{10,... | collective-permute-start | bytes 1179656 | tf_op jit(solution)/shard_map/ppermute | solution.py:295
  9.8 1.4 copy-start.4
  11.2 1.3 copy-start.11
  11.2 1.4 copy-start.10
  11.2 6.2 %copy-start.2 = (bf16[768,768]{1,0:T(8,128)(2,1)S(1)}, bf16[768,768]{1,0:T(8,128)(2,1)}, u32[]{:S(2)}) copy-start(bf16[768,768]{1,0:T(8,128)(2,1)} %refs_0_.8) | copy-start | bytes 3538948
  12.6 13.6 %collective-permute-start.1 = (bf16[8,32,768]{2,1,0:T(8,128)(2,1)S(1)}, bf16[8,32,768]{2,1,0:T(8,128)(2,1)S(1)}, u32[]{:S(2)}, u32[]{:S(2)}) collective-permute-start(bf16[8,32,768]{2,1,0:T(8,128)(2,1)S(1)} %copy-done.11), channel_id=1, source_target_pairs={{0,1},{1,0},{2,3},{3,2},{4,5},{5,4},{6,7},{7,6},{8,9},{9,8},{10,11... | collective-permute-start | bytes 1179656 | tf_op jit(solution)/shard_map/ppermute | solution.py:295
  12.7 28.4 %collective-permute-start = (bf16[8,32,768]{2,1,0:T(8,128)(2,1)S(1)}, bf16[8,32,768]{2,1,0:T(8,128)(2,1)S(1)}, u32[]{:S(2)}, u32[]{:S(2)}) collective-permute-start(bf16[8,32,768]{2,1,0:T(8,128)(2,1)S(1)} %copy-done.10), channel_id=1, source_target_pairs={{0,2},{1,3},{2,0},{3,1},{4,6},{5,7},{6,4},{7,5},{8,10},{9,11},{10,... | collective-permute-start | bytes 1179656 | tf_op jit(solution)/shard_map/ppermute | solution.py:295
  42.7 1.8 %collective-permute-start.3 = (f32[3,128,256]{2,1,0:T(8,128)S(1)}, f32[3,128,256]{2,1,0:T(8,128)S(1)}, u32[]{:S(2)}, u32[]{:S(2)}) collective-permute-start(f32[3,128,256]{2,1,0:T(8,128)S(1)} %row_scores.3), channel_id=1, source_target_pairs={{0,4},{4,0},{1,5},{5,1},{2,6},{6,2},{3,7},{7,3},{8,12},{12,8},{9,1... | collective-permute-start | bytes 1179656 | tf_op jit(solution)/shard_map/ppermute | solution.py:353
  56.8 5.6 %collective-permute-start.4 = (f32[48,256]{1,0:T(8,128)S(1)}, f32[48,256]{1,0:T(8,128)S(1)}, u32[]{:S(2)}, u32[]{:S(2)}) collective-permute-start(f32[48,256]{1,0:T(8,128)S(1)} %row_sum.1.mine_ref), channel_id=1, source_target_pairs={{0,2},{2,0},{1,3},{3,1},{4,6},{6,4},{5,7},{7,5},{8,10},{10,8},{9,1... | collective-permute-start | bytes 147464 | tf_op jit(solution)/shard_map/ppermute | solution.py:377
  71.6 1.4 copy-start.5
  71.6 1.4 collective-permute-start.5
  73.0 41.7 %copy-start.8 = (bf16[768,768]{1,0:T(8,128)(2,1)S(1)}, bf16[768,768]{1,0:T(8,128)(2,1)}, u32[]{:S(2)}) copy-start(bf16[768,768]{1,0:T(8,128)(2,1)} %wv_ref.3) | copy-start | bytes 3538948
  73.0 41.7 %copy-start.9 = (bf16[768,768]{1,0:T(8,128)(2,1)S(1)}, bf16[768,768]{1,0:T(8,128)(2,1)}, u32[]{:S(2)}) copy-start(bf16[768,768]{1,0:T(8,128)(2,1)} %wo_ref.5) | copy-start | bytes 3538948
  75.8 39.0 %copy-start.6 = (bf16[768,768]{1,0:T(8,128)(2,1)S(1)}, bf16[768,768]{1,0:T(8,128)(2,1)}, u32[]{:S(2)}) copy-start(bf16[768,768]{1,0:T(8,128)(2,1)} %wq_ref.3) | copy-start | bytes 3538948
  75.8 39.0 %copy-start.7 = (bf16[768,768]{1,0:T(8,128)(2,1)S(1)}, bf16[768,768]{1,0:T(8,128)(2,1)}, u32[]{:S(2)}) copy-start(bf16[768,768]{1,0:T(8,128)(2,1)} %wk_ref.3) | copy-start | bytes 3538948
  119.6 11.2 %collective-permute-start.10 = (bf16[2,2,32,768]{3,2,1,0:T(8,128)(2,1)S(1)}, bf16[2,2,32,768]{3,2,1,0:T(8,128)(2,1)S(1)}, u32[]{:S(2)}, u32[]{:S(2)}) collective-permute-start(bf16[2,2,32,768]{3,2,1,0:T(8,128)(2,1)S(1)} %get-tuple-element.94), channel_id=1, source_target_pairs={{0,8},{8,0},{16,24},{24,16},{1,9},{9,1},{17,25},{25,17},{2,10},{10... | collective-permute-start | bytes 589832 | tf_op jit(solution)/shard_map/ppermute | solution.py:298
  121.2 12.0 %collective-permute-start.11 = (bf16[2,2,32,768]{3,2,1,0:T(8,128)(2,1)S(1)}, bf16[2,2,32,768]{3,2,1,0:T(8,128)(2,1)S(1)}, u32[]{:S(2)}, u32[]{:S(2)}) collective-permute-start(bf16[2,2,32,768]{3,2,1,0:T(8,128)(2,1)S(1)} %get-tuple-element.95), channel_id=1, source_target_pairs={{0,16},{8,24},{16,0},{24,8},{1,17},{9,25},{17,1},{25,9},{2,18},{10... | collective-permute-start | bytes 589832 | tf_op jit(solution)/shard_map/ppermute | solution.py:298
  122.5 10.7 %collective-permute-start.12 = (bf16[2,2,32,768]{3,2,1,0:T(8,128)(2,1)S(1)}, bf16[2,2,32,768]{3,2,1,0:T(8,128)(2,1)S(1)}, u32[]{:S(2)}, u32[]{:S(2)}) collective-permute-start(bf16[2,2,32,768]{3,2,1,0:T(8,128)(2,1)S(1)} %get-tuple-element.96), channel_id=1, source_target_pairs={{0,24},{8,16},{16,8},{24,0},{1,25},{9,17},{17,9},{25,1},{2,26},{10... | collective-permute-start | bytes 589832 | tf_op jit(solution)/shard_map/ppermute | solution.py:298
  128.0 7.9 %collective-permute-start.6 = (bf16[2,2,32,768]{3,2,1,0:T(8,128)(2,1)S(1)}, bf16[2,2,32,768]{3,2,1,0:T(8,128)(2,1)S(1)}, u32[]{:S(2)}, u32[]{:S(2)}) collective-permute-start(bf16[2,2,32,768]{3,2,1,0:T(8,128)(2,1)S(1)} %get-tuple-element.90), channel_id=1, source_target_pairs={{0,8},{8,0},{16,24},{24,16},{1,9},{9,1},{17,25},{25,17},{2,10},{10... | collective-permute-start | bytes 589832 | tf_op jit(solution)/shard_map/ppermute | solution.py:298
  129.6 12.0 %collective-permute-start.7 = (bf16[2,2,32,768]{3,2,1,0:T(8,128)(2,1)S(1)}, bf16[2,2,32,768]{3,2,1,0:T(8,128)(2,1)S(1)}, u32[]{:S(2)}, u32[]{:S(2)}) collective-permute-start(bf16[2,2,32,768]{3,2,1,0:T(8,128)(2,1)S(1)} %get-tuple-element.91), channel_id=1, source_target_pairs={{0,16},{8,24},{16,0},{24,8},{1,17},{9,25},{17,1},{25,9},{2,18},{10... | collective-permute-start | bytes 589832 | tf_op jit(solution)/shard_map/ppermute | solution.py:298
  130.8 10.7 %collective-permute-start.8 = (bf16[2,2,32,768]{3,2,1,0:T(8,128)(2,1)S(1)}, bf16[2,2,32,768]{3,2,1,0:T(8,128)(2,1)S(1)}, u32[]{:S(2)}, u32[]{:S(2)}) collective-permute-start(bf16[2,2,32,768]{3,2,1,0:T(8,128)(2,1)S(1)} %get-tuple-element.92), channel_id=1, source_target_pairs={{0,24},{8,16},{16,8},{24,0},{1,25},{9,17},{17,9},{25,1},{2,26},{10... | collective-permute-start | bytes 589832 | tf_op jit(solution)/shard_map/ppermute | solution.py:298
  133.3 8.5 %collective-permute-start.13 = (bf16[4,2,32,768]{3,2,1,0:T(8,128)(2,1)S(1)}, bf16[4,2,32,768]{3,2,1,0:T(8,128)(2,1)S(1)}, u32[]{:S(2)}, u32[]{:S(2)}) collective-permute-start(bf16[4,2,32,768]{3,2,1,0:T(8,128)(2,1)S(1)} %pad_maximum_fusion.1), channel_id=1, source_target_pairs={{0,4},{4,0},{1,5},{5,1},{2,6},{6,2},{3,7},{7,3},{8,12},{12,8},{9,1... | collective-permute-start | bytes 1179656 | tf_op jit(solution)/shard_map/ppermute | solution.py:430
  141.6 1.8 %collective-permute-start.9 = (bf16[4,2,32,768]{3,2,1,0:T(8,128)(2,1)S(1)}, bf16[4,2,32,768]{3,2,1,0:T(8,128)(2,1)S(1)}, u32[]{:S(2)}, u32[]{:S(2)}) collective-permute-start(bf16[4,2,32,768]{3,2,1,0:T(8,128)(2,1)S(1)} %pad_maximum_fusion), channel_id=1, source_target_pairs={{0,4},{4,0},{1,5},{5,1},{2,6},{6,2},{3,7},{7,3},{8,12},{12,8},{9,1... | collective-permute-start | bytes 1179656 | tf_op jit(solution)/shard_map/ppermute | solution.py:430
  (2 other events, 2.5 us)

commit v7 on v6

--- a/solution.py
+++ b/solution.py
@@ -126,12 +126,24 @@
         prob_ref[at] = prob
 
 
-def row_attend(low_ref, prob_ref, v_ref, o_ref):
+def moved_order(rows, parts, piece, inner):
+    def source(token):
+        rest, row = parted(token, rows)
+        rest, step = parted(rest, inner)
+        owner, part = parted(rest, parts)
+        return (row * parts + part) * piece + owner * inner + step
+
+    return permutation(rows * parts * piece, source)
+
+
+def row_attend(seq_size, parts, low_ref, prob_ref, v_ref, o_ref, held_ref):
     rows, _, width = v_ref.shape
     pair = 2 * (width // HEADS)
+    count = prob_ref.shape[0]
     masks = head_masks(pair, pair // 2)
-    for at in range(prob_ref.shape[0]):
+    for at in range(count):
         lanes = pl.ds(pl.multiple_of((low_ref[0] + at) * pair, pair), pair)
+        own = slice(at * pair, (at + 1) * pair)
         prob = prob_ref[at]
         for row in range(0, rows, 2):
             fields = [v_ref[row + step, :, lanes] for step in range(2)]
@@ -140,34 +152,33 @@
                 axis=0,
             )
             result = dot(prob, values).astype(BF16)
-            o_ref[row, :, lanes] = result[:, :pair]
-            o_ref[row + 1, :, lanes] = result[:, pair:]
-
-
-def row_update(seq_size, parts, chunks, low_ref, prob_ref, v_ref, x_ref, wo_ref, *refs):
-    mid_ref, o_ref = refs[-2:]
-    row_attend(low_ref, prob_ref, v_ref, o_ref)
-    rows, cols, width = o_ref.shape
-    at = 0
-    step_at = 0
-    for piece in chunks:
-        tokens = rows * parts * piece
-        inner = piece // seq_size
-
-        def source(token):
-            rest, row = parted(token, rows)
-            rest, step = parted(rest, inner)
-            owner, part = parted(rest, parts)
-            return (row * parts + part) * piece + owner * inner + step
-
-        attended = o_ref[:, at * parts : (at + piece) * parts, :].reshape(tokens, width)
-        residual = x_ref[...].astype(F32).reshape(rows, parts, cols // parts, width)
-        residual = residual[:, :, at : at + piece].reshape(tokens, width)
-        mid = residual + dot(attended, wo_ref[...])
-        moved = dot(permutation(tokens, source), mid.astype(BF16)).astype(BF16)
-        mid_ref[:, step_at : step_at + inner] = moved.reshape(-1, inner, rows, width)
-        at += piece
-        step_at += inner
+            held_ref[row, :, own] = result[:, :pair]
+            held_ref[row + 1, :, own] = result[:, pair:]
+    lanes = pl.ds(pl.multiple_of(low_ref[0] * pair, pair), count * pair)
+    order = moved_order(rows, parts, SLOT, SLOT // seq_size)
+    tokens = o_ref.shape[1]
+    for chunk in range(o_ref.shape[0]):
+        field = held_ref[:, chunk * SLOT * parts : (chunk + 1) * SLOT * parts, :]
+        o_ref[chunk, :, lanes] = dot(order, field.reshape(tokens, count * pair)).astype(BF16)
+
+
+def row_keep(seq_size, parts, x_ref, kept_ref):
+    rows, cols, width = x_ref.shape
+    order = moved_order(rows, parts, SLOT, SLOT // seq_size)
+    for chunk in range(kept_ref.shape[0]):
+        field = x_ref[...].reshape(rows, parts, cols // parts, width)
+        field = field[:, :, chunk * SLOT : (chunk + 1) * SLOT].reshape(-1, width)
+        kept_ref[chunk] = dot(order, field).astype(BF16)
+
+
+def row_update(seq_size, parts, low_ref, prob_ref, v_ref, kept_ref, wo_ref, _, mid_ref, o_ref, held_ref):
+    row_attend(seq_size, parts, low_ref, prob_ref, v_ref, o_ref, held_ref)
+    _, _, rows, width = mid_ref.shape
+    inner = SLOT // seq_size
+    for chunk in range(o_ref.shape[0]):
+        mid = kept_ref[chunk].astype(F32) + dot(o_ref[chunk], wo_ref[...])
+        own = slice(chunk * inner, (chunk + 1) * inner)
+        mid_ref[:, own] = mid.astype(BF16).reshape(-1, inner, rows, width)
 
 
 def column_update(first_at, seq_ref, mid_ref, wq_ref, wk_ref, wv_ref, wo_ref, *refs):
@@ -367,6 +378,16 @@
     )(partial)
     partial, fields = lax.optimization_barrier((partial, fields[2:]))
     v, x = projected(last, [row_value], fields, 1)
+    moved_shape = (len(chunks), own_rows * res_size * SLOT, width)
+    kept = pl.pallas_call(
+        functools.partial(row_keep, seq_size, res_size),
+        in_specs=[vmem],
+        out_specs=vmem,
+        out_shape=jax.ShapeDtypeStruct(moved_shape, BF16),
+        compiler_params=params(),
+        cost_estimate=cost(2 * own_rows * cols * width * 512, 3e6),
+        name="row_keep",
+    )(x)
     prob = pl.pallas_call(
         functools.partial(row_softmax, head_dim ** (-0.5) / math.sqrt(all_rows)),
         in_specs=[vmem, vmem],
@@ -375,35 +396,38 @@
         compiler_params=params(),
         name="row_softmax",
     )(partial, lax.ppermute(partial, "half", swap))
-    prob, v = lax.optimization_barrier((prob, v))
+    prob, v, kept = lax.optimization_barrier((prob, v, kept))
     prob = lax.all_to_all(prob, ("pair", "inner"), split_axis=0, concat_axis=0, tiled=True)
     prob = prob.reshape(half_pairs, cols, 2 * cols)
     prob_other = lax.ppermute(prob, "core", swap)
 
+    held = pltpu.VMEM((own_rows, cols, width // CORES), BF16)
     attended = pl.pallas_call(
-        row_attend,
+        functools.partial(row_attend, seq_size, res_size),
         in_specs=[smem, vmem, vmem],
         out_specs=vmem,
-        out_shape=jax.ShapeDtypeStruct((own_rows, cols, width), BF16),
+        out_shape=jax.ShapeDtypeStruct(moved_shape, BF16),
+        scratch_shapes=[held],
         compiler_params=params(),
         cost_estimate=cost(2 * own_rows * cols * cols * width, 3e6),
         name="row_attend",
     )(halves[1], prob, v)
     mid, _ = pl.pallas_call(
-        functools.partial(row_update, seq_size, res_size, chunks),
+        functools.partial(row_update, seq_size, res_size),
         in_specs=[smem] + [vmem] * 5,
         out_specs=[vmem, vmem],
         out_shape=[
             jax.ShapeDtypeStruct(
                 (seq_size * res_size, block // seq_size, own_rows, width), BF16
             ),
-            jax.ShapeDtypeStruct((own_rows, cols, width), BF16),
+            jax.ShapeDtypeStruct(moved_shape, BF16),
         ],
+        scratch_shapes=[held],
         input_output_aliases={5: 1},
         compiler_params=params(),
         cost_estimate=cost(2 * own_rows * cols * width * (width + cols), 8e6),
         name="row_update",
-    )(halves[0], prob_other, v, x, row_out, attended)
+    )(halves[0], prob_other, v, kept, row_out, attended)
 
     moved = lax.all_to_all(
         mid, ("pair", "core", "half", "inner"), split_axis=0, concat_axis=0, tiled=True

time: 145 us -> 145 us (level)
  waiting for transfers between devices: 39.8 us -> 38.1 us
    pallas_call x2 -> x3, Pallas kernels: 3.15 us -> 4.51 us  [the longest x1 2.44 us: on_device(): pl.pallas_call(functools.partial(row_update, seq_size, res_size), in_spec...]
  transfers between devices with their start and end apart: 14 -> 14, of which waited for: 10 -> 10; matrix products, arithmetic and copies ran while one was open for 0% -> 0% of each run, Pallas kernels for 8% -> 9%
where the time goes in v7:
time: 145 us; the launch traced here: 144 us
  blocking collectives  60.2 us (42%)
  waiting for transfers between devices  38.1 us (26%)
  Pallas kernels  25.9 us (18%)
  starting transfers between devices  15.6 us (11%)
  local copies, waits for them, and re-layouts  4.05 us (3%)
    all_to_all x1, blocking collectives, on_device(): lax.all_to_all(mid, ('pair', 'core', 'half', 'inner'), split_axis=0, conc...  39 us
    ppermute x3, waiting for transfers between devices, across(): lax.ppermute(field, ('half', 'inner'), [(at, at ^ step) for at in range(r...  25.2 us
    all_to_all x1, blocking collectives, on_device(): lax.all_to_all((mine + other).reshape(share), ('pair', 'inner'), split_ax...  12.2 us
    ppermute x6, waiting for transfers between devices, around(): lax.ppermute(field, 'pair', [(at, at ^ step) for at in range(pairs_size)])  9.72 us
    pallas_call x2, Pallas kernels, on_device(): pl.pallas_call(functools.partial(column_update, first_at), in_specs=[smem...  9.65 us
    all_to_all x1, blocking collectives, on_device(): lax.all_to_all(prob, ('pair', 'inner'), split_axis=0, concat_axis=0, tile...  9.02 us
    ppermute x6, starting transfers between devices, around(): lax.ppermute(field, 'pair', [(at, at ^ step) for at in range(pairs_size)])  7.11 us
    ppermute x3, starting transfers between devices, across(): lax.ppermute(field, ('half', 'inner'), [(at, at ^ step) for at in range(r...  5.76 us
  transfers between devices with their start and end apart: 14, of which 10 were waited for; matrix products, arithmetic and copies ran while one was open for 0% of the time, Pallas kernels for 9%

profile of v7, /device:TPU:0, one launch (start us, length us, event | category | flops | bytes accessed | tf_op | source)
XLA Modules:
  0.0 144.4 jit_solution(15438730604789276008)
XLA Ops:
  0.0 2.2 %row_shares.1 = (bf16[8,32,768]{2,1,0:T(8,128)(2,1)}, bf16[8,32,768]{2,1,0:T(8,128)(2,1)}, bf16[8,32,768]{2,1,0:T(8,128)(2,1)}) custom-call(s32[1]{0:T(128)} %bitcast.3.part_ref.at_ref, bf16[32,32,768]{2,1,0:T(8,128)(2,1)} %x_ref), custom_call_target="tpu_custom_call" | custom-call | tf_op jit(solution)/shard_map/row_shares/pallas_call | solution.py:311
  2.2 5.1 %collective-permute-start.2 = (bf16[8,32,768]{2,1,0:T(8,128)(2,1)}, bf16[8,32,768]{2,1,0:T(8,128)(2,1)S(1)}, u32[]{:S(2)}, u32[]{:S(2)}) collective-permute-start(bf16[8,32,768]{2,1,0:T(8,128)(2,1)} %get-tuple-element.67), channel_id=1, source_target_pairs={{0,3},{1,2},{2,1},{3,0},{4,7},{5,6},{6,5},{7,4},{8,11},{9,10},{10,... | collective-permute-start | bytes 1179656 | tf_op jit(solution)/shard_map/ppermute | solution.py:306
  9.8 1.4 copy-done.4
  11.2 1.3 row_project.5
  13.2 4.3 %collective-permute-done.2.x_ref = bf16[8,32,768]{2,1,0:T(8,128)(2,1)S(1)} collective-permute-done((bf16[8,32,768]{2,1,0:T(8,128)(2,1)}, bf16[8,32,768]{2,1,0:T(8,128)(2,1)S(1)}, u32[]{:S(2)}, u32[]{:S(2)}) %collective-permute-start.2) | collective-permute-done | bytes 393248 | tf_op jit(solution)/shard_map/ppermute | solution.py:306
  17.5 1.3 row_project.6
  18.8 7.3 %collective-permute-done.1.x_ref = bf16[8,32,768]{2,1,0:T(8,128)(2,1)S(1)} collective-permute-done((bf16[8,32,768]{2,1,0:T(8,128)(2,1)S(1)}, bf16[8,32,768]{2,1,0:T(8,128)(2,1)S(1)}, u32[]{:S(2)}, u32[]{:S(2)}) %collective-permute-start.1) | collective-permute-done | bytes 393248 | tf_op jit(solution)/shard_map/ppermute | solution.py:306
  26.1 1.3 row_project.7
  27.4 13.6 %collective-permute-done.x_ref = bf16[8,32,768]{2,1,0:T(8,128)(2,1)S(1)} collective-permute-done((bf16[8,32,768]{2,1,0:T(8,128)(2,1)S(1)}, bf16[8,32,768]{2,1,0:T(8,128)(2,1)S(1)}, u32[]{:S(2)}, u32[]{:S(2)}) %collective-permute-start) | collective-permute-done | bytes 393248 | tf_op jit(solution)/shard_map/ppermute | solution.py:306
  44.6 12.2 %all_to_all.15.parts_ref = f32[8,48,256]{2,1,0:T(8,128)S(1)} all-to-all(f32[8,48,256]{2,1,0:T(8,128)S(1)} %bitcast.11), channel_id=1, replica_groups=mesh['pair'=4,'core'=2,'half'=2,'inner'=2] {'pair','inner'}, dimensions={0} | all-to-all | bytes 786432 | tf_op jit(solution)/shard_map/all_to_all | solution.py:368
  56.8 2.5 %collective-permute-start.4 = (f32[48,256]{1,0:T(8,128)S(1)}, f32[48,256]{1,0:T(8,128)S(1)}, u32[]{:S(2)}, u32[]{:S(2)}) collective-permute-start(f32[48,256]{1,0:T(8,128)S(1)} %row_sum.1.mine_ref), channel_id=1, source_target_pairs={{0,2},{2,0},{1,3},{3,1},{4,6},{6,4},{5,7},{7,5},{8,10},{10,8},{9,1... | collective-permute-start | bytes 147464 | tf_op jit(solution)/shard_map/ppermute | solution.py:398
  61.0 1.4 collective-permute-done.4.other_ref
  62.6 9.0 %all_to_all.16 = bf16[8,48,256]{2,1,0:T(8,128)(2,1)S(1)} all-to-all(bf16[8,48,256]{2,1,0:T(8,128)(2,1)S(1)} %row_softmax.1), channel_id=1, replica_groups=mesh['pair'=4,'core'=2,'half'=2,'inner'=2] {'pair','inner'}, dimensions={0} | all-to-all | bytes 393216 | tf_op jit(solution)/shard_map/all_to_all | solution.py:400
  73.0 2.4 %row_update.1 = (bf16[32,4,8,768]{3,2,1,0:T(8,128)(2,1)S(1)}, bf16[2,512,768]{2,1,0:T(8,128)(2,1)S(1)}) custom-call(s32[1]{0:T(128)} %bitcast.base_ref.low_ref, bf16[3,128,256]{2,1,0:T(8,128)(2,1)S(1)} %collective-permute-done.5.prob_ref, bf16[8,128,768]{2,1,0:T(8,128)(2,1)S(1)} %get-tuple-element.88.v_ref, ...), custom_call_target="tpu_custom_call", output_to_operand_aliasing={{1}: (5, {})} | custom-call | flops 1409286144 | bytes 8000000 | tf_op jit(solution)/shard_map/row_update/pallas_call | solution.py:415
  75.5 39.0 %all_to_all.17.mid_ref = bf16[32,4,8,768]{3,2,1,0:T(8,128)(2,1)S(1)} all-to-all(bf16[32,4,8,768]{3,2,1,0:T(8,128)(2,1)S(1)} %get-tuple-element.90), channel_id=1, replica_groups=mesh['pair'=4,'core'=2,'half'=2,'inner'=2] {'pair','core','half','inner'}, dimensions={0} | all-to-all | bytes 3145728 | tf_op jit(solution)/shard_map/all_to_all | solution.py:432
  114.5 4.8 %column_update.3 = (bf16[2,2,32,768]{3,2,1,0:T(8,128)(2,1)S(1)}, bf16[2,2,32,768]{3,2,1,0:T(8,128)(2,1)S(1)}, bf16[2,2,32,768]{3,2,1,0:T(8,128)(2,1)S(1)}, bf16[2,2,32,768]{3,2,1,0:T(8,128)(2,1)S(1)}) custom-call(s32[1]{0:T(128)} %bitcast.2.seq_ref, bf16[32,4,8,768]{3,2,1,0:T(8,128)(2,1)S(1)} %all_to_all.17.mid_ref, bf16[768,768]{1,0:T(8,128)(2,1)S(1)} %copy-done.6, ...), custom_call_target="tpu_custom_call" | custom-call | flops 3019898880 | bytes 8000000 | tf_op jit(solution)/shard_map/column_update/pallas_call | solution.py:440
  119.3 1.5 %collective-permute-start.10 = (bf16[2,2,32,768]{3,2,1,0:T(8,128)(2,1)S(1)}, bf16[2,2,32,768]{3,2,1,0:T(8,128)(2,1)S(1)}, u32[]{:S(2)}, u32[]{:S(2)}) collective-permute-start(bf16[2,2,32,768]{3,2,1,0:T(8,128)(2,1)S(1)} %get-tuple-element.96), channel_id=1, source_target_pairs={{0,8},{8,0},{16,24},{24,16},{1,9},{9,1},{17,25},{25,17},{2,10},{10... | collective-permute-start | bytes 589832 | tf_op jit(solution)/shard_map/ppermute | solution.py:309
  120.9 1.3 collective-permute-start.11
  122.9 4.8 %column_update.2 = (bf16[2,2,32,768]{3,2,1,0:T(8,128)(2,1)S(1)}, bf16[2,2,32,768]{3,2,1,0:T(8,128)(2,1)S(1)}, bf16[2,2,32,768]{3,2,1,0:T(8,128)(2,1)S(1)}, bf16[2,2,32,768]{3,2,1,0:T(8,128)(2,1)S(1)}) custom-call(s32[1]{0:T(128)} %bitcast.2.seq_ref, bf16[32,4,8,768]{3,2,1,0:T(8,128)(2,1)S(1)} %all_to_all.17.mid_ref, bf16[768,768]{1,0:T(8,128)(2,1)S(1)} %copy-done.6, ...), custom_call_target="tpu_custom_call" | custom-call | flops 3019898880 | bytes 8000000 | tf_op jit(solution)/shard_map/column_update/pallas_call | solution.py:440
  127.7 1.5 %collective-permute-start.6 = (bf16[2,2,32,768]{3,2,1,0:T(8,128)(2,1)S(1)}, bf16[2,2,32,768]{3,2,1,0:T(8,128)(2,1)S(1)}, u32[]{:S(2)}, u32[]{:S(2)}) collective-permute-start(bf16[2,2,32,768]{3,2,1,0:T(8,128)(2,1)S(1)} %get-tuple-element.92), channel_id=1, source_target_pairs={{0,8},{8,0},{16,24},{24,16},{1,9},{9,1},{17,25},{25,17},{2,10},{10... | collective-permute-start | bytes 589832 | tf_op jit(solution)/shard_map/ppermute | solution.py:309
  129.3 1.3 collective-permute-start.7
  131.3 1.5 %collective-permute-done.11.refs_2_ = bf16[2,2,32,768]{3,2,1,0:T(8,128)(2,1)S(1)} collective-permute-done((bf16[2,2,32,768]{3,2,1,0:T(8,128)(2,1)S(1)}, bf16[2,2,32,768]{3,2,1,0:T(8,128)(2,1)S(1)}, u32[]{:S(2)}, u32[]{:S(2)}) %collective-permute-start.11) | collective-permute-done | bytes 196640 | tf_op jit(solution)/shard_map/ppermute | solution.py:309
  133.0 2.6 %collective-permute-done.6.refs_1_ = bf16[2,2,32,768]{3,2,1,0:T(8,128)(2,1)S(1)} collective-permute-done((bf16[2,2,32,768]{3,2,1,0:T(8,128)(2,1)S(1)}, bf16[2,2,32,768]{3,2,1,0:T(8,128)(2,1)S(1)}, u32[]{:S(2)}, u32[]{:S(2)}) %collective-permute-start.6) | collective-permute-done | bytes 196640 | tf_op jit(solution)/shard_map/ppermute | solution.py:309
  135.6 5.6 %collective-permute-done.7.refs_2_ = bf16[2,2,32,768]{3,2,1,0:T(8,128)(2,1)S(1)} collective-permute-done((bf16[2,2,32,768]{3,2,1,0:T(8,128)(2,1)S(1)}, bf16[2,2,32,768]{3,2,1,0:T(8,128)(2,1)S(1)}, u32[]{:S(2)}, u32[]{:S(2)}) %collective-permute-start.7) | collective-permute-done | bytes 196640 | tf_op jit(solution)/shard_map/ppermute | solution.py:309
  (59 shorter events, 14.7 us)
Async XLA Ops:
  0.0 7.3 %copy-start = (bf16[768,768]{1,0:T(8,128)(2,1)S(1)}, bf16[768,768]{1,0:T(8,128)(2,1)}, u32[]{:S(2)}) copy-start(bf16[768,768]{1,0:T(8,128)(2,1)} %refs_0_.9) | copy-start | bytes 3538948
  2.2 15.3 %collective-permute-start.2 = (bf16[8,32,768]{2,1,0:T(8,128)(2,1)}, bf16[8,32,768]{2,1,0:T(8,128)(2,1)S(1)}, u32[]{:S(2)}, u32[]{:S(2)}) collective-permute-start(bf16[8,32,768]{2,1,0:T(8,128)(2,1)} %get-tuple-element.67), channel_id=1, source_target_pairs={{0,3},{1,2},{2,1},{3,0},{4,7},{5,6},{6,5},{7,4},{8,11},{9,10},{10,... | collective-permute-start | bytes 1179656 | tf_op jit(solution)/shard_map/ppermute | solution.py:306
  9.8 1.4 copy-start.4
  11.2 1.3 copy-start.11
  11.2 1.4 copy-start.10
  11.2 6.2 %copy-start.2 = (bf16[768,768]{1,0:T(8,128)(2,1)S(1)}, bf16[768,768]{1,0:T(8,128)(2,1)}, u32[]{:S(2)}) copy-start(bf16[768,768]{1,0:T(8,128)(2,1)} %refs_0_.8) | copy-start | bytes 3538948
  12.6 13.6 %collective-permute-start.1 = (bf16[8,32,768]{2,1,0:T(8,128)(2,1)S(1)}, bf16[8,32,768]{2,1,0:T(8,128)(2,1)S(1)}, u32[]{:S(2)}, u32[]{:S(2)}) collective-permute-start(bf16[8,32,768]{2,1,0:T(8,128)(2,1)S(1)} %copy-done.11), channel_id=1, source_target_pairs={{0,1},{1,0},{2,3},{3,2},{4,5},{5,4},{6,7},{7,6},{8,9},{9,8},{10,11... | collective-permute-start | bytes 1179656 | tf_op jit(solution)/shard_map/ppermute | solution.py:306
  12.7 28.4 %collective-permute-start = (bf16[8,32,768]{2,1,0:T(8,128)(2,1)S(1)}, bf16[8,32,768]{2,1,0:T(8,128)(2,1)S(1)}, u32[]{:S(2)}, u32[]{:S(2)}) collective-permute-start(bf16[8,32,768]{2,1,0:T(8,128)(2,1)S(1)} %copy-done.10), channel_id=1, source_target_pairs={{0,2},{1,3},{2,0},{3,1},{4,6},{5,7},{6,4},{7,5},{8,10},{9,11},{10,... | collective-permute-start | bytes 1179656 | tf_op jit(solution)/shard_map/ppermute | solution.py:306
  42.7 1.8 %collective-permute-start.3 = (f32[3,128,256]{2,1,0:T(8,128)S(1)}, f32[3,128,256]{2,1,0:T(8,128)S(1)}, u32[]{:S(2)}, u32[]{:S(2)}) collective-permute-start(f32[3,128,256]{2,1,0:T(8,128)S(1)} %row_scores.3), channel_id=1, source_target_pairs={{0,4},{4,0},{1,5},{5,1},{2,6},{6,2},{3,7},{7,3},{8,12},{12,8},{9,1... | collective-permute-start | bytes 1179656 | tf_op jit(solution)/shard_map/ppermute | solution.py:364
  56.8 5.6 %collective-permute-start.4 = (f32[48,256]{1,0:T(8,128)S(1)}, f32[48,256]{1,0:T(8,128)S(1)}, u32[]{:S(2)}, u32[]{:S(2)}) collective-permute-start(f32[48,256]{1,0:T(8,128)S(1)} %row_sum.1.mine_ref), channel_id=1, source_target_pairs={{0,2},{2,0},{1,3},{3,1},{4,6},{6,4},{5,7},{7,5},{8,10},{10,8},{9,1... | collective-permute-start | bytes 147464 | tf_op jit(solution)/shard_map/ppermute | solution.py:398
  71.6 1.4 %copy-start.5 = (bf16[768,768]{1,0:T(8,128)(2,1)S(1)}, bf16[768,768]{1,0:T(8,128)(2,1)}, u32[]{:S(2)}) copy-start(bf16[768,768]{1,0:T(8,128)(2,1)} %wo_ref.3) | copy-start | bytes 3538948
  71.6 1.4 collective-permute-start.5
  73.0 41.4 %copy-start.8 = (bf16[768,768]{1,0:T(8,128)(2,1)S(1)}, bf16[768,768]{1,0:T(8,128)(2,1)}, u32[]{:S(2)}) copy-start(bf16[768,768]{1,0:T(8,128)(2,1)} %wv_ref.3) | copy-start | bytes 3538948
  73.0 41.4 %copy-start.9 = (bf16[768,768]{1,0:T(8,128)(2,1)S(1)}, bf16[768,768]{1,0:T(8,128)(2,1)}, u32[]{:S(2)}) copy-start(bf16[768,768]{1,0:T(8,128)(2,1)} %wo_ref.5) | copy-start | bytes 3538948
  75.5 39.0 %copy-start.6 = (bf16[768,768]{1,0:T(8,128)(2,1)S(1)}, bf16[768,768]{1,0:T(8,128)(2,1)}, u32[]{:S(2)}) copy-start(bf16[768,768]{1,0:T(8,128)(2,1)} %wq_ref.3) | copy-start | bytes 3538948
  75.5 39.0 %copy-start.7 = (bf16[768,768]{1,0:T(8,128)(2,1)S(1)}, bf16[768,768]{1,0:T(8,128)(2,1)}, u32[]{:S(2)}) copy-start(bf16[768,768]{1,0:T(8,128)(2,1)} %wk_ref.3) | copy-start | bytes 3538948
  119.3 11.2 %collective-permute-start.10 = (bf16[2,2,32,768]{3,2,1,0:T(8,128)(2,1)S(1)}, bf16[2,2,32,768]{3,2,1,0:T(8,128)(2,1)S(1)}, u32[]{:S(2)}, u32[]{:S(2)}) collective-permute-start(bf16[2,2,32,768]{3,2,1,0:T(8,128)(2,1)S(1)} %get-tuple-element.96), channel_id=1, source_target_pairs={{0,8},{8,0},{16,24},{24,16},{1,9},{9,1},{17,25},{25,17},{2,10},{10... | collective-permute-start | bytes 589832 | tf_op jit(solution)/shard_map/ppermute | solution.py:309
  120.9 12.0 %collective-permute-start.11 = (bf16[2,2,32,768]{3,2,1,0:T(8,128)(2,1)S(1)}, bf16[2,2,32,768]{3,2,1,0:T(8,128)(2,1)S(1)}, u32[]{:S(2)}, u32[]{:S(2)}) collective-permute-start(bf16[2,2,32,768]{3,2,1,0:T(8,128)(2,1)S(1)} %get-tuple-element.97), channel_id=1, source_target_pairs={{0,16},{8,24},{16,0},{24,8},{1,17},{9,25},{17,1},{25,9},{2,18},{10... | collective-permute-start | bytes 589832 | tf_op jit(solution)/shard_map/ppermute | solution.py:309
  122.1 10.7 %collective-permute-start.12 = (bf16[2,2,32,768]{3,2,1,0:T(8,128)(2,1)S(1)}, bf16[2,2,32,768]{3,2,1,0:T(8,128)(2,1)S(1)}, u32[]{:S(2)}, u32[]{:S(2)}) collective-permute-start(bf16[2,2,32,768]{3,2,1,0:T(8,128)(2,1)S(1)} %get-tuple-element.98), channel_id=1, source_target_pairs={{0,24},{8,16},{16,8},{24,0},{1,25},{9,17},{17,9},{25,1},{2,26},{10... | collective-permute-start | bytes 589832 | tf_op jit(solution)/shard_map/ppermute | solution.py:309
  127.7 7.9 %collective-permute-start.6 = (bf16[2,2,32,768]{3,2,1,0:T(8,128)(2,1)S(1)}, bf16[2,2,32,768]{3,2,1,0:T(8,128)(2,1)S(1)}, u32[]{:S(2)}, u32[]{:S(2)}) collective-permute-start(bf16[2,2,32,768]{3,2,1,0:T(8,128)(2,1)S(1)} %get-tuple-element.92), channel_id=1, source_target_pairs={{0,8},{8,0},{16,24},{24,16},{1,9},{9,1},{17,25},{25,17},{2,10},{10... | collective-permute-start | bytes 589832 | tf_op jit(solution)/shard_map/ppermute | solution.py:309
  129.3 11.9 %collective-permute-start.7 = (bf16[2,2,32,768]{3,2,1,0:T(8,128)(2,1)S(1)}, bf16[2,2,32,768]{3,2,1,0:T(8,128)(2,1)S(1)}, u32[]{:S(2)}, u32[]{:S(2)}) collective-permute-start(bf16[2,2,32,768]{3,2,1,0:T(8,128)(2,1)S(1)} %get-tuple-element.93), channel_id=1, source_target_pairs={{0,16},{8,24},{16,0},{24,8},{1,17},{9,25},{17,1},{25,9},{2,18},{10... | collective-permute-start | bytes 589832 | tf_op jit(solution)/shard_map/ppermute | solution.py:309
  130.5 10.7 %collective-permute-start.8 = (bf16[2,2,32,768]{3,2,1,0:T(8,128)(2,1)S(1)}, bf16[2,2,32,768]{3,2,1,0:T(8,128)(2,1)S(1)}, u32[]{:S(2)}, u32[]{:S(2)}) collective-permute-start(bf16[2,2,32,768]{3,2,1,0:T(8,128)(2,1)S(1)} %get-tuple-element.94), channel_id=1, source_target_pairs={{0,24},{8,16},{16,8},{24,0},{1,25},{9,17},{17,9},{25,1},{2,26},{10... | collective-permute-start | bytes 589832 | tf_op jit(solution)/shard_map/ppermute | solution.py:309
  133.0 8.5 %collective-permute-start.13 = (bf16[4,2,32,768]{3,2,1,0:T(8,128)(2,1)S(1)}, bf16[4,2,32,768]{3,2,1,0:T(8,128)(2,1)S(1)}, u32[]{:S(2)}, u32[]{:S(2)}) collective-permute-start(bf16[4,2,32,768]{3,2,1,0:T(8,128)(2,1)S(1)} %pad_maximum_fusion.1), channel_id=1, source_target_pairs={{0,4},{4,0},{1,5},{5,1},{2,6},{6,2},{3,7},{7,3},{8,12},{12,8},{9,1... | collective-permute-start | bytes 1179656 | tf_op jit(solution)/shard_map/ppermute | solution.py:454
  141.3 1.8 %collective-permute-start.9 = (bf16[4,2,32,768]{3,2,1,0:T(8,128)(2,1)S(1)}, bf16[4,2,32,768]{3,2,1,0:T(8,128)(2,1)S(1)}, u32[]{:S(2)}, u32[]{:S(2)}) collective-permute-start(bf16[4,2,32,768]{3,2,1,0:T(8,128)(2,1)S(1)} %pad_maximum_fusion), channel_id=1, source_target_pairs={{0,4},{4,0},{1,5},{5,1},{2,6},{6,2},{3,7},{7,3},{8,12},{12,8},{9,1... | collective-permute-start | bytes 1179656 | tf_op jit(solution)/shard_map/ppermute | solution.py:454
  (2 other events, 2.5 us)

commit v8 on v7

--- a/solution.py
+++ b/solution.py
@@ -321,7 +321,9 @@
         compiler_params=params(FULL_VMEM_BYTES),
         name="row_shares",
     )(part.reshape(1), states)
-    blocks = [states, None] + [across(share, step + 2) for step, share in enumerate(shares[1:])]
+    blocks = {0: states, 1: across(shares[0], 1)}
+    for step in range(3, res_size):
+        blocks[step] = across(shares[step - 1], step)
     halves = ((1 - core) * half_pairs).reshape(1), (core * half_pairs).reshape(1)
     places = [(part ^ step).reshape(1) for step in range(res_size)]
     own, halves, place, places = lax.optimization_barrier(
@@ -346,8 +348,8 @@
     for step in early:
         fields = projected(step, [row_query, row_key, row_value], fields, 1)
         if step == 0:
-            near, fields = lax.optimization_barrier((shares[0], fields))
-            blocks[1] = across(near, 1)
+            far, fields = lax.optimization_barrier((shares[1], fields))
+            blocks[2] = across(far, 2)
     q, k = projected(last, [row_query, row_key], fields[:2], 0)
 
     def scores(base):

time: 145 us -> 145 us (level)
    unnamed x24 -> x22, local copies, waits for them, and re-layouts: 3.99 us -> 3.98 us
where the time goes in v8:
time: 145 us; the launch traced here: 144 us
  blocking collectives  60.2 us (42%)
  waiting for transfers between devices  38.1 us (26%)
  Pallas kernels  25.9 us (18%)
  starting transfers between devices  15.7 us (11%)
  local copies, waits for them, and re-layouts  4.05 us (3%)
    all_to_all x1, blocking collectives, on_device(): lax.all_to_all(mid, ('pair', 'core', 'half', 'inner'), split_axis=0, conc...  39 us
    ppermute x3, waiting for transfers between devices, across(): lax.ppermute(field, ('half', 'inner'), [(at, at ^ step) for at in range(r...  25.1 us
    all_to_all x1, blocking collectives, on_device(): lax.all_to_all((mine + other).reshape(share), ('pair', 'inner'), split_ax...  12.2 us
    ppermute x6, waiting for transfers between devices, around(): lax.ppermute(field, 'pair', [(at, at ^ step) for at in range(pairs_size)])  9.72 us
    pallas_call x2, Pallas kernels, on_device(): pl.pallas_call(functools.partial(column_update, first_at), in_specs=[smem...  9.65 us
    all_to_all x1, blocking collectives, on_device(): lax.all_to_all(prob, ('pair', 'inner'), split_axis=0, concat_axis=0, tile...  9.02 us
    ppermute x6, starting transfers between devices, around(): lax.ppermute(field, 'pair', [(at, at ^ step) for at in range(pairs_size)])  7.11 us
    ppermute x3, starting transfers between devices, across(): lax.ppermute(field, ('half', 'inner'), [(at, at ^ step) for at in range(r...  5.82 us
  transfers between devices with their start and end apart: 14, of which 10 were waited for; matrix products, arithmetic and copies ran while one was open for 0% of the time, Pallas kernels for 9%

profile of v8, /device:TPU:0, one launch (start us, length us, event | category | flops | bytes accessed | tf_op | source)
XLA Modules:
  0.0 144.5 jit_solution(4995699693725314735)
XLA Ops:
  0.0 2.2 %row_shares.1 = (bf16[8,32,768]{2,1,0:T(8,128)(2,1)}, bf16[8,32,768]{2,1,0:T(8,128)(2,1)}, bf16[8,32,768]{2,1,0:T(8,128)(2,1)}) custom-call(s32[1]{0:T(128)} %bitcast.3.part_ref.at_ref, bf16[32,32,768]{2,1,0:T(8,128)(2,1)} %x_ref), custom_call_target="tpu_custom_call" | custom-call | tf_op jit(solution)/shard_map/row_shares/pallas_call | solution.py:311
  2.2 5.1 %collective-permute-start.2 = (bf16[8,32,768]{2,1,0:T(8,128)(2,1)}, bf16[8,32,768]{2,1,0:T(8,128)(2,1)S(1)}, u32[]{:S(2)}, u32[]{:S(2)}) collective-permute-start(bf16[8,32,768]{2,1,0:T(8,128)(2,1)} %get-tuple-element.67), channel_id=1, source_target_pairs={{0,3},{1,2},{2,1},{3,0},{4,7},{5,6},{6,5},{7,4},{8,11},{9,10},{10,... | collective-permute-start | bytes 1179656 | tf_op jit(solution)/shard_map/ppermute | solution.py:306
  9.8 1.4 copy-done.4
  11.3 1.3 row_project.5
  13.3 4.3 %collective-permute-done.2.x_ref = bf16[8,32,768]{2,1,0:T(8,128)(2,1)S(1)} collective-permute-done((bf16[8,32,768]{2,1,0:T(8,128)(2,1)}, bf16[8,32,768]{2,1,0:T(8,128)(2,1)S(1)}, u32[]{:S(2)}, u32[]{:S(2)}) %collective-permute-start.2) | collective-permute-done | bytes 393248 | tf_op jit(solution)/shard_map/ppermute | solution.py:306
  17.5 1.3 row_project.6
  18.8 7.3 %collective-permute-done.1.x_ref = bf16[8,32,768]{2,1,0:T(8,128)(2,1)S(1)} collective-permute-done((bf16[8,32,768]{2,1,0:T(8,128)(2,1)}, bf16[8,32,768]{2,1,0:T(8,128)(2,1)S(1)}, u32[]{:S(2)}, u32[]{:S(2)}) %collective-permute-start.1) | collective-permute-done | bytes 393248 | tf_op jit(solution)/shard_map/ppermute | solution.py:306
  26.2 1.3 row_project.7
  27.5 13.6 %collective-permute-done.x_ref = bf16[8,32,768]{2,1,0:T(8,128)(2,1)S(1)} collective-permute-done((bf16[8,32,768]{2,1,0:T(8,128)(2,1)S(1)}, bf16[8,32,768]{2,1,0:T(8,128)(2,1)S(1)}, u32[]{:S(2)}, u32[]{:S(2)}) %collective-permute-start) | collective-permute-done | bytes 393248 | tf_op jit(solution)/shard_map/ppermute | solution.py:306
  44.6 12.2 %all_to_all.15.parts_ref = f32[8,48,256]{2,1,0:T(8,128)S(1)} all-to-all(f32[8,48,256]{2,1,0:T(8,128)S(1)} %bitcast.11), channel_id=1, replica_groups=mesh['pair'=4,'core'=2,'half'=2,'inner'=2] {'pair','inner'}, dimensions={0} | all-to-all | bytes 786432 | tf_op jit(solution)/shard_map/all_to_all | solution.py:370
  56.8 2.5 %collective-permute-start.4 = (f32[48,256]{1,0:T(8,128)S(1)}, f32[48,256]{1,0:T(8,128)S(1)}, u32[]{:S(2)}, u32[]{:S(2)}) collective-permute-start(f32[48,256]{1,0:T(8,128)S(1)} %row_sum.1.mine_ref), channel_id=1, source_target_pairs={{0,2},{2,0},{1,3},{3,1},{4,6},{6,4},{5,7},{7,5},{8,10},{10,8},{9,1... | collective-permute-start | bytes 147464 | tf_op jit(solution)/shard_map/ppermute | solution.py:400
  61.0 1.3 collective-permute-done.4.other_ref
  62.6 9.0 %all_to_all.16 = bf16[8,48,256]{2,1,0:T(8,128)(2,1)S(1)} all-to-all(bf16[8,48,256]{2,1,0:T(8,128)(2,1)S(1)} %row_softmax.1), channel_id=1, replica_groups=mesh['pair'=4,'core'=2,'half'=2,'inner'=2] {'pair','inner'}, dimensions={0} | all-to-all | bytes 393216 | tf_op jit(solution)/shard_map/all_to_all | solution.py:402
  73.0 2.4 %row_update.1 = (bf16[32,4,8,768]{3,2,1,0:T(8,128)(2,1)S(1)}, bf16[2,512,768]{2,1,0:T(8,128)(2,1)S(1)}) custom-call(s32[1]{0:T(128)} %bitcast.base_ref.low_ref, bf16[3,128,256]{2,1,0:T(8,128)(2,1)S(1)} %collective-permute-done.5.prob_ref, bf16[8,128,768]{2,1,0:T(8,128)(2,1)S(1)} %get-tuple-element.88.v_ref, ...), custom_call_target="tpu_custom_call", output_to_operand_aliasing={{1}: (5, {})} | custom-call | flops 1409286144 | bytes 8000000 | tf_op jit(solution)/shard_map/row_update/pallas_call | solution.py:417
  75.5 39.0 %all_to_all.17.mid_ref = bf16[32,4,8,768]{3,2,1,0:T(8,128)(2,1)S(1)} all-to-all(bf16[32,4,8,768]{3,2,1,0:T(8,128)(2,1)S(1)} %get-tuple-element.90), channel_id=1, replica_groups=mesh['pair'=4,'core'=2,'half'=2,'inner'=2] {'pair','core','half','inner'}, dimensions={0} | all-to-all | bytes 3145728 | tf_op jit(solution)/shard_map/all_to_all | solution.py:434
  114.5 4.8 %column_update.3 = (bf16[2,2,32,768]{3,2,1,0:T(8,128)(2,1)S(1)}, bf16[2,2,32,768]{3,2,1,0:T(8,128)(2,1)S(1)}, bf16[2,2,32,768]{3,2,1,0:T(8,128)(2,1)S(1)}, bf16[2,2,32,768]{3,2,1,0:T(8,128)(2,1)S(1)}) custom-call(s32[1]{0:T(128)} %bitcast.2.seq_ref, bf16[32,4,8,768]{3,2,1,0:T(8,128)(2,1)S(1)} %all_to_all.17.mid_ref, bf16[768,768]{1,0:T(8,128)(2,1)S(1)} %copy-done.6, ...), custom_call_target="tpu_custom_call" | custom-call | flops 3019898880 | bytes 8000000 | tf_op jit(solution)/shard_map/column_update/pallas_call | solution.py:442
  119.3 1.5 %collective-permute-start.10 = (bf16[2,2,32,768]{3,2,1,0:T(8,128)(2,1)S(1)}, bf16[2,2,32,768]{3,2,1,0:T(8,128)(2,1)S(1)}, u32[]{:S(2)}, u32[]{:S(2)}) collective-permute-start(bf16[2,2,32,768]{3,2,1,0:T(8,128)(2,1)S(1)} %get-tuple-element.96), channel_id=1, source_target_pairs={{0,8},{8,0},{16,24},{24,16},{1,9},{9,1},{17,25},{25,17},{2,10},{10... | collective-permute-start | bytes 589832 | tf_op jit(solution)/shard_map/ppermute | solution.py:309
  120.9 1.3 collective-permute-start.11
  122.9 4.8 %column_update.2 = (bf16[2,2,32,768]{3,2,1,0:T(8,128)(2,1)S(1)}, bf16[2,2,32,768]{3,2,1,0:T(8,128)(2,1)S(1)}, bf16[2,2,32,768]{3,2,1,0:T(8,128)(2,1)S(1)}, bf16[2,2,32,768]{3,2,1,0:T(8,128)(2,1)S(1)}) custom-call(s32[1]{0:T(128)} %bitcast.2.seq_ref, bf16[32,4,8,768]{3,2,1,0:T(8,128)(2,1)S(1)} %all_to_all.17.mid_ref, bf16[768,768]{1,0:T(8,128)(2,1)S(1)} %copy-done.6, ...), custom_call_target="tpu_custom_call" | custom-call | flops 3019898880 | bytes 8000000 | tf_op jit(solution)/shard_map/column_update/pallas_call | solution.py:442
  127.7 1.5 %collective-permute-start.6 = (bf16[2,2,32,768]{3,2,1,0:T(8,128)(2,1)S(1)}, bf16[2,2,32,768]{3,2,1,0:T(8,128)(2,1)S(1)}, u32[]{:S(2)}, u32[]{:S(2)}) collective-permute-start(bf16[2,2,32,768]{3,2,1,0:T(8,128)(2,1)S(1)} %get-tuple-element.92), channel_id=1, source_target_pairs={{0,8},{8,0},{16,24},{24,16},{1,9},{9,1},{17,25},{25,17},{2,10},{10... | collective-permute-start | bytes 589832 | tf_op jit(solution)/shard_map/ppermute | solution.py:309
  129.3 1.3 collective-permute-start.7
  131.3 1.5 %collective-permute-done.11.refs_2_ = bf16[2,2,32,768]{3,2,1,0:T(8,128)(2,1)S(1)} collective-permute-done((bf16[2,2,32,768]{3,2,1,0:T(8,128)(2,1)S(1)}, bf16[2,2,32,768]{3,2,1,0:T(8,128)(2,1)S(1)}, u32[]{:S(2)}, u32[]{:S(2)}) %collective-permute-start.11) | collective-permute-done | bytes 196640 | tf_op jit(solution)/shard_map/ppermute | solution.py:309
  133.0 2.6 %collective-permute-done.6.refs_1_ = bf16[2,2,32,768]{3,2,1,0:T(8,128)(2,1)S(1)} collective-permute-done((bf16[2,2,32,768]{3,2,1,0:T(8,128)(2,1)S(1)}, bf16[2,2,32,768]{3,2,1,0:T(8,128)(2,1)S(1)}, u32[]{:S(2)}, u32[]{:S(2)}) %collective-permute-start.6) | collective-permute-done | bytes 196640 | tf_op jit(solution)/shard_map/ppermute | solution.py:309
  135.6 5.6 %collective-permute-done.7.refs_2_ = bf16[2,2,32,768]{3,2,1,0:T(8,128)(2,1)S(1)} collective-permute-done((bf16[2,2,32,768]{3,2,1,0:T(8,128)(2,1)S(1)}, bf16[2,2,32,768]{3,2,1,0:T(8,128)(2,1)S(1)}, u32[]{:S(2)}, u32[]{:S(2)}) %collective-permute-start.7) | collective-permute-done | bytes 196640 | tf_op jit(solution)/shard_map/ppermute | solution.py:309
  (57 shorter events, 14.8 us)
Async XLA Ops:
  0.0 7.3 %copy-start = (bf16[768,768]{1,0:T(8,128)(2,1)S(1)}, bf16[768,768]{1,0:T(8,128)(2,1)}, u32[]{:S(2)}) copy-start(bf16[768,768]{1,0:T(8,128)(2,1)} %refs_0_.9) | copy-start | bytes 3538948
  2.2 15.4 %collective-permute-start.2 = (bf16[8,32,768]{2,1,0:T(8,128)(2,1)}, bf16[8,32,768]{2,1,0:T(8,128)(2,1)S(1)}, u32[]{:S(2)}, u32[]{:S(2)}) collective-permute-start(bf16[8,32,768]{2,1,0:T(8,128)(2,1)} %get-tuple-element.67), channel_id=1, source_target_pairs={{0,3},{1,2},{2,1},{3,0},{4,7},{5,6},{6,5},{7,4},{8,11},{9,10},{10,... | collective-permute-start | bytes 1179656 | tf_op jit(solution)/shard_map/ppermute | solution.py:306
  7.3 18.9 %collective-permute-start.1 = (bf16[8,32,768]{2,1,0:T(8,128)(2,1)}, bf16[8,32,768]{2,1,0:T(8,128)(2,1)S(1)}, u32[]{:S(2)}, u32[]{:S(2)}) collective-permute-start(bf16[8,32,768]{2,1,0:T(8,128)(2,1)} %get-tuple-element.65), channel_id=1, source_target_pairs={{0,1},{1,0},{2,3},{3,2},{4,5},{5,4},{6,7},{7,6},{8,9},{9,8},{10,11... | collective-permute-start | bytes 1179656 | tf_op jit(solution)/shard_map/ppermute | solution.py:306
  7.3 1.3 copy-start.1
  9.8 1.4 copy-start.4
  11.2 1.3 copy-start.10
  11.2 6.3 %copy-start.2 = (bf16[768,768]{1,0:T(8,128)(2,1)S(1)}, bf16[768,768]{1,0:T(8,128)(2,1)}, u32[]{:S(2)}) copy-start(bf16[768,768]{1,0:T(8,128)(2,1)} %refs_0_.8) | copy-start | bytes 3538948
  12.6 28.5 %collective-permute-start = (bf16[8,32,768]{2,1,0:T(8,128)(2,1)S(1)}, bf16[8,32,768]{2,1,0:T(8,128)(2,1)S(1)}, u32[]{:S(2)}, u32[]{:S(2)}) collective-permute-start(bf16[8,32,768]{2,1,0:T(8,128)(2,1)S(1)} %copy-done.10), channel_id=1, source_target_pairs={{0,2},{1,3},{2,0},{3,1},{4,6},{5,7},{6,4},{7,5},{8,10},{9,11},{10,... | collective-permute-start | bytes 1179656 | tf_op jit(solution)/shard_map/ppermute | solution.py:306
  42.7 1.8 %collective-permute-start.3 = (f32[3,128,256]{2,1,0:T(8,128)S(1)}, f32[3,128,256]{2,1,0:T(8,128)S(1)}, u32[]{:S(2)}, u32[]{:S(2)}) collective-permute-start(f32[3,128,256]{2,1,0:T(8,128)S(1)} %row_scores.3), channel_id=1, source_target_pairs={{0,4},{4,0},{1,5},{5,1},{2,6},{6,2},{3,7},{7,3},{8,12},{12,8},{9,1... | collective-permute-start | bytes 1179656 | tf_op jit(solution)/shard_map/ppermute | solution.py:366
  56.8 5.6 %collective-permute-start.4 = (f32[48,256]{1,0:T(8,128)S(1)}, f32[48,256]{1,0:T(8,128)S(1)}, u32[]{:S(2)}, u32[]{:S(2)}) collective-permute-start(f32[48,256]{1,0:T(8,128)S(1)} %row_sum.1.mine_ref), channel_id=1, source_target_pairs={{0,2},{2,0},{1,3},{3,1},{4,6},{6,4},{5,7},{7,5},{8,10},{10,8},{9,1... | collective-permute-start | bytes 147464 | tf_op jit(solution)/shard_map/ppermute | solution.py:400
  71.6 1.4 %copy-start.5 = (bf16[768,768]{1,0:T(8,128)(2,1)S(1)}, bf16[768,768]{1,0:T(8,128)(2,1)}, u32[]{:S(2)}) copy-start(bf16[768,768]{1,0:T(8,128)(2,1)} %wo_ref.3) | copy-start | bytes 3538948
  71.6 1.4 collective-permute-start.5
  73.0 41.4 %copy-start.8 = (bf16[768,768]{1,0:T(8,128)(2,1)S(1)}, bf16[768,768]{1,0:T(8,128)(2,1)}, u32[]{:S(2)}) copy-start(bf16[768,768]{1,0:T(8,128)(2,1)} %wv_ref.3) | copy-start | bytes 3538948
  73.0 41.4 %copy-start.9 = (bf16[768,768]{1,0:T(8,128)(2,1)S(1)}, bf16[768,768]{1,0:T(8,128)(2,1)}, u32[]{:S(2)}) copy-start(bf16[768,768]{1,0:T(8,128)(2,1)} %wo_ref.5) | copy-start | bytes 3538948
  75.5 39.0 %copy-start.6 = (bf16[768,768]{1,0:T(8,128)(2,1)S(1)}, bf16[768,768]{1,0:T(8,128)(2,1)}, u32[]{:S(2)}) copy-start(bf16[768,768]{1,0:T(8,128)(2,1)} %wq_ref.3) | copy-start | bytes 3538948
  75.5 39.0 %copy-start.7 = (bf16[768,768]{1,0:T(8,128)(2,1)S(1)}, bf16[768,768]{1,0:T(8,128)(2,1)}, u32[]{:S(2)}) copy-start(bf16[768,768]{1,0:T(8,128)(2,1)} %wk_ref.3) | copy-start | bytes 3538948
  119.3 11.2 %collective-permute-start.10 = (bf16[2,2,32,768]{3,2,1,0:T(8,128)(2,1)S(1)}, bf16[2,2,32,768]{3,2,1,0:T(8,128)(2,1)S(1)}, u32[]{:S(2)}, u32[]{:S(2)}) collective-permute-start(bf16[2,2,32,768]{3,2,1,0:T(8,128)(2,1)S(1)} %get-tuple-element.96), channel_id=1, source_target_pairs={{0,8},{8,0},{16,24},{24,16},{1,9},{9,1},{17,25},{25,17},{2,10},{10... | collective-permute-start | bytes 589832 | tf_op jit(solution)/shard_map/ppermute | solution.py:309
  120.9 12.0 %collective-permute-start.11 = (bf16[2,2,32,768]{3,2,1,0:T(8,128)(2,1)S(1)}, bf16[2,2,32,768]{3,2,1,0:T(8,128)(2,1)S(1)}, u32[]{:S(2)}, u32[]{:S(2)}) collective-permute-start(bf16[2,2,32,768]{3,2,1,0:T(8,128)(2,1)S(1)} %get-tuple-element.97), channel_id=1, source_target_pairs={{0,16},{8,24},{16,0},{24,8},{1,17},{9,25},{17,1},{25,9},{2,18},{10... | collective-permute-start | bytes 589832 | tf_op jit(solution)/shard_map/ppermute | solution.py:309
  122.2 10.7 %collective-permute-start.12 = (bf16[2,2,32,768]{3,2,1,0:T(8,128)(2,1)S(1)}, bf16[2,2,32,768]{3,2,1,0:T(8,128)(2,1)S(1)}, u32[]{:S(2)}, u32[]{:S(2)}) collective-permute-start(bf16[2,2,32,768]{3,2,1,0:T(8,128)(2,1)S(1)} %get-tuple-element.98), channel_id=1, source_target_pairs={{0,24},{8,16},{16,8},{24,0},{1,25},{9,17},{17,9},{25,1},{2,26},{10... | collective-permute-start | bytes 589832 | tf_op jit(solution)/shard_map/ppermute | solution.py:309
  127.7 7.9 %collective-permute-start.6 = (bf16[2,2,32,768]{3,2,1,0:T(8,128)(2,1)S(1)}, bf16[2,2,32,768]{3,2,1,0:T(8,128)(2,1)S(1)}, u32[]{:S(2)}, u32[]{:S(2)}) collective-permute-start(bf16[2,2,32,768]{3,2,1,0:T(8,128)(2,1)S(1)} %get-tuple-element.92), channel_id=1, source_target_pairs={{0,8},{8,0},{16,24},{24,16},{1,9},{9,1},{17,25},{25,17},{2,10},{10... | collective-permute-start | bytes 589832 | tf_op jit(solution)/shard_map/ppermute | solution.py:309
  129.3 11.9 %collective-permute-start.7 = (bf16[2,2,32,768]{3,2,1,0:T(8,128)(2,1)S(1)}, bf16[2,2,32,768]{3,2,1,0:T(8,128)(2,1)S(1)}, u32[]{:S(2)}, u32[]{:S(2)}) collective-permute-start(bf16[2,2,32,768]{3,2,1,0:T(8,128)(2,1)S(1)} %get-tuple-element.93), channel_id=1, source_target_pairs={{0,16},{8,24},{16,0},{24,8},{1,17},{9,25},{17,1},{25,9},{2,18},{10... | collective-permute-start | bytes 589832 | tf_op jit(solution)/shard_map/ppermute | solution.py:309
  130.5 10.7 %collective-permute-start.8 = (bf16[2,2,32,768]{3,2,1,0:T(8,128)(2,1)S(1)}, bf16[2,2,32,768]{3,2,1,0:T(8,128)(2,1)S(1)}, u32[]{:S(2)}, u32[]{:S(2)}) collective-permute-start(bf16[2,2,32,768]{3,2,1,0:T(8,128)(2,1)S(1)} %get-tuple-element.94), channel_id=1, source_target_pairs={{0,24},{8,16},{16,8},{24,0},{1,25},{9,17},{17,9},{25,1},{2,26},{10... | collective-permute-start | bytes 589832 | tf_op jit(solution)/shard_map/ppermute | solution.py:309
  133.0 8.5 %collective-permute-start.13 = (bf16[4,2,32,768]{3,2,1,0:T(8,128)(2,1)S(1)}, bf16[4,2,32,768]{3,2,1,0:T(8,128)(2,1)S(1)}, u32[]{:S(2)}, u32[]{:S(2)}) collective-permute-start(bf16[4,2,32,768]{3,2,1,0:T(8,128)(2,1)S(1)} %pad_maximum_fusion.1), channel_id=1, source_target_pairs={{0,4},{4,0},{1,5},{5,1},{2,6},{6,2},{3,7},{7,3},{8,12},{12,8},{9,1... | collective-permute-start | bytes 1179656 | tf_op jit(solution)/shard_map/ppermute | solution.py:456
  141.3 1.8 %collective-permute-start.9 = (bf16[4,2,32,768]{3,2,1,0:T(8,128)(2,1)S(1)}, bf16[4,2,32,768]{3,2,1,0:T(8,128)(2,1)S(1)}, u32[]{:S(2)}, u32[]{:S(2)}) collective-permute-start(bf16[4,2,32,768]{3,2,1,0:T(8,128)(2,1)S(1)} %pad_maximum_fusion), channel_id=1, source_target_pairs={{0,4},{4,0},{1,5},{5,1},{2,6},{6,2},{3,7},{7,3},{8,12},{12,8},{9,1... | collective-permute-start | bytes 1179656 | tf_op jit(solution)/shard_map/ppermute | solution.py:456
  (1 other events, 1.3 us)

commit v9 on v8

--- a/solution.py
+++ b/solution.py
@@ -226,9 +226,15 @@
 
 
 def in_order(refs, at, pairs_size):
-    straight = refs[at * (pairs_size + 1) : at * (pairs_size + 1) + pairs_size]
-    crossed = refs[at * (pairs_size + 1) + pairs_size]
-    return [field for step in range(pairs_size) for field in (straight[step].at[0], crossed.at[step])]
+    first = at * (pairs_size + 2)
+    straight = refs[first : first + pairs_size]
+    crossed = refs[first + pairs_size : first + pairs_size + 2]
+    half = pairs_size // 2
+    return [
+        field
+        for step in range(pairs_size)
+        for field in (straight[step].at[0], crossed[step // half].at[step % half])
+    ]
 
 
 def assemble(seq_size, pieces, slot, seq_ref, *refs):
@@ -453,8 +459,11 @@
         )(place, moved, col_query, col_key, col_value, col_out)
         first_at += at_once
         arrived = [updated[0]] + [around(updated[step], step) for step in range(1, pairs_size)]
-        crossed = lax.ppermute(jnp.stack([field[1] for field in arrived]), "core", swap)
-        home.append(arrived + [crossed])
+        crossed = [
+            lax.ppermute(jnp.stack([field[1] for field in fields]), "core", swap)
+            for fields in (arrived[: pairs_size // 2], arrived[pairs_size // 2 :])
+        ]
+        home.append(arrived + crossed)
 
     steps = 2
     out = []

time: 145 us -> 144 us (level)
  transfers between devices with their start and end apart: 14 -> 16, of which waited for: 10 -> 10; matrix products, arithmetic and copies ran while one was open for 0% -> 0% of each run, Pallas kernels for 9% -> 9%
where the time goes in v9:
time: 144 us
  blocking collectives  60.2 us (42%)
  waiting for transfers between devices  37.1 us (26%)
  Pallas kernels  25.9 us (18%)
  starting transfers between devices  16.4 us (11%)
  local copies, waits for them, and re-layouts  4.05 us (3%)
    all_to_all x1, blocking collectives, on_device(): lax.all_to_all(mid, ('pair', 'core', 'half', 'inner'), split_axis=0, conc...  39 us
    ppermute x3, waiting for transfers between devices, across(): lax.ppermute(field, ('half', 'inner'), [(at, at ^ step) for at in range(r...  25.1 us
    all_to_all x1, blocking collectives, on_device(): lax.all_to_all((mine + other).reshape(share), ('pair', 'inner'), split_ax...  12.2 us
    pallas_call x2, Pallas kernels, on_device(): pl.pallas_call(functools.partial(column_update, first_at), in_specs=[smem...  9.65 us
    ppermute x6, waiting for transfers between devices, around(): lax.ppermute(field, 'pair', [(at, at ^ step) for at in range(pairs_size)])  9.04 us
    all_to_all x1, blocking collectives, on_device(): lax.all_to_all(prob, ('pair', 'inner'), split_axis=0, concat_axis=0, tile...  9.02 us
    ppermute x6, starting transfers between devices, around(): lax.ppermute(field, 'pair', [(at, at ^ step) for at in range(pairs_size)])  7.11 us
    ppermute x3, starting transfers between devices, across(): lax.ppermute(field, ('half', 'inner'), [(at, at ^ step) for at in range(r...  5.82 us
  transfers between devices with their start and end apart: 16, of which 10 were waited for; matrix products, arithmetic and copies ran while one was open for 0% of the time, Pallas kernels for 9%

profile of v9, /device:TPU:0, one launch (start us, length us, event | category | flops | bytes accessed | tf_op | source)
XLA Modules:
  0.0 144.1 jit_solution(7489883259949719958)
XLA Ops:
  0.0 2.2 %row_shares.1 = (bf16[8,32,768]{2,1,0:T(8,128)(2,1)}, bf16[8,32,768]{2,1,0:T(8,128)(2,1)}, bf16[8,32,768]{2,1,0:T(8,128)(2,1)}) custom-call(s32[1]{0:T(128)} %bitcast.3.part_ref.at_ref, bf16[32,32,768]{2,1,0:T(8,128)(2,1)} %x_ref), custom_call_target="tpu_custom_call" | custom-call | tf_op jit(solution)/shard_map/row_shares/pallas_call | solution.py:317
  2.2 5.1 %collective-permute-start.2 = (bf16[8,32,768]{2,1,0:T(8,128)(2,1)}, bf16[8,32,768]{2,1,0:T(8,128)(2,1)S(1)}, u32[]{:S(2)}, u32[]{:S(2)}) collective-permute-start(bf16[8,32,768]{2,1,0:T(8,128)(2,1)} %get-tuple-element.67), channel_id=1, source_target_pairs={{0,3},{1,2},{2,1},{3,0},{4,7},{5,6},{6,5},{7,4},{8,11},{9,10},{10,... | collective-permute-start | bytes 1179656 | tf_op jit(solution)/shard_map/ppermute | solution.py:312
  9.8 1.4 copy-done.4
  11.2 1.3 row_project.5
  13.3 4.3 %collective-permute-done.2.x_ref = bf16[8,32,768]{2,1,0:T(8,128)(2,1)S(1)} collective-permute-done((bf16[8,32,768]{2,1,0:T(8,128)(2,1)}, bf16[8,32,768]{2,1,0:T(8,128)(2,1)S(1)}, u32[]{:S(2)}, u32[]{:S(2)}) %collective-permute-start.2) | collective-permute-done | bytes 393248 | tf_op jit(solution)/shard_map/ppermute | solution.py:312
  17.5 1.3 row_project.6
  18.8 7.3 %collective-permute-done.1.x_ref = bf16[8,32,768]{2,1,0:T(8,128)(2,1)S(1)} collective-permute-done((bf16[8,32,768]{2,1,0:T(8,128)(2,1)}, bf16[8,32,768]{2,1,0:T(8,128)(2,1)S(1)}, u32[]{:S(2)}, u32[]{:S(2)}) %collective-permute-start.1) | collective-permute-done | bytes 393248 | tf_op jit(solution)/shard_map/ppermute | solution.py:312
  26.2 1.3 row_project.7
  27.5 13.6 %collective-permute-done.x_ref = bf16[8,32,768]{2,1,0:T(8,128)(2,1)S(1)} collective-permute-done((bf16[8,32,768]{2,1,0:T(8,128)(2,1)S(1)}, bf16[8,32,768]{2,1,0:T(8,128)(2,1)S(1)}, u32[]{:S(2)}, u32[]{:S(2)}) %collective-permute-start) | collective-permute-done | bytes 393248 | tf_op jit(solution)/shard_map/ppermute | solution.py:312
  44.6 12.2 %all_to_all.15.parts_ref = f32[8,48,256]{2,1,0:T(8,128)S(1)} all-to-all(f32[8,48,256]{2,1,0:T(8,128)S(1)} %bitcast.11), channel_id=1, replica_groups=mesh['pair'=4,'core'=2,'half'=2,'inner'=2] {'pair','inner'}, dimensions={0} | all-to-all | bytes 786432 | tf_op jit(solution)/shard_map/all_to_all | solution.py:376
  56.8 2.5 %collective-permute-start.4 = (f32[48,256]{1,0:T(8,128)S(1)}, f32[48,256]{1,0:T(8,128)S(1)}, u32[]{:S(2)}, u32[]{:S(2)}) collective-permute-start(f32[48,256]{1,0:T(8,128)S(1)} %row_sum.1.mine_ref), channel_id=1, source_target_pairs={{0,2},{2,0},{1,3},{3,1},{4,6},{6,4},{5,7},{7,5},{8,10},{10,8},{9,1... | collective-permute-start | bytes 147464 | tf_op jit(solution)/shard_map/ppermute | solution.py:406
  61.0 1.3 collective-permute-done.4.other_ref
  62.6 9.0 %all_to_all.16 = bf16[8,48,256]{2,1,0:T(8,128)(2,1)S(1)} all-to-all(bf16[8,48,256]{2,1,0:T(8,128)(2,1)S(1)} %row_softmax.1), channel_id=1, replica_groups=mesh['pair'=4,'core'=2,'half'=2,'inner'=2] {'pair','inner'}, dimensions={0} | all-to-all | bytes 393216 | tf_op jit(solution)/shard_map/all_to_all | solution.py:408
  73.0 2.4 %row_update.1 = (bf16[32,4,8,768]{3,2,1,0:T(8,128)(2,1)S(1)}, bf16[2,512,768]{2,1,0:T(8,128)(2,1)S(1)}) custom-call(s32[1]{0:T(128)} %bitcast.base_ref.low_ref, bf16[3,128,256]{2,1,0:T(8,128)(2,1)S(1)} %collective-permute-done.5.prob_ref, bf16[8,128,768]{2,1,0:T(8,128)(2,1)S(1)} %get-tuple-element.88.v_ref, ...), custom_call_target="tpu_custom_call", output_to_operand_aliasing={{1}: (5, {})} | custom-call | flops 1409286144 | bytes 8000000 | tf_op jit(solution)/shard_map/row_update/pallas_call | solution.py:423
  75.5 39.0 %all_to_all.17.mid_ref = bf16[32,4,8,768]{3,2,1,0:T(8,128)(2,1)S(1)} all-to-all(bf16[32,4,8,768]{3,2,1,0:T(8,128)(2,1)S(1)} %get-tuple-element.90), channel_id=1, replica_groups=mesh['pair'=4,'core'=2,'half'=2,'inner'=2] {'pair','core','half','inner'}, dimensions={0} | all-to-all | bytes 3145728 | tf_op jit(solution)/shard_map/all_to_all | solution.py:440
  114.5 4.8 %column_update.3 = (bf16[2,2,32,768]{3,2,1,0:T(8,128)(2,1)S(1)}, bf16[2,2,32,768]{3,2,1,0:T(8,128)(2,1)S(1)}, bf16[2,2,32,768]{3,2,1,0:T(8,128)(2,1)S(1)}, bf16[2,2,32,768]{3,2,1,0:T(8,128)(2,1)S(1)}) custom-call(s32[1]{0:T(128)} %bitcast.2.seq_ref, bf16[32,4,8,768]{3,2,1,0:T(8,128)(2,1)S(1)} %all_to_all.17.mid_ref, bf16[768,768]{1,0:T(8,128)(2,1)S(1)} %copy-done.6, ...), custom_call_target="tpu_custom_call" | custom-call | flops 3019898880 | bytes 8000000 | tf_op jit(solution)/shard_map/column_update/pallas_call | solution.py:448
  119.3 1.5 %collective-permute-start.11 = (bf16[2,2,32,768]{3,2,1,0:T(8,128)(2,1)S(1)}, bf16[2,2,32,768]{3,2,1,0:T(8,128)(2,1)S(1)}, u32[]{:S(2)}, u32[]{:S(2)}) collective-permute-start(bf16[2,2,32,768]{3,2,1,0:T(8,128)(2,1)S(1)} %get-tuple-element.96), channel_id=1, source_target_pairs={{0,8},{8,0},{16,24},{24,16},{1,9},{9,1},{17,25},{25,17},{2,10},{10... | collective-permute-start | bytes 589832 | tf_op jit(solution)/shard_map/ppermute | solution.py:315
  120.9 1.3 collective-permute-start.12
  122.9 4.8 %column_update.2 = (bf16[2,2,32,768]{3,2,1,0:T(8,128)(2,1)S(1)}, bf16[2,2,32,768]{3,2,1,0:T(8,128)(2,1)S(1)}, bf16[2,2,32,768]{3,2,1,0:T(8,128)(2,1)S(1)}, bf16[2,2,32,768]{3,2,1,0:T(8,128)(2,1)S(1)}) custom-call(s32[1]{0:T(128)} %bitcast.2.seq_ref, bf16[32,4,8,768]{3,2,1,0:T(8,128)(2,1)S(1)} %all_to_all.17.mid_ref, bf16[768,768]{1,0:T(8,128)(2,1)S(1)} %copy-done.6, ...), custom_call_target="tpu_custom_call" | custom-call | flops 3019898880 | bytes 8000000 | tf_op jit(solution)/shard_map/column_update/pallas_call | solution.py:448
  127.7 1.5 %collective-permute-start.6 = (bf16[2,2,32,768]{3,2,1,0:T(8,128)(2,1)S(1)}, bf16[2,2,32,768]{3,2,1,0:T(8,128)(2,1)S(1)}, u32[]{:S(2)}, u32[]{:S(2)}) collective-permute-start(bf16[2,2,32,768]{3,2,1,0:T(8,128)(2,1)S(1)} %get-tuple-element.92), channel_id=1, source_target_pairs={{0,8},{8,0},{16,24},{24,16},{1,9},{9,1},{17,25},{25,17},{2,10},{10... | collective-permute-start | bytes 589832 | tf_op jit(solution)/shard_map/ppermute | solution.py:315
  129.3 1.3 collective-permute-start.7
  131.3 1.5 %collective-permute-done.12.refs_2_ = bf16[2,2,32,768]{3,2,1,0:T(8,128)(2,1)S(1)} collective-permute-done((bf16[2,2,32,768]{3,2,1,0:T(8,128)(2,1)S(1)}, bf16[2,2,32,768]{3,2,1,0:T(8,128)(2,1)S(1)}, u32[]{:S(2)}, u32[]{:S(2)}) %collective-permute-start.12) | collective-permute-done | bytes 196640 | tf_op jit(solution)/shard_map/ppermute | solution.py:315
  133.5 2.2 %collective-permute-done.6.refs_1_ = bf16[2,2,32,768]{3,2,1,0:T(8,128)(2,1)S(1)} collective-permute-done((bf16[2,2,32,768]{3,2,1,0:T(8,128)(2,1)S(1)}, bf16[2,2,32,768]{3,2,1,0:T(8,128)(2,1)S(1)}, u32[]{:S(2)}, u32[]{:S(2)}) %collective-permute-start.6) | collective-permute-done | bytes 196640 | tf_op jit(solution)/shard_map/ppermute | solution.py:315
  135.8 5.4 %collective-permute-done.7.refs_2_ = bf16[2,2,32,768]{3,2,1,0:T(8,128)(2,1)S(1)} collective-permute-done((bf16[2,2,32,768]{3,2,1,0:T(8,128)(2,1)S(1)}, bf16[2,2,32,768]{3,2,1,0:T(8,128)(2,1)S(1)}, u32[]{:S(2)}, u32[]{:S(2)}) %collective-permute-start.7) | collective-permute-done | bytes 196640 | tf_op jit(solution)/shard_map/ppermute | solution.py:315
  (63 shorter events, 15.1 us)
Async XLA Ops:
  0.0 7.3 %copy-start = (bf16[768,768]{1,0:T(8,128)(2,1)S(1)}, bf16[768,768]{1,0:T(8,128)(2,1)}, u32[]{:S(2)}) copy-start(bf16[768,768]{1,0:T(8,128)(2,1)} %refs_0_.9) | copy-start | bytes 3538948
  2.2 15.4 %collective-permute-start.2 = (bf16[8,32,768]{2,1,0:T(8,128)(2,1)}, bf16[8,32,768]{2,1,0:T(8,128)(2,1)S(1)}, u32[]{:S(2)}, u32[]{:S(2)}) collective-permute-start(bf16[8,32,768]{2,1,0:T(8,128)(2,1)} %get-tuple-element.67), channel_id=1, source_target_pairs={{0,3},{1,2},{2,1},{3,0},{4,7},{5,6},{6,5},{7,4},{8,11},{9,10},{10,... | collective-permute-start | bytes 1179656 | tf_op jit(solution)/shard_map/ppermute | solution.py:312
  7.3 18.9 %collective-permute-start.1 = (bf16[8,32,768]{2,1,0:T(8,128)(2,1)}, bf16[8,32,768]{2,1,0:T(8,128)(2,1)S(1)}, u32[]{:S(2)}, u32[]{:S(2)}) collective-permute-start(bf16[8,32,768]{2,1,0:T(8,128)(2,1)} %get-tuple-element.65), channel_id=1, source_target_pairs={{0,1},{1,0},{2,3},{3,2},{4,5},{5,4},{6,7},{7,6},{8,9},{9,8},{10,11... | collective-permute-start | bytes 1179656 | tf_op jit(solution)/shard_map/ppermute | solution.py:312
  9.8 1.4 copy-start.4
  11.2 6.3 %copy-start.2 = (bf16[768,768]{1,0:T(8,128)(2,1)S(1)}, bf16[768,768]{1,0:T(8,128)(2,1)}, u32[]{:S(2)}) copy-start(bf16[768,768]{1,0:T(8,128)(2,1)} %refs_0_.8) | copy-start | bytes 3538948
  12.6 28.5 %collective-permute-start = (bf16[8,32,768]{2,1,0:T(8,128)(2,1)S(1)}, bf16[8,32,768]{2,1,0:T(8,128)(2,1)S(1)}, u32[]{:S(2)}, u32[]{:S(2)}) collective-permute-start(bf16[8,32,768]{2,1,0:T(8,128)(2,1)S(1)} %copy-done.10), channel_id=1, source_target_pairs={{0,2},{1,3},{2,0},{3,1},{4,6},{5,7},{6,4},{7,5},{8,10},{9,11},{10,... | collective-permute-start | bytes 1179656 | tf_op jit(solution)/shard_map/ppermute | solution.py:312
  42.7 1.8 %collective-permute-start.3 = (f32[3,128,256]{2,1,0:T(8,128)S(1)}, f32[3,128,256]{2,1,0:T(8,128)S(1)}, u32[]{:S(2)}, u32[]{:S(2)}) collective-permute-start(f32[3,128,256]{2,1,0:T(8,128)S(1)} %row_scores.3), channel_id=1, source_target_pairs={{0,4},{4,0},{1,5},{5,1},{2,6},{6,2},{3,7},{7,3},{8,12},{12,8},{9,1... | collective-permute-start | bytes 1179656 | tf_op jit(solution)/shard_map/ppermute | solution.py:372
  56.8 5.6 %collective-permute-start.4 = (f32[48,256]{1,0:T(8,128)S(1)}, f32[48,256]{1,0:T(8,128)S(1)}, u32[]{:S(2)}, u32[]{:S(2)}) collective-permute-start(f32[48,256]{1,0:T(8,128)S(1)} %row_sum.1.mine_ref), channel_id=1, source_target_pairs={{0,2},{2,0},{1,3},{3,1},{4,6},{6,4},{5,7},{7,5},{8,10},{10,8},{9,1... | collective-permute-start | bytes 147464 | tf_op jit(solution)/shard_map/ppermute | solution.py:406
  71.6 1.4 %copy-start.5 = (bf16[768,768]{1,0:T(8,128)(2,1)S(1)}, bf16[768,768]{1,0:T(8,128)(2,1)}, u32[]{:S(2)}) copy-start(bf16[768,768]{1,0:T(8,128)(2,1)} %wo_ref.3) | copy-start | bytes 3538948
  71.6 1.4 %collective-permute-start.5 = (bf16[3,128,256]{2,1,0:T(8,128)(2,1)S(1)}, bf16[3,128,256]{2,1,0:T(8,128)(2,1)S(1)}, u32[]{:S(2)}, u32[]{:S(2)}) collective-permute-start(bf16[3,128,256]{2,1,0:T(8,128)(2,1)S(1)} %bitcast.9), channel_id=1, source_target_pairs={{0,4},{4,0},{1,5},{5,1},{2,6},{6,2},{3,7},{7,3},{8,12},{12,8},{9,1... | collective-permute-start | bytes 589832 | tf_op jit(solution)/shard_map/ppermute | solution.py:410
  73.0 41.4 %copy-start.8 = (bf16[768,768]{1,0:T(8,128)(2,1)S(1)}, bf16[768,768]{1,0:T(8,128)(2,1)}, u32[]{:S(2)}) copy-start(bf16[768,768]{1,0:T(8,128)(2,1)} %wv_ref.3) | copy-start | bytes 3538948
  73.0 41.4 %copy-start.9 = (bf16[768,768]{1,0:T(8,128)(2,1)S(1)}, bf16[768,768]{1,0:T(8,128)(2,1)}, u32[]{:S(2)}) copy-start(bf16[768,768]{1,0:T(8,128)(2,1)} %wo_ref.5) | copy-start | bytes 3538948
  75.5 39.0 %copy-start.6 = (bf16[768,768]{1,0:T(8,128)(2,1)S(1)}, bf16[768,768]{1,0:T(8,128)(2,1)}, u32[]{:S(2)}) copy-start(bf16[768,768]{1,0:T(8,128)(2,1)} %wq_ref.3) | copy-start | bytes 3538948
  75.5 39.0 %copy-start.7 = (bf16[768,768]{1,0:T(8,128)(2,1)S(1)}, bf16[768,768]{1,0:T(8,128)(2,1)}, u32[]{:S(2)}) copy-start(bf16[768,768]{1,0:T(8,128)(2,1)} %wk_ref.3) | copy-start | bytes 3538948
  119.3 11.3 %collective-permute-start.11 = (bf16[2,2,32,768]{3,2,1,0:T(8,128)(2,1)S(1)}, bf16[2,2,32,768]{3,2,1,0:T(8,128)(2,1)S(1)}, u32[]{:S(2)}, u32[]{:S(2)}) collective-permute-start(bf16[2,2,32,768]{3,2,1,0:T(8,128)(2,1)S(1)} %get-tuple-element.96), channel_id=1, source_target_pairs={{0,8},{8,0},{16,24},{24,16},{1,9},{9,1},{17,25},{25,17},{2,10},{10... | collective-permute-start | bytes 589832 | tf_op jit(solution)/shard_map/ppermute | solution.py:315
  120.9 12.0 %collective-permute-start.12 = (bf16[2,2,32,768]{3,2,1,0:T(8,128)(2,1)S(1)}, bf16[2,2,32,768]{3,2,1,0:T(8,128)(2,1)S(1)}, u32[]{:S(2)}, u32[]{:S(2)}) collective-permute-start(bf16[2,2,32,768]{3,2,1,0:T(8,128)(2,1)S(1)} %get-tuple-element.97), channel_id=1, source_target_pairs={{0,16},{8,24},{16,0},{24,8},{1,17},{9,25},{17,1},{25,9},{2,18},{10... | collective-permute-start | bytes 589832 | tf_op jit(solution)/shard_map/ppermute | solution.py:315
  122.2 10.7 %collective-permute-start.13 = (bf16[2,2,32,768]{3,2,1,0:T(8,128)(2,1)S(1)}, bf16[2,2,32,768]{3,2,1,0:T(8,128)(2,1)S(1)}, u32[]{:S(2)}, u32[]{:S(2)}) collective-permute-start(bf16[2,2,32,768]{3,2,1,0:T(8,128)(2,1)S(1)} %get-tuple-element.98), channel_id=1, source_target_pairs={{0,24},{8,16},{16,8},{24,0},{1,25},{9,17},{17,9},{25,1},{2,26},{10... | collective-permute-start | bytes 589832 | tf_op jit(solution)/shard_map/ppermute | solution.py:315
  127.7 7.9 %collective-permute-start.6 = (bf16[2,2,32,768]{3,2,1,0:T(8,128)(2,1)S(1)}, bf16[2,2,32,768]{3,2,1,0:T(8,128)(2,1)S(1)}, u32[]{:S(2)}, u32[]{:S(2)}) collective-permute-start(bf16[2,2,32,768]{3,2,1,0:T(8,128)(2,1)S(1)} %get-tuple-element.92), channel_id=1, source_target_pairs={{0,8},{8,0},{16,24},{24,16},{1,9},{9,1},{17,25},{25,17},{2,10},{10... | collective-permute-start | bytes 589832 | tf_op jit(solution)/shard_map/ppermute | solution.py:315
  129.3 11.9 %collective-permute-start.7 = (bf16[2,2,32,768]{3,2,1,0:T(8,128)(2,1)S(1)}, bf16[2,2,32,768]{3,2,1,0:T(8,128)(2,1)S(1)}, u32[]{:S(2)}, u32[]{:S(2)}) collective-permute-start(bf16[2,2,32,768]{3,2,1,0:T(8,128)(2,1)S(1)} %get-tuple-element.93), channel_id=1, source_target_pairs={{0,16},{8,24},{16,0},{24,8},{1,17},{9,25},{17,1},{25,9},{2,18},{10... | collective-permute-start | bytes 589832 | tf_op jit(solution)/shard_map/ppermute | solution.py:315
  130.6 10.6 %collective-permute-start.8 = (bf16[2,2,32,768]{3,2,1,0:T(8,128)(2,1)S(1)}, bf16[2,2,32,768]{3,2,1,0:T(8,128)(2,1)S(1)}, u32[]{:S(2)}, u32[]{:S(2)}) collective-permute-start(bf16[2,2,32,768]{3,2,1,0:T(8,128)(2,1)S(1)} %get-tuple-element.94), channel_id=1, source_target_pairs={{0,24},{8,16},{16,8},{24,0},{1,25},{9,17},{17,9},{25,1},{2,26},{10... | collective-permute-start | bytes 589832 | tf_op jit(solution)/shard_map/ppermute | solution.py:315
  132.9 8.5 %collective-permute-start.14 = (bf16[2,2,32,768]{3,2,1,0:T(8,128)(2,1)S(1)}, bf16[2,2,32,768]{3,2,1,0:T(8,128)(2,1)S(1)}, u32[]{:S(2)}, u32[]{:S(2)}) collective-permute-start(bf16[2,2,32,768]{3,2,1,0:T(8,128)(2,1)S(1)} %pad_maximum_fusion.2), channel_id=1, source_target_pairs={{0,4},{4,0},{1,5},{5,1},{2,6},{6,2},{3,7},{7,3},{8,12},{12,8},{9,1... | collective-permute-start | bytes 589832 | tf_op jit(solution)/shard_map/ppermute | solution.py:463
  132.9 8.5 %collective-permute-start.15 = (bf16[2,2,32,768]{3,2,1,0:T(8,128)(2,1)S(1)}, bf16[2,2,32,768]{3,2,1,0:T(8,128)(2,1)S(1)}, u32[]{:S(2)}, u32[]{:S(2)}) collective-permute-start(bf16[2,2,32,768]{3,2,1,0:T(8,128)(2,1)S(1)} %pad_maximum_fusion.3), channel_id=1, source_target_pairs={{0,4},{4,0},{1,5},{5,1},{2,6},{6,2},{3,7},{7,3},{8,12},{12,8},{9,1... | collective-permute-start | bytes 589832 | tf_op jit(solution)/shard_map/ppermute | solution.py:463
  135.7 6.9 %collective-permute-start.9 = (bf16[2,2,32,768]{3,2,1,0:T(8,128)(2,1)S(1)}, bf16[2,2,32,768]{3,2,1,0:T(8,128)(2,1)S(1)}, u32[]{:S(2)}, u32[]{:S(2)}) collective-permute-start(bf16[2,2,32,768]{3,2,1,0:T(8,128)(2,1)S(1)} %pad_maximum_fusion), channel_id=1, source_target_pairs={{0,4},{4,0},{1,5},{5,1},{2,6},{6,2},{3,7},{7,3},{8,12},{12,8},{9,1... | collective-permute-start | bytes 589832 | tf_op jit(solution)/shard_map/ppermute | solution.py:463
  141.3 1.5 %collective-permute-start.10 = (bf16[2,2,32,768]{3,2,1,0:T(8,128)(2,1)S(1)}, bf16[2,2,32,768]{3,2,1,0:T(8,128)(2,1)S(1)}, u32[]{:S(2)}, u32[]{:S(2)}) collective-permute-start(bf16[2,2,32,768]{3,2,1,0:T(8,128)(2,1)S(1)} %pad_maximum_fusion.1), channel_id=1, source_target_pairs={{0,4},{4,0},{1,5},{5,1},{2,6},{6,2},{3,7},{7,3},{8,12},{12,8},{9,1... | collective-permute-start | bytes 589832 | tf_op jit(solution)/shard_map/ppermute | solution.py:463
  (3 other events, 3.9 us)

commit v10 on v9

--- a/solution.py
+++ b/solution.py
@@ -191,7 +191,7 @@
     mid = mid_ref[:, first_at : first_at + at_once].astype(F32)
     mid = jnp.concatenate([mid[:, at].reshape(all_rows, width) for at in range(at_once)], axis=0)
     normed = normalize(mid)
-    q = (dot(normed, wq_ref[...]).astype(BF16) * scale).astype(BF16)
+    q = (dot(normed, wq_ref[...]) * scale).astype(BF16)
     k = dot(normed, wk_ref[...]).astype(BF16)
     v = dot(normed, wv_ref[...]).astype(BF16)
     masks = head_masks(pair, head_dim)

time: 144 us -> 144 us (level)
  no operation moved by 1% of the time
where the time goes in v10:
time: 144 us
  blocking collectives  60.2 us (42%)
  waiting for transfers between devices  37.1 us (26%)
  Pallas kernels  25.9 us (18%)
  starting transfers between devices  16.4 us (11%)
  local copies, waits for them, and re-layouts  4.05 us (3%)
    all_to_all x1, blocking collectives, on_device(): lax.all_to_all(mid, ('pair', 'core', 'half', 'inner'), split_axis=0, conc...  39 us
    ppermute x3, waiting for transfers between devices, across(): lax.ppermute(field, ('half', 'inner'), [(at, at ^ step) for at in range(r...  25.1 us
    all_to_all x1, blocking collectives, on_device(): lax.all_to_all((mine + other).reshape(share), ('pair', 'inner'), split_ax...  12.2 us
    pallas_call x2, Pallas kernels, on_device(): pl.pallas_call(functools.partial(column_update, first_at), in_specs=[smem...  9.65 us
    ppermute x6, waiting for transfers between devices, around(): lax.ppermute(field, 'pair', [(at, at ^ step) for at in range(pairs_size)])  9.04 us
    all_to_all x1, blocking collectives, on_device(): lax.all_to_all(prob, ('pair', 'inner'), split_axis=0, concat_axis=0, tile...  9.02 us
    ppermute x6, starting transfers between devices, around(): lax.ppermute(field, 'pair', [(at, at ^ step) for at in range(pairs_size)])  7.11 us
    ppermute x3, starting transfers between devices, across(): lax.ppermute(field, ('half', 'inner'), [(at, at ^ step) for at in range(r...  5.82 us
  transfers between devices with their start and end apart: 16, of which 10 were waited for; matrix products, arithmetic and copies ran while one was open for 0% of the time, Pallas kernels for 9%

profile of v10, /device:TPU:0, one launch (start us, length us, event | category | flops | bytes accessed | tf_op | source)
XLA Modules:
  0.0 144.1 jit_solution(11893889581422147124)
XLA Ops:
  0.0 2.2 %row_shares.1 = (bf16[8,32,768]{2,1,0:T(8,128)(2,1)}, bf16[8,32,768]{2,1,0:T(8,128)(2,1)}, bf16[8,32,768]{2,1,0:T(8,128)(2,1)}) custom-call(s32[1]{0:T(128)} %bitcast.3.part_ref.at_ref, bf16[32,32,768]{2,1,0:T(8,128)(2,1)} %x_ref), custom_call_target="tpu_custom_call" | custom-call | tf_op jit(solution)/shard_map/row_shares/pallas_call | solution.py:317
  2.2 5.1 %collective-permute-start.2 = (bf16[8,32,768]{2,1,0:T(8,128)(2,1)}, bf16[8,32,768]{2,1,0:T(8,128)(2,1)S(1)}, u32[]{:S(2)}, u32[]{:S(2)}) collective-permute-start(bf16[8,32,768]{2,1,0:T(8,128)(2,1)} %get-tuple-element.67), channel_id=1, source_target_pairs={{0,3},{1,2},{2,1},{3,0},{4,7},{5,6},{6,5},{7,4},{8,11},{9,10},{10,... | collective-permute-start | bytes 1179656 | tf_op jit(solution)/shard_map/ppermute | solution.py:312
  9.8 1.4 copy-done.4
  11.2 1.3 row_project.5
  13.3 4.3 %collective-permute-done.2.x_ref = bf16[8,32,768]{2,1,0:T(8,128)(2,1)S(1)} collective-permute-done((bf16[8,32,768]{2,1,0:T(8,128)(2,1)}, bf16[8,32,768]{2,1,0:T(8,128)(2,1)S(1)}, u32[]{:S(2)}, u32[]{:S(2)}) %collective-permute-start.2) | collective-permute-done | bytes 393248 | tf_op jit(solution)/shard_map/ppermute | solution.py:312
  17.5 1.3 row_project.6
  18.8 7.3 %collective-permute-done.1.x_ref = bf16[8,32,768]{2,1,0:T(8,128)(2,1)S(1)} collective-permute-done((bf16[8,32,768]{2,1,0:T(8,128)(2,1)}, bf16[8,32,768]{2,1,0:T(8,128)(2,1)S(1)}, u32[]{:S(2)}, u32[]{:S(2)}) %collective-permute-start.1) | collective-permute-done | bytes 393248 | tf_op jit(solution)/shard_map/ppermute | solution.py:312
  26.2 1.3 row_project.7
  27.5 13.6 %collective-permute-done.x_ref = bf16[8,32,768]{2,1,0:T(8,128)(2,1)S(1)} collective-permute-done((bf16[8,32,768]{2,1,0:T(8,128)(2,1)S(1)}, bf16[8,32,768]{2,1,0:T(8,128)(2,1)S(1)}, u32[]{:S(2)}, u32[]{:S(2)}) %collective-permute-start) | collective-permute-done | bytes 393248 | tf_op jit(solution)/shard_map/ppermute | solution.py:312
  44.6 12.2 %all_to_all.15.parts_ref = f32[8,48,256]{2,1,0:T(8,128)S(1)} all-to-all(f32[8,48,256]{2,1,0:T(8,128)S(1)} %bitcast.11), channel_id=1, replica_groups=mesh['pair'=4,'core'=2,'half'=2,'inner'=2] {'pair','inner'}, dimensions={0} | all-to-all | bytes 786432 | tf_op jit(solution)/shard_map/all_to_all | solution.py:376
  56.8 2.5 %collective-permute-start.4 = (f32[48,256]{1,0:T(8,128)S(1)}, f32[48,256]{1,0:T(8,128)S(1)}, u32[]{:S(2)}, u32[]{:S(2)}) collective-permute-start(f32[48,256]{1,0:T(8,128)S(1)} %row_sum.1.mine_ref), channel_id=1, source_target_pairs={{0,2},{2,0},{1,3},{3,1},{4,6},{6,4},{5,7},{7,5},{8,10},{10,8},{9,1... | collective-permute-start | bytes 147464 | tf_op jit(solution)/shard_map/ppermute | solution.py:406
  61.0 1.3 collective-permute-done.4.other_ref
  62.6 9.0 %all_to_all.16 = bf16[8,48,256]{2,1,0:T(8,128)(2,1)S(1)} all-to-all(bf16[8,48,256]{2,1,0:T(8,128)(2,1)S(1)} %row_softmax.1), channel_id=1, replica_groups=mesh['pair'=4,'core'=2,'half'=2,'inner'=2] {'pair','inner'}, dimensions={0} | all-to-all | bytes 393216 | tf_op jit(solution)/shard_map/all_to_all | solution.py:408
  73.0 2.4 %row_update.1 = (bf16[32,4,8,768]{3,2,1,0:T(8,128)(2,1)S(1)}, bf16[2,512,768]{2,1,0:T(8,128)(2,1)S(1)}) custom-call(s32[1]{0:T(128)} %bitcast.base_ref.low_ref, bf16[3,128,256]{2,1,0:T(8,128)(2,1)S(1)} %collective-permute-done.5.prob_ref, bf16[8,128,768]{2,1,0:T(8,128)(2,1)S(1)} %get-tuple-element.88.v_ref, ...), custom_call_target="tpu_custom_call", output_to_operand_aliasing={{1}: (5, {})} | custom-call | flops 1409286144 | bytes 8000000 | tf_op jit(solution)/shard_map/row_update/pallas_call | solution.py:423
  75.5 39.0 %all_to_all.17.mid_ref = bf16[32,4,8,768]{3,2,1,0:T(8,128)(2,1)S(1)} all-to-all(bf16[32,4,8,768]{3,2,1,0:T(8,128)(2,1)S(1)} %get-tuple-element.90), channel_id=1, replica_groups=mesh['pair'=4,'core'=2,'half'=2,'inner'=2] {'pair','core','half','inner'}, dimensions={0} | all-to-all | bytes 3145728 | tf_op jit(solution)/shard_map/all_to_all | solution.py:440
  114.5 4.8 %column_update.3 = (bf16[2,2,32,768]{3,2,1,0:T(8,128)(2,1)S(1)}, bf16[2,2,32,768]{3,2,1,0:T(8,128)(2,1)S(1)}, bf16[2,2,32,768]{3,2,1,0:T(8,128)(2,1)S(1)}, bf16[2,2,32,768]{3,2,1,0:T(8,128)(2,1)S(1)}) custom-call(s32[1]{0:T(128)} %bitcast.2.seq_ref, bf16[32,4,8,768]{3,2,1,0:T(8,128)(2,1)S(1)} %all_to_all.17.mid_ref, bf16[768,768]{1,0:T(8,128)(2,1)S(1)} %copy-done.6, ...), custom_call_target="tpu_custom_call" | custom-call | flops 3019898880 | bytes 8000000 | tf_op jit(solution)/shard_map/column_update/pallas_call | solution.py:448
  119.3 1.5 %collective-permute-start.11 = (bf16[2,2,32,768]{3,2,1,0:T(8,128)(2,1)S(1)}, bf16[2,2,32,768]{3,2,1,0:T(8,128)(2,1)S(1)}, u32[]{:S(2)}, u32[]{:S(2)}) collective-permute-start(bf16[2,2,32,768]{3,2,1,0:T(8,128)(2,1)S(1)} %get-tuple-element.96), channel_id=1, source_target_pairs={{0,8},{8,0},{16,24},{24,16},{1,9},{9,1},{17,25},{25,17},{2,10},{10... | collective-permute-start | bytes 589832 | tf_op jit(solution)/shard_map/ppermute | solution.py:315
  120.9 1.3 collective-permute-start.12
  122.9 4.8 %column_update.2 = (bf16[2,2,32,768]{3,2,1,0:T(8,128)(2,1)S(1)}, bf16[2,2,32,768]{3,2,1,0:T(8,128)(2,1)S(1)}, bf16[2,2,32,768]{3,2,1,0:T(8,128)(2,1)S(1)}, bf16[2,2,32,768]{3,2,1,0:T(8,128)(2,1)S(1)}) custom-call(s32[1]{0:T(128)} %bitcast.2.seq_ref, bf16[32,4,8,768]{3,2,1,0:T(8,128)(2,1)S(1)} %all_to_all.17.mid_ref, bf16[768,768]{1,0:T(8,128)(2,1)S(1)} %copy-done.6, ...), custom_call_target="tpu_custom_call" | custom-call | flops 3019898880 | bytes 8000000 | tf_op jit(solution)/shard_map/column_update/pallas_call | solution.py:448
  127.7 1.5 %collective-permute-start.6 = (bf16[2,2,32,768]{3,2,1,0:T(8,128)(2,1)S(1)}, bf16[2,2,32,768]{3,2,1,0:T(8,128)(2,1)S(1)}, u32[]{:S(2)}, u32[]{:S(2)}) collective-permute-start(bf16[2,2,32,768]{3,2,1,0:T(8,128)(2,1)S(1)} %get-tuple-element.92), channel_id=1, source_target_pairs={{0,8},{8,0},{16,24},{24,16},{1,9},{9,1},{17,25},{25,17},{2,10},{10... | collective-permute-start | bytes 589832 | tf_op jit(solution)/shard_map/ppermute | solution.py:315
  129.3 1.3 collective-permute-start.7
  131.3 1.5 %collective-permute-done.12.refs_2_ = bf16[2,2,32,768]{3,2,1,0:T(8,128)(2,1)S(1)} collective-permute-done((bf16[2,2,32,768]{3,2,1,0:T(8,128)(2,1)S(1)}, bf16[2,2,32,768]{3,2,1,0:T(8,128)(2,1)S(1)}, u32[]{:S(2)}, u32[]{:S(2)}) %collective-permute-start.12) | collective-permute-done | bytes 196640 | tf_op jit(solution)/shard_map/ppermute | solution.py:315
  133.5 2.2 %collective-permute-done.6.refs_1_ = bf16[2,2,32,768]{3,2,1,0:T(8,128)(2,1)S(1)} collective-permute-done((bf16[2,2,32,768]{3,2,1,0:T(8,128)(2,1)S(1)}, bf16[2,2,32,768]{3,2,1,0:T(8,128)(2,1)S(1)}, u32[]{:S(2)}, u32[]{:S(2)}) %collective-permute-start.6) | collective-permute-done | bytes 196640 | tf_op jit(solution)/shard_map/ppermute | solution.py:315
  135.9 5.4 %collective-permute-done.7.refs_2_ = bf16[2,2,32,768]{3,2,1,0:T(8,128)(2,1)S(1)} collective-permute-done((bf16[2,2,32,768]{3,2,1,0:T(8,128)(2,1)S(1)}, bf16[2,2,32,768]{3,2,1,0:T(8,128)(2,1)S(1)}, u32[]{:S(2)}, u32[]{:S(2)}) %collective-permute-start.7) | collective-permute-done | bytes 196640 | tf_op jit(solution)/shard_map/ppermute | solution.py:315
  (63 shorter events, 15.1 us)
Async XLA Ops:
  0.0 7.3 %copy-start = (bf16[768,768]{1,0:T(8,128)(2,1)S(1)}, bf16[768,768]{1,0:T(8,128)(2,1)}, u32[]{:S(2)}) copy-start(bf16[768,768]{1,0:T(8,128)(2,1)} %refs_0_.9) | copy-start | bytes 3538948
  2.2 15.4 %collective-permute-start.2 = (bf16[8,32,768]{2,1,0:T(8,128)(2,1)}, bf16[8,32,768]{2,1,0:T(8,128)(2,1)S(1)}, u32[]{:S(2)}, u32[]{:S(2)}) collective-permute-start(bf16[8,32,768]{2,1,0:T(8,128)(2,1)} %get-tuple-element.67), channel_id=1, source_target_pairs={{0,3},{1,2},{2,1},{3,0},{4,7},{5,6},{6,5},{7,4},{8,11},{9,10},{10,... | collective-permute-start | bytes 1179656 | tf_op jit(solution)/shard_map/ppermute | solution.py:312
  7.3 18.9 %collective-permute-start.1 = (bf16[8,32,768]{2,1,0:T(8,128)(2,1)}, bf16[8,32,768]{2,1,0:T(8,128)(2,1)S(1)}, u32[]{:S(2)}, u32[]{:S(2)}) collective-permute-start(bf16[8,32,768]{2,1,0:T(8,128)(2,1)} %get-tuple-element.65), channel_id=1, source_target_pairs={{0,1},{1,0},{2,3},{3,2},{4,5},{5,4},{6,7},{7,6},{8,9},{9,8},{10,11... | collective-permute-start | bytes 1179656 | tf_op jit(solution)/shard_map/ppermute | solution.py:312
  9.8 1.4 copy-start.4
  11.2 6.3 %copy-start.2 = (bf16[768,768]{1,0:T(8,128)(2,1)S(1)}, bf16[768,768]{1,0:T(8,128)(2,1)}, u32[]{:S(2)}) copy-start(bf16[768,768]{1,0:T(8,128)(2,1)} %refs_0_.8) | copy-start | bytes 3538948
  12.6 28.5 %collective-permute-start = (bf16[8,32,768]{2,1,0:T(8,128)(2,1)S(1)}, bf16[8,32,768]{2,1,0:T(8,128)(2,1)S(1)}, u32[]{:S(2)}, u32[]{:S(2)}) collective-permute-start(bf16[8,32,768]{2,1,0:T(8,128)(2,1)S(1)} %copy-done.10), channel_id=1, source_target_pairs={{0,2},{1,3},{2,0},{3,1},{4,6},{5,7},{6,4},{7,5},{8,10},{9,11},{10,... | collective-permute-start | bytes 1179656 | tf_op jit(solution)/shard_map/ppermute | solution.py:312
  42.7 1.8 %collective-permute-start.3 = (f32[3,128,256]{2,1,0:T(8,128)S(1)}, f32[3,128,256]{2,1,0:T(8,128)S(1)}, u32[]{:S(2)}, u32[]{:S(2)}) collective-permute-start(f32[3,128,256]{2,1,0:T(8,128)S(1)} %row_scores.3), channel_id=1, source_target_pairs={{0,4},{4,0},{1,5},{5,1},{2,6},{6,2},{3,7},{7,3},{8,12},{12,8},{9,1... | collective-permute-start | bytes 1179656 | tf_op jit(solution)/shard_map/ppermute | solution.py:372
  56.8 5.6 %collective-permute-start.4 = (f32[48,256]{1,0:T(8,128)S(1)}, f32[48,256]{1,0:T(8,128)S(1)}, u32[]{:S(2)}, u32[]{:S(2)}) collective-permute-start(f32[48,256]{1,0:T(8,128)S(1)} %row_sum.1.mine_ref), channel_id=1, source_target_pairs={{0,2},{2,0},{1,3},{3,1},{4,6},{6,4},{5,7},{7,5},{8,10},{10,8},{9,1... | collective-permute-start | bytes 147464 | tf_op jit(solution)/shard_map/ppermute | solution.py:406
  71.6 1.4 %copy-start.5 = (bf16[768,768]{1,0:T(8,128)(2,1)S(1)}, bf16[768,768]{1,0:T(8,128)(2,1)}, u32[]{:S(2)}) copy-start(bf16[768,768]{1,0:T(8,128)(2,1)} %wo_ref.3) | copy-start | bytes 3538948
  71.6 1.4 %collective-permute-start.5 = (bf16[3,128,256]{2,1,0:T(8,128)(2,1)S(1)}, bf16[3,128,256]{2,1,0:T(8,128)(2,1)S(1)}, u32[]{:S(2)}, u32[]{:S(2)}) collective-permute-start(bf16[3,128,256]{2,1,0:T(8,128)(2,1)S(1)} %bitcast.9), channel_id=1, source_target_pairs={{0,4},{4,0},{1,5},{5,1},{2,6},{6,2},{3,7},{7,3},{8,12},{12,8},{9,1... | collective-permute-start | bytes 589832 | tf_op jit(solution)/shard_map/ppermute | solution.py:410
  73.0 41.4 %copy-start.8 = (bf16[768,768]{1,0:T(8,128)(2,1)S(1)}, bf16[768,768]{1,0:T(8,128)(2,1)}, u32[]{:S(2)}) copy-start(bf16[768,768]{1,0:T(8,128)(2,1)} %wv_ref.3) | copy-start | bytes 3538948
  73.0 41.4 %copy-start.9 = (bf16[768,768]{1,0:T(8,128)(2,1)S(1)}, bf16[768,768]{1,0:T(8,128)(2,1)}, u32[]{:S(2)}) copy-start(bf16[768,768]{1,0:T(8,128)(2,1)} %wo_ref.5) | copy-start | bytes 3538948
  75.5 39.0 %copy-start.6 = (bf16[768,768]{1,0:T(8,128)(2,1)S(1)}, bf16[768,768]{1,0:T(8,128)(2,1)}, u32[]{:S(2)}) copy-start(bf16[768,768]{1,0:T(8,128)(2,1)} %wq_ref.3) | copy-start | bytes 3538948
  75.5 39.0 %copy-start.7 = (bf16[768,768]{1,0:T(8,128)(2,1)S(1)}, bf16[768,768]{1,0:T(8,128)(2,1)}, u32[]{:S(2)}) copy-start(bf16[768,768]{1,0:T(8,128)(2,1)} %wk_ref.3) | copy-start | bytes 3538948
  119.3 11.2 %collective-permute-start.11 = (bf16[2,2,32,768]{3,2,1,0:T(8,128)(2,1)S(1)}, bf16[2,2,32,768]{3,2,1,0:T(8,128)(2,1)S(1)}, u32[]{:S(2)}, u32[]{:S(2)}) collective-permute-start(bf16[2,2,32,768]{3,2,1,0:T(8,128)(2,1)S(1)} %get-tuple-element.96), channel_id=1, source_target_pairs={{0,8},{8,0},{16,24},{24,16},{1,9},{9,1},{17,25},{25,17},{2,10},{10... | collective-permute-start | bytes 589832 | tf_op jit(solution)/shard_map/ppermute | solution.py:315
  120.9 12.0 %collective-permute-start.12 = (bf16[2,2,32,768]{3,2,1,0:T(8,128)(2,1)S(1)}, bf16[2,2,32,768]{3,2,1,0:T(8,128)(2,1)S(1)}, u32[]{:S(2)}, u32[]{:S(2)}) collective-permute-start(bf16[2,2,32,768]{3,2,1,0:T(8,128)(2,1)S(1)} %get-tuple-element.97), channel_id=1, source_target_pairs={{0,16},{8,24},{16,0},{24,8},{1,17},{9,25},{17,1},{25,9},{2,18},{10... | collective-permute-start | bytes 589832 | tf_op jit(solution)/shard_map/ppermute | solution.py:315
  122.2 10.7 %collective-permute-start.13 = (bf16[2,2,32,768]{3,2,1,0:T(8,128)(2,1)S(1)}, bf16[2,2,32,768]{3,2,1,0:T(8,128)(2,1)S(1)}, u32[]{:S(2)}, u32[]{:S(2)}) collective-permute-start(bf16[2,2,32,768]{3,2,1,0:T(8,128)(2,1)S(1)} %get-tuple-element.98), channel_id=1, source_target_pairs={{0,24},{8,16},{16,8},{24,0},{1,25},{9,17},{17,9},{25,1},{2,26},{10... | collective-permute-start | bytes 589832 | tf_op jit(solution)/shard_map/ppermute | solution.py:315
  127.7 7.9 %collective-permute-start.6 = (bf16[2,2,32,768]{3,2,1,0:T(8,128)(2,1)S(1)}, bf16[2,2,32,768]{3,2,1,0:T(8,128)(2,1)S(1)}, u32[]{:S(2)}, u32[]{:S(2)}) collective-permute-start(bf16[2,2,32,768]{3,2,1,0:T(8,128)(2,1)S(1)} %get-tuple-element.92), channel_id=1, source_target_pairs={{0,8},{8,0},{16,24},{24,16},{1,9},{9,1},{17,25},{25,17},{2,10},{10... | collective-permute-start | bytes 589832 | tf_op jit(solution)/shard_map/ppermute | solution.py:315
  129.3 11.9 %collective-permute-start.7 = (bf16[2,2,32,768]{3,2,1,0:T(8,128)(2,1)S(1)}, bf16[2,2,32,768]{3,2,1,0:T(8,128)(2,1)S(1)}, u32[]{:S(2)}, u32[]{:S(2)}) collective-permute-start(bf16[2,2,32,768]{3,2,1,0:T(8,128)(2,1)S(1)} %get-tuple-element.93), channel_id=1, source_target_pairs={{0,16},{8,24},{16,0},{24,8},{1,17},{9,25},{17,1},{25,9},{2,18},{10... | collective-permute-start | bytes 589832 | tf_op jit(solution)/shard_map/ppermute | solution.py:315
  130.6 10.6 %collective-permute-start.8 = (bf16[2,2,32,768]{3,2,1,0:T(8,128)(2,1)S(1)}, bf16[2,2,32,768]{3,2,1,0:T(8,128)(2,1)S(1)}, u32[]{:S(2)}, u32[]{:S(2)}) collective-permute-start(bf16[2,2,32,768]{3,2,1,0:T(8,128)(2,1)S(1)} %get-tuple-element.94), channel_id=1, source_target_pairs={{0,24},{8,16},{16,8},{24,0},{1,25},{9,17},{17,9},{25,1},{2,26},{10... | collective-permute-start | bytes 589832 | tf_op jit(solution)/shard_map/ppermute | solution.py:315
  132.9 8.5 %collective-permute-start.14 = (bf16[2,2,32,768]{3,2,1,0:T(8,128)(2,1)S(1)}, bf16[2,2,32,768]{3,2,1,0:T(8,128)(2,1)S(1)}, u32[]{:S(2)}, u32[]{:S(2)}) collective-permute-start(bf16[2,2,32,768]{3,2,1,0:T(8,128)(2,1)S(1)} %pad_maximum_fusion.2), channel_id=1, source_target_pairs={{0,4},{4,0},{1,5},{5,1},{2,6},{6,2},{3,7},{7,3},{8,12},{12,8},{9,1... | collective-permute-start | bytes 589832 | tf_op jit(solution)/shard_map/ppermute | solution.py:463
  132.9 8.5 %collective-permute-start.15 = (bf16[2,2,32,768]{3,2,1,0:T(8,128)(2,1)S(1)}, bf16[2,2,32,768]{3,2,1,0:T(8,128)(2,1)S(1)}, u32[]{:S(2)}, u32[]{:S(2)}) collective-permute-start(bf16[2,2,32,768]{3,2,1,0:T(8,128)(2,1)S(1)} %pad_maximum_fusion.3), channel_id=1, source_target_pairs={{0,4},{4,0},{1,5},{5,1},{2,6},{6,2},{3,7},{7,3},{8,12},{12,8},{9,1... | collective-permute-start | bytes 589832 | tf_op jit(solution)/shard_map/ppermute | solution.py:463
  135.7 6.9 %collective-permute-start.9 = (bf16[2,2,32,768]{3,2,1,0:T(8,128)(2,1)S(1)}, bf16[2,2,32,768]{3,2,1,0:T(8,128)(2,1)S(1)}, u32[]{:S(2)}, u32[]{:S(2)}) collective-permute-start(bf16[2,2,32,768]{3,2,1,0:T(8,128)(2,1)S(1)} %pad_maximum_fusion), channel_id=1, source_target_pairs={{0,4},{4,0},{1,5},{5,1},{2,6},{6,2},{3,7},{7,3},{8,12},{12,8},{9,1... | collective-permute-start | bytes 589832 | tf_op jit(solution)/shard_map/ppermute | solution.py:463
  141.3 1.5 %collective-permute-start.10 = (bf16[2,2,32,768]{3,2,1,0:T(8,128)(2,1)S(1)}, bf16[2,2,32,768]{3,2,1,0:T(8,128)(2,1)S(1)}, u32[]{:S(2)}, u32[]{:S(2)}) collective-permute-start(bf16[2,2,32,768]{3,2,1,0:T(8,128)(2,1)S(1)} %pad_maximum_fusion.1), channel_id=1, source_target_pairs={{0,4},{4,0},{1,5},{5,1},{2,6},{6,2},{3,7},{7,3},{8,12},{12,8},{9,1... | collective-permute-start | bytes 589832 | tf_op jit(solution)/shard_map/ppermute | solution.py:463
  (3 other events, 3.9 us)
